TPU v7x, 512 devices: a whole 4x8x8 slice. The times are simulated.
512 devices in a mesh: tm: 128 (over y, z, core), space: 4 (over x).
Axes of the slice: x: 4, y: 8, z: 8, core: 2. Of those that a mesh axis runs over, the one named last changes fastest.
Arguments:
- source: float32 [128, 32, 128, 128], P('tm', 'space'), may hold values from -8 to 8
- conductivity: float32 [32, 128, 128], P('space'), may hold values from 0.5 to 4
Outputs:
- solution: float32 [128, 32, 128, 128], P('tm', 'space')
- final_defect: float32 [128, 32, 128, 128], P('tm', 'space')
All inputs are finite; a program needn't handle non-finite values.
Results may differ from a plain program's by a relative error of at most 0.000034.
Values sent between devices are 32-bit elements; how exact they have to be, the bound alone decides.
No kernel may reach another device: no remote copies, remote signals or barrier semaphores. Data moves between devices by JAX's collectives and lax.ppermute only.
A program may use at most 64 MiB of HBM per device.

v0:
```python
import jax
import jax.numpy as jnp
from jax import lax
from jax.sharding import PartitionSpec as P

NU = 2
NC = 4


OMEGA = 0.8
FINE = (1.0, 1.0, 1.0)
COARSE = (0.25, 0.25, 1.0)


def padded_2(shard, sides, width):
    for axis, dim in sides:
        peers, length = (lax.axis_size(axis), shard.shape[dim])
        up = [(i, (i + 1) % peers) for i in range(peers - 1)]
        down = [(j, i) for i, j in up]
        last = lax.slice_in_dim(shard, length - width, length, axis=dim)
        first = lax.slice_in_dim(shard, 0, width, axis=dim)
        before = lax.ppermute(last, axis, up)
        after = lax.ppermute(first, axis, down)
        shard = jnp.concatenate([before, shard, after], axis=dim)
    return shard


def shifted(shard, axis, by):
    peers = lax.axis_size(axis)
    pairs = [(i, i + by) for i in range(peers) if 0 <= i + by < peers]
    return lax.ppermute(shard, axis, pairs)


def swapped(value, axis, bit):
    mask = 2**bit
    pairs = [(source, source ^ mask) for source in range(lax.axis_size(axis))]
    return lax.ppermute(value, axis, pairs)


def stencil(padded, weights):
    weight_z, weight_x, weight_y = weights
    centre = padded[1:-1, :, 1:-1]
    widened = jnp.pad(padded[1:-1], ((0, 0), (1, 1), (0, 0)))
    along_z = 2.0 * centre - padded[2:, :, 1:-1] - padded[:-2, :, 1:-1]
    along_x = 2.0 * centre - widened[:, 2:, 1:-1] - widened[:, :-2, 1:-1]
    along_y = 2.0 * centre - padded[1:-1, :, 2:] - padded[1:-1, :, :-2]
    return weight_z * along_z + weight_x * along_x + weight_y * along_y


def defect(current, right_side, earlier, padded, conduct, stretch, weights):
    applied = current + stretch * conduct * stencil(padded, weights)
    return right_side + earlier - applied


def relaxed(current, right_side, earlier, padded, conduct, stretch, weights):
    weight_sum = 2.0 * (weights[0] + weights[1] + weights[2])
    diagonal = 1.0 + stretch * conduct * weight_sum
    return (
        current
        + OMEGA * defect(current, right_side, earlier, padded, conduct, stretch, weights) / diagonal
    )


def coarsen(values):
    return 0.25 * (
        values[..., 0::2, 0::2, :]
        + values[..., 1::2, 0::2, :]
        + (values[..., 0::2, 1::2, :] + values[..., 1::2, 1::2, :])
    )


def refine(values):
    return jnp.repeat(jnp.repeat(values, 2, axis=-3), 2, axis=-2)


def zero_columns(values):
    return jnp.pad(values, ((0, 0), (0, 0), (1, 1)))


def plane_faces(values):
    return padded_2(values, (("space", 0),), 1)


def coarse_planes_framed(values):
    return padded_2(values, (("space", 0),), 1)


def fine_frame(values):
    return zero_columns(plane_faces(values))


def step_prior(values):
    return shifted(values, "tm", 1)


def pair_prior(values):
    return shifted(values, "tm", 2)


def group_prior(values):
    return shifted(values, "tm", 4)


def smooth(current, right_side, conduct, stretch, weights, repeats, earlier_of, framing):
    for turn_index in range(repeats):
        current = relaxed(
            current, right_side, earlier_of(current), framing(current), conduct, stretch, weights
        )
    return current


def body(source, conductivity):
    right_side = source[0]
    solution = smooth(
        jnp.zeros_like(right_side), right_side, conductivity, 1.0, FINE, NU, step_prior, fine_frame
    )
    defect_fine = defect(
        solution, right_side, step_prior(solution), fine_frame(solution), conductivity, 1.0, FINE
    )
    middle_full = defect_fine + swapped(defect_fine, "tm", 0)
    middle = smooth(
        jnp.zeros_like(middle_full),
        middle_full,
        conductivity,
        2.0,
        FINE,
        NU,
        pair_prior,
        fine_frame,
    )
    middle_defect = defect(
        middle, middle_full, pair_prior(middle), fine_frame(middle), conductivity, 2.0, FINE
    )
    summed = middle_defect + swapped(middle_defect, "tm", 1)
    coarse_rhs = coarsen(summed)
    coarse_cond = coarsen(conductivity)

    def coarse_frame(values):
        return zero_columns(coarse_planes_framed(values))

    coarse = smooth(
        jnp.zeros_like(coarse_rhs),
        coarse_rhs,
        coarse_cond,
        4.0,
        COARSE,
        NC,
        group_prior,
        coarse_frame,
    )
    middle = middle + refine(coarse)
    middle = smooth(middle, middle_full, conductivity, 2.0, FINE, NU, pair_prior, fine_frame)
    solution = solution + middle
    solution = smooth(solution, right_side, conductivity, 1.0, FINE, NU, step_prior, fine_frame)
    final_defect = defect(
        solution, right_side, step_prior(solution), fine_frame(solution), conductivity, 1.0, FINE
    )
    return (solution[None], final_defect[None])


def solution(mesh):
    return jax.shard_map(
        body,
        mesh=mesh,
        in_specs=(P("tm", "space", None, None), P("space", None, None)),
        out_specs=(P("tm", "space", None, None), P("tm", "space", None, None)),
        check_vma=False,
    )
```

profile of v0, /device:TPU:32, one launch (start us, length us, event | category | flops | bytes accessed | tf_op | source)
XLA Modules:
  0.0 256.4 jit_solution(13573442902984381298)
XLA Ops:
  3.9 4.5 %collective-permute-start.2 = (f32[1,128,128]{2,1,0:T(8,128)S(1)}, f32[1,128,128]{2,1,0:T(8,128)S(1)}, u32[]{:S(2)}, u32[]{:S(2)}) collective-permute-start(f32[1,128,128]{2,1,0:T(8,128)S(1)} %broadcast.105), channel_id=1, source_target_pairs={{0,1},{1,2},{2,3},{4,5},{5,6},{6,7},{8,9},{9,10},{10,11},{12,13},{... | collective-permute-start | bytes 196616 | tf_op jit(solution)/shard_map/ppermute | solution.py:22
  10.9 6.9 %collective-permute-done = f32[8,128,128]{2,1,0:T(8,128)S(1)} collective-permute-done((f32[8,128,128]{2,1,0:T(8,128)S(1)}, f32[8,128,128]{2,1,0:T(8,128)S(1)}, u32[]{:S(2)}, u32[]{:S(2)}) %collective-permute-start) | collective-permute-done | bytes 524320 | tf_op jit(solution)/shard_map/ppermute | solution.py:31
  21.6 4.5 %collective-permute-start.5 = (f32[1,128,128]{2,1,0:T(8,128)S(1)}, f32[1,128,128]{2,1,0:T(8,128)S(1)}, u32[]{:S(2)}, u32[]{:S(2)}) collective-permute-start(f32[1,128,128]{2,1,0:T(8,128)S(1)} %get-tuple-element.25), channel_id=1, source_target_pairs={{0,1},{1,2},{2,3},{4,5},{5,6},{6,7},{8,9},{9,10},{10,11},{12,13},{... | collective-permute-start | bytes 196616 | tf_op jit(solution)/shard_map/ppermute | solution.py:22
  28.6 3.6 %collective-permute-done.3 = f32[8,128,128]{2,1,0:T(8,128)S(1)} collective-permute-done((f32[8,128,128]{2,1,0:T(8,128)S(1)}, f32[8,128,128]{2,1,0:T(8,128)S(1)}, u32[]{:S(2)}, u32[]{:S(2)}) %collective-permute-start.3) | collective-permute-done | bytes 524320 | tf_op jit(solution)/shard_map/ppermute | solution.py:31
  36.1 4.5 %collective-permute-start.8 = (f32[1,128,128]{2,1,0:T(8,128)S(1)}, f32[1,128,128]{2,1,0:T(8,128)S(1)}, u32[]{:S(2)}, u32[]{:S(2)}) collective-permute-start(f32[1,128,128]{2,1,0:T(8,128)S(1)} %get-tuple-element.23), channel_id=1, source_target_pairs={{0,1},{1,2},{2,3},{4,5},{5,6},{6,7},{8,9},{9,10},{10,11},{12,13},{... | collective-permute-start | bytes 196616 | tf_op jit(solution)/shard_map/ppermute | solution.py:22
  49.3 10.3 %collective-permute-done.10 = f32[8,128,128]{2,1,0:T(8,128)S(1)} collective-permute-done((f32[8,128,128]{2,1,0:T(8,128)S(1)}, f32[8,128,128]{2,1,0:T(8,128)S(1)}, u32[]{:S(2)}, u32[]{:S(2)}) %collective-permute-start.10) | collective-permute-done | bytes 524320 | tf_op jit(solution)/shard_map/ppermute | solution.py:31
  63.0 4.5 %collective-permute-start.13 = (f32[1,128,128]{2,1,0:T(8,128)S(1)}, f32[1,128,128]{2,1,0:T(8,128)S(1)}, u32[]{:S(2)}, u32[]{:S(2)}) collective-permute-start(f32[1,128,128]{2,1,0:T(8,128)S(1)} %get-tuple-element.21), channel_id=1, source_target_pairs={{0,1},{1,2},{2,3},{4,5},{5,6},{6,7},{8,9},{9,10},{10,11},{12,13},{... | collective-permute-start | bytes 196616 | tf_op jit(solution)/shard_map/ppermute | solution.py:22
  69.9 7.8 %collective-permute-done.11 = f32[8,128,128]{2,1,0:T(8,128)S(1)} collective-permute-done((f32[8,128,128]{2,1,0:T(8,128)S(1)}, f32[8,128,128]{2,1,0:T(8,128)S(1)}, u32[]{:S(2)}, u32[]{:S(2)}) %collective-permute-start.11) | collective-permute-done | bytes 524320 | tf_op jit(solution)/shard_map/ppermute | solution.py:31
  81.7 4.5 %collective-permute-start.16 = (f32[1,128,128]{2,1,0:T(8,128)S(1)}, f32[1,128,128]{2,1,0:T(8,128)S(1)}, u32[]{:S(2)}, u32[]{:S(2)}) collective-permute-start(f32[1,128,128]{2,1,0:T(8,128)S(1)} %get-tuple-element.19), channel_id=1, source_target_pairs={{0,1},{1,2},{2,3},{4,5},{5,6},{6,7},{8,9},{9,10},{10,11},{12,13},{... | collective-permute-start | bytes 196616 | tf_op jit(solution)/shard_map/ppermute | solution.py:22
  88.6 6.9 %collective-permute-done.14 = f32[8,128,128]{2,1,0:T(8,128)S(1)} collective-permute-done((f32[8,128,128]{2,1,0:T(8,128)S(1)}, f32[8,128,128]{2,1,0:T(8,128)S(1)}, u32[]{:S(2)}, u32[]{:S(2)}) %collective-permute-start.14) | collective-permute-done | bytes 524320 | tf_op jit(solution)/shard_map/ppermute | solution.py:31
  99.5 5.1 %collective-permute-start.20 = (f32[1,64,128]{2,1,0:T(8,128)S(1)}, f32[1,64,128]{2,1,0:T(8,128)}, u32[]{:S(2)}, u32[]{:S(2)}) collective-permute-start(f32[1,64,128]{2,1,0:T(8,128)S(1)} %broadcast.111), channel_id=1, source_target_pairs={{0,1},{1,2},{2,3},{4,5},{5,6},{6,7},{8,9},{9,10},{10,11},{12,13},{... | collective-permute-start | bytes 98312 | tf_op jit(solution)/shard_map/ppermute | solution.py:22
  127.0 4.5 %collective-permute-start.23 = (f32[1,64,128]{2,1,0:T(8,128)S(1)}, f32[1,64,128]{2,1,0:T(8,128)S(1)}, u32[]{:S(2)}, u32[]{:S(2)}) collective-permute-start(f32[1,64,128]{2,1,0:T(8,128)S(1)} %get-tuple-element.31), channel_id=1, source_target_pairs={{0,1},{1,2},{2,3},{4,5},{5,6},{6,7},{8,9},{9,10},{10,11},{12,13},{... | collective-permute-start | bytes 98312 | tf_op jit(solution)/shard_map/ppermute | solution.py:22
  133.7 9.8 %collective-permute-done.21 = f32[4,64,128]{2,1,0:T(8,128)S(1)} collective-permute-done((f32[4,64,128]{2,1,0:T(8,128)S(1)}, f32[4,64,128]{2,1,0:T(8,128)S(1)}, u32[]{:S(2)}, u32[]{:S(2)}) %collective-permute-start.21) | collective-permute-done | bytes 131104 | tf_op jit(solution)/shard_map/ppermute | solution.py:31
  144.9 4.5 %collective-permute-start.26 = (f32[1,64,128]{2,1,0:T(8,128)S(1)}, f32[1,64,128]{2,1,0:T(8,128)S(1)}, u32[]{:S(2)}, u32[]{:S(2)}) collective-permute-start(f32[1,64,128]{2,1,0:T(8,128)S(1)} %get-tuple-element.29), channel_id=1, source_target_pairs={{0,1},{1,2},{2,3},{4,5},{5,6},{6,7},{8,9},{9,10},{10,11},{12,13},{... | collective-permute-start | bytes 98312 | tf_op jit(solution)/shard_map/ppermute | solution.py:22
  151.7 10.6 %collective-permute-done.24 = f32[4,64,128]{2,1,0:T(8,128)S(1)} collective-permute-done((f32[4,64,128]{2,1,0:T(8,128)S(1)}, f32[4,64,128]{2,1,0:T(8,128)S(1)}, u32[]{:S(2)}, u32[]{:S(2)}) %collective-permute-start.24) | collective-permute-done | bytes 131104 | tf_op jit(solution)/shard_map/ppermute | solution.py:31
  163.7 4.5 %collective-permute-start.29 = (f32[1,64,128]{2,1,0:T(8,128)S(1)}, f32[1,64,128]{2,1,0:T(8,128)S(1)}, u32[]{:S(2)}, u32[]{:S(2)}) collective-permute-start(f32[1,64,128]{2,1,0:T(8,128)S(1)} %get-tuple-element.27), channel_id=1, source_target_pairs={{0,1},{1,2},{2,3},{4,5},{5,6},{6,7},{8,9},{9,10},{10,11},{12,13},{... | collective-permute-start | bytes 98312 | tf_op jit(solution)/shard_map/ppermute | solution.py:22
  170.5 10.3 %collective-permute-done.27 = f32[4,64,128]{2,1,0:T(8,128)S(1)} collective-permute-done((f32[4,64,128]{2,1,0:T(8,128)S(1)}, f32[4,64,128]{2,1,0:T(8,128)S(1)}, u32[]{:S(2)}, u32[]{:S(2)}) %collective-permute-start.27) | collective-permute-done | bytes 131104 | tf_op jit(solution)/shard_map/ppermute | solution.py:31
  185.8 4.5 %collective-permute-start.32 = (f32[1,128,128]{2,1,0:T(8,128)S(1)}, f32[1,128,128]{2,1,0:T(8,128)S(1)}, u32[]{:S(2)}, u32[]{:S(2)}) collective-permute-start(f32[1,128,128]{2,1,0:T(8,128)S(1)} %get-tuple-element.17), channel_id=1, source_target_pairs={{0,1},{1,2},{2,3},{4,5},{5,6},{6,7},{8,9},{9,10},{10,11},{12,13},{... | collective-permute-start | bytes 196616 | tf_op jit(solution)/shard_map/ppermute | solution.py:22
  192.7 3.8 %collective-permute-done.30 = f32[8,128,128]{2,1,0:T(8,128)S(1)} collective-permute-done((f32[8,128,128]{2,1,0:T(8,128)S(1)}, f32[8,128,128]{2,1,0:T(8,128)S(1)}, u32[]{:S(2)}, u32[]{:S(2)}) %collective-permute-start.30) | collective-permute-done | bytes 524320 | tf_op jit(solution)/shard_map/ppermute | solution.py:31
  200.4 4.7 %collective-permute-start.35 = (f32[1,128,128]{2,1,0:T(8,128)S(1)}, f32[1,128,128]{2,1,0:T(8,128)S(1)}, u32[]{:S(2)}, u32[]{:S(2)}) collective-permute-start(f32[1,128,128]{2,1,0:T(8,128)S(1)} %get-tuple-element.15), channel_id=1, source_target_pairs={{0,1},{1,2},{2,3},{4,5},{5,6},{6,7},{8,9},{9,10},{10,11},{12,13},{... | collective-permute-start | bytes 196616 | tf_op jit(solution)/shard_map/ppermute | solution.py:22
  207.4 4.2 %collective-permute-done.33 = f32[8,128,128]{2,1,0:T(8,128)S(1)} collective-permute-done((f32[8,128,128]{2,1,0:T(8,128)S(1)}, f32[8,128,128]{2,1,0:T(8,128)S(1)}, u32[]{:S(2)}, u32[]{:S(2)}) %collective-permute-start.33) | collective-permute-done | bytes 524320 | tf_op jit(solution)/shard_map/ppermute | solution.py:31
  215.5 4.5 %collective-permute-start.38 = (f32[1,128,128]{2,1,0:T(8,128)S(1)}, f32[1,128,128]{2,1,0:T(8,128)S(1)}, u32[]{:S(2)}, u32[]{:S(2)}) collective-permute-start(f32[1,128,128]{2,1,0:T(8,128)S(1)} %get-tuple-element.13), channel_id=1, source_target_pairs={{0,1},{1,2},{2,3},{4,5},{5,6},{6,7},{8,9},{9,10},{10,11},{12,13},{... | collective-permute-start | bytes 196616 | tf_op jit(solution)/shard_map/ppermute | solution.py:22
  230.0 4.5 %collective-permute-start.41 = (f32[1,128,128]{2,1,0:T(8,128)S(1)}, f32[1,128,128]{2,1,0:T(8,128)S(1)}, u32[]{:S(2)}, u32[]{:S(2)}) collective-permute-start(f32[1,128,128]{2,1,0:T(8,128)S(1)} %get-tuple-element.11), channel_id=1, source_target_pairs={{0,1},{1,2},{2,3},{4,5},{5,6},{6,7},{8,9},{9,10},{10,11},{12,13},{... | collective-permute-start | bytes 196616 | tf_op jit(solution)/shard_map/ppermute | solution.py:22
  244.4 4.5 %collective-permute-start.44 = (f32[1,128,128]{2,1,0:T(8,128)S(1)}, f32[1,128,128]{2,1,0:T(8,128)S(1)}, u32[]{:S(2)}, u32[]{:S(2)}) collective-permute-start(f32[1,128,128]{2,1,0:T(8,128)S(1)} %get-tuple-element.9), channel_id=1, source_target_pairs={{0,1},{1,2},{2,3},{4,5},{5,6},{6,7},{8,9},{9,10},{10,11},{12,13},{... | collective-permute-start | bytes 196616 | tf_op jit(solution)/shard_map/ppermute | solution.py:22
  (145 shorter events, 116.3 us)
Async XLA Ops:
  0.7 17.1 %collective-permute-start = (f32[8,128,128]{2,1,0:T(8,128)S(1)}, f32[8,128,128]{2,1,0:T(8,128)S(1)}, u32[]{:S(2)}, u32[]{:S(2)}) collective-permute-start(f32[8,128,128]{2,1,0:T(8,128)S(1)} %slice.484), channel_id=1, source_target_pairs={{0,4},{4,8},{8,12},{12,16},{16,20},{20,24},{24,28},{28,32},{32,36}... | collective-permute-start | bytes 1572872 | tf_op jit(solution)/shard_map/ppermute | solution.py:31
  18.4 13.8 %collective-permute-start.3 = (f32[8,128,128]{2,1,0:T(8,128)S(1)}, f32[8,128,128]{2,1,0:T(8,128)S(1)}, u32[]{:S(2)}, u32[]{:S(2)}) collective-permute-start(f32[8,128,128]{2,1,0:T(8,128)S(1)} %get-tuple-element.7), channel_id=1, source_target_pairs={{0,4},{4,8},{8,12},{12,16},{16,20},{20,24},{24,28},{28,32},{32,36}... | collective-permute-start | bytes 1572872 | tf_op jit(solution)/shard_map/ppermute | solution.py:31
  32.8 13.8 %collective-permute-start.6 = (f32[8,128,128]{2,1,0:T(8,128)S(1)}, f32[8,128,128]{2,1,0:T(8,128)S(1)}, u32[]{:S(2)}, u32[]{:S(2)}) collective-permute-start(f32[8,128,128]{2,1,0:T(8,128)S(1)} %fusion.16), channel_id=1, source_target_pairs={{0,4},{4,8},{8,12},{12,16},{16,20},{20,24},{24,28},{28,32},{32,36}... | collective-permute-start | bytes 1572872 | tf_op jit(solution)/shard_map/ppermute | solution.py:31
  34.8 7.8 %collective-permute-start.7 = (f32[1,128,128]{2,1,0:T(8,128)S(1)}, f32[1,128,128]{2,1,0:T(8,128)S(1)}, u32[]{:S(2)}, u32[]{:S(2)}) collective-permute-start(f32[1,128,128]{2,1,0:T(8,128)S(1)} %get-tuple-element.24), channel_id=1, source_target_pairs={{1,0},{2,1},{3,2},{5,4},{6,5},{7,6},{9,8},{10,9},{11,10},{13,12},{... | collective-permute-start | bytes 196616 | tf_op jit(solution)/shard_map/ppermute | solution.py:23
  36.1 6.5 %collective-permute-start.8 = (f32[1,128,128]{2,1,0:T(8,128)S(1)}, f32[1,128,128]{2,1,0:T(8,128)S(1)}, u32[]{:S(2)}, u32[]{:S(2)}) collective-permute-start(f32[1,128,128]{2,1,0:T(8,128)S(1)} %get-tuple-element.23), channel_id=1, source_target_pairs={{0,1},{1,2},{2,3},{4,5},{5,6},{6,7},{8,9},{9,10},{10,11},{12,13},{... | collective-permute-start | bytes 196616 | tf_op jit(solution)/shard_map/ppermute | solution.py:22
  40.6 18.9 %collective-permute-start.10 = (f32[8,128,128]{2,1,0:T(8,128)S(1)}, f32[8,128,128]{2,1,0:T(8,128)S(1)}, u32[]{:S(2)}, u32[]{:S(2)}) collective-permute-start(f32[8,128,128]{2,1,0:T(8,128)S(1)} %slice.484), channel_id=1, source_target_pairs={{0,8},{4,12},{8,16},{12,20},{16,24},{20,28},{24,32},{28,36},{32,40... | collective-permute-start | bytes 1572872 | tf_op jit(solution)/shard_map/ppermute | solution.py:31
  47.3 12.2 %collective-permute-start.9 = (f32[8,128,128]{2,1,0:T(8,128)S(1)}, f32[8,128,128]{2,1,0:T(8,128)S(1)}, u32[]{:S(2)}, u32[]{:S(2)}) collective-permute-start(f32[8,128,128]{2,1,0:T(8,128)S(1)} %fusion.23), channel_id=1, source_target_pairs={{0,4},{4,0},{8,12},{12,8},{16,20},{20,16},{24,28},{28,24},{32,36},... | collective-permute-start | bytes 1572872 | tf_op jit(solution)/shard_map/ppermute | solution.py:37
  59.7 18.0 %collective-permute-start.11 = (f32[8,128,128]{2,1,0:T(8,128)S(1)}, f32[8,128,128]{2,1,0:T(8,128)S(1)}, u32[]{:S(2)}, u32[]{:S(2)}) collective-permute-start(f32[8,128,128]{2,1,0:T(8,128)S(1)} %get-tuple-element.5), channel_id=1, source_target_pairs={{0,8},{4,12},{8,16},{12,20},{16,24},{20,28},{24,32},{28,36},{32,40... | collective-permute-start | bytes 1572872 | tf_op jit(solution)/shard_map/ppermute | solution.py:31
  78.4 17.1 %collective-permute-start.14 = (f32[8,128,128]{2,1,0:T(8,128)S(1)}, f32[8,128,128]{2,1,0:T(8,128)S(1)}, u32[]{:S(2)}, u32[]{:S(2)}) collective-permute-start(f32[8,128,128]{2,1,0:T(8,128)S(1)} %fusion.33), channel_id=1, source_target_pairs={{0,8},{4,12},{8,16},{12,20},{16,24},{20,28},{24,32},{28,36},{32,40... | collective-permute-start | bytes 1572872 | tf_op jit(solution)/shard_map/ppermute | solution.py:31
  96.2 18.6 %collective-permute-start.17 = (f32[8,128,128]{2,1,0:T(8,128)S(1)}, f32[8,128,128]{2,1,0:T(8,128)}, u32[]{:S(2)}, u32[]{:S(2)}) collective-permute-start(f32[8,128,128]{2,1,0:T(8,128)S(1)} %fusion.40), channel_id=1, source_target_pairs={{0,8},{4,12},{8,0},{12,4},{16,24},{20,28},{24,16},{28,20},{32,40},... | collective-permute-start | bytes 1572872 | tf_op jit(solution)/shard_map/ppermute | solution.py:37
  98.2 14.2 %collective-permute-start.19 = (f32[1,64,128]{2,1,0:T(8,128)S(1)}, f32[1,64,128]{2,1,0:T(8,128)S(1)}, u32[]{:S(2)}, u32[]{:S(2)}) collective-permute-start(f32[1,64,128]{2,1,0:T(8,128)S(1)} %broadcast.111), channel_id=1, source_target_pairs={{1,0},{2,1},{3,2},{5,4},{6,5},{7,6},{9,8},{10,9},{11,10},{13,12},{... | collective-permute-start | bytes 98312 | tf_op jit(solution)/shard_map/ppermute | solution.py:23
  99.5 13.5 %collective-permute-start.20 = (f32[1,64,128]{2,1,0:T(8,128)S(1)}, f32[1,64,128]{2,1,0:T(8,128)}, u32[]{:S(2)}, u32[]{:S(2)}) collective-permute-start(f32[1,64,128]{2,1,0:T(8,128)S(1)} %broadcast.111), channel_id=1, source_target_pairs={{0,1},{1,2},{2,3},{4,5},{5,6},{6,7},{8,9},{9,10},{10,11},{12,13},{... | collective-permute-start | bytes 98312 | tf_op jit(solution)/shard_map/ppermute | solution.py:22
  105.3 18.9 %collective-permute-start.18 = (f32[4,64,128]{2,1,0:T(8,128)}, f32[4,64,128]{2,1,0:T(8,128)}, u32[]{:S(2)}, u32[]{:S(2)}) collective-permute-start(f32[4,64,128]{2,1,0:T(8,128)} %broadcast_in_dim.15), channel_id=1, source_target_pairs={{0,16},{4,20},{8,24},{12,28},{16,32},{20,36},{24,40},{28,44},{32,4... | collective-permute-start | bytes 393224 | tf_op jit(solution)/shard_map/ppermute | solution.py:31
  125.7 7.8 %collective-permute-start.22 = (f32[1,64,128]{2,1,0:T(8,128)S(1)}, f32[1,64,128]{2,1,0:T(8,128)S(1)}, u32[]{:S(2)}, u32[]{:S(2)}) collective-permute-start(f32[1,64,128]{2,1,0:T(8,128)S(1)} %get-tuple-element.32), channel_id=1, source_target_pairs={{1,0},{2,1},{3,2},{5,4},{6,5},{7,6},{9,8},{10,9},{11,10},{13,12},{... | collective-permute-start | bytes 98312 | tf_op jit(solution)/shard_map/ppermute | solution.py:23
  131.5 11.9 %collective-permute-start.21 = (f32[4,64,128]{2,1,0:T(8,128)S(1)}, f32[4,64,128]{2,1,0:T(8,128)S(1)}, u32[]{:S(2)}, u32[]{:S(2)}) collective-permute-start(f32[4,64,128]{2,1,0:T(8,128)S(1)} %get-tuple-element.2), channel_id=1, source_target_pairs={{0,16},{4,20},{8,24},{12,28},{16,32},{20,36},{24,40},{28,44},{32,4... | collective-permute-start | bytes 393224 | tf_op jit(solution)/shard_map/ppermute | solution.py:31
  143.6 7.8 %collective-permute-start.25 = (f32[1,64,128]{2,1,0:T(8,128)S(1)}, f32[1,64,128]{2,1,0:T(8,128)S(1)}, u32[]{:S(2)}, u32[]{:S(2)}) collective-permute-start(f32[1,64,128]{2,1,0:T(8,128)S(1)} %get-tuple-element.30), channel_id=1, source_target_pairs={{1,0},{2,1},{3,2},{5,4},{6,5},{7,6},{9,8},{10,9},{11,10},{13,12},{... | collective-permute-start | bytes 98312 | tf_op jit(solution)/shard_map/ppermute | solution.py:23
  149.5 12.7 %collective-permute-start.24 = (f32[4,64,128]{2,1,0:T(8,128)S(1)}, f32[4,64,128]{2,1,0:T(8,128)S(1)}, u32[]{:S(2)}, u32[]{:S(2)}) collective-permute-start(f32[4,64,128]{2,1,0:T(8,128)S(1)} %fusion.124), channel_id=1, source_target_pairs={{0,16},{4,20},{8,24},{12,28},{16,32},{20,36},{24,40},{28,44},{32,4... | collective-permute-start | bytes 393224 | tf_op jit(solution)/shard_map/ppermute | solution.py:31
  162.4 7.8 %collective-permute-start.28 = (f32[1,64,128]{2,1,0:T(8,128)S(1)}, f32[1,64,128]{2,1,0:T(8,128)S(1)}, u32[]{:S(2)}, u32[]{:S(2)}) collective-permute-start(f32[1,64,128]{2,1,0:T(8,128)S(1)} %get-tuple-element.28), channel_id=1, source_target_pairs={{1,0},{2,1},{3,2},{5,4},{6,5},{7,6},{9,8},{10,9},{11,10},{13,12},{... | collective-permute-start | bytes 98312 | tf_op jit(solution)/shard_map/ppermute | solution.py:23
  168.3 12.5 %collective-permute-start.27 = (f32[4,64,128]{2,1,0:T(8,128)S(1)}, f32[4,64,128]{2,1,0:T(8,128)S(1)}, u32[]{:S(2)}, u32[]{:S(2)}) collective-permute-start(f32[4,64,128]{2,1,0:T(8,128)S(1)} %fusion.135), channel_id=1, source_target_pairs={{0,16},{4,20},{8,24},{12,28},{16,32},{20,36},{24,40},{28,44},{32,4... | collective-permute-start | bytes 393224 | tf_op jit(solution)/shard_map/ppermute | solution.py:31
  181.2 15.3 %collective-permute-start.30 = (f32[8,128,128]{2,1,0:T(8,128)S(1)}, f32[8,128,128]{2,1,0:T(8,128)S(1)}, u32[]{:S(2)}, u32[]{:S(2)}) collective-permute-start(f32[8,128,128]{2,1,0:T(8,128)S(1)} %add.361), channel_id=1, source_target_pairs={{0,8},{4,12},{8,16},{12,20},{16,24},{20,28},{24,32},{28,36},{32,40... | collective-permute-start | bytes 1572872 | tf_op jit(solution)/shard_map/ppermute | solution.py:31
  197.2 14.4 %collective-permute-start.33 = (f32[8,128,128]{2,1,0:T(8,128)S(1)}, f32[8,128,128]{2,1,0:T(8,128)S(1)}, u32[]{:S(2)}, u32[]{:S(2)}) collective-permute-start(f32[8,128,128]{2,1,0:T(8,128)S(1)} %fusion.50), channel_id=1, source_target_pairs={{0,8},{4,12},{8,16},{12,20},{16,24},{20,28},{24,32},{28,36},{32,40... | collective-permute-start | bytes 1572872 | tf_op jit(solution)/shard_map/ppermute | solution.py:31
  212.2 13.8 %collective-permute-start.36 = (f32[8,128,128]{2,1,0:T(8,128)S(1)}, f32[8,128,128]{2,1,0:T(8,128)S(1)}, u32[]{:S(2)}, u32[]{:S(2)}) collective-permute-start(f32[8,128,128]{2,1,0:T(8,128)S(1)} %fusion.61), channel_id=1, source_target_pairs={{0,4},{4,8},{8,12},{12,16},{16,20},{20,24},{24,28},{28,32},{32,36}... | collective-permute-start | bytes 1572872 | tf_op jit(solution)/shard_map/ppermute | solution.py:31
  226.7 13.8 %collective-permute-start.39 = (f32[8,128,128]{2,1,0:T(8,128)S(1)}, f32[8,128,128]{2,1,0:T(8,128)S(1)}, u32[]{:S(2)}, u32[]{:S(2)}) collective-permute-start(f32[8,128,128]{2,1,0:T(8,128)S(1)} %fusion.71), channel_id=1, source_target_pairs={{0,4},{4,8},{8,12},{12,16},{16,20},{20,24},{24,28},{28,32},{32,36}... | collective-permute-start | bytes 1572872 | tf_op jit(solution)/shard_map/ppermute | solution.py:31
  241.2 13.8 %collective-permute-start.42 = (f32[8,128,128]{2,1,0:T(8,128)S(1)}, f32[8,128,128]{2,1,0:T(8,128)S(1)}, u32[]{:S(2)}, u32[]{:S(2)}) collective-permute-start(f32[8,128,128]{2,1,0:T(8,128)S(1)} %fusion.81), channel_id=1, source_target_pairs={{0,4},{4,8},{8,12},{12,16},{16,20},{20,24},{24,28},{28,32},{32,36}... | collective-permute-start | bytes 1572872 | tf_op jit(solution)/shard_map/ppermute | solution.py:31
  (25 other events, 161.4 us)
where the time goes:
time: 258 us; the launch traced here: 256 us
  starting transfers between devices  117 us (45%)
  waiting for transfers between devices  106 us (41%)
  other arithmetic  17.1 us (7%)
  local copies, waits for them, and re-layouts  15.8 us (6%)
    ppermute x15, waiting for transfers between devices, shifted(): return lax.ppermute(shard, axis, pairs)  88.7 us
    ppermute x14, starting transfers between devices, padded_2(): before = lax.ppermute(last, axis, up)  64.5 us
    ppermute x15, starting transfers between devices, shifted(): return lax.ppermute(shard, axis, pairs)  30.1 us
    ppermute x14, starting transfers between devices, padded_2(): after = lax.ppermute(first, axis, down)  18.1 us
    ppermute x14, waiting for transfers between devices, padded_2(): before = lax.ppermute(last, axis, up)  14.3 us
    concatenate x14, other arithmetic, padded_2(): shard = jnp.concatenate([before, shard, after], axis=dim)  5.63 us
  transfers between devices with their start and end apart: 45, of which 32 were waited for; matrix products, arithmetic and copies ran while one was open for 9% of the time, Pallas kernels for 0%

commit v1 on v0

v1 whole, which is shorter than its diff:
```python
import jax
import jax.numpy as jnp
from jax import lax
from jax.sharding import PartitionSpec as P

OMEGA = 0.8
FINE = (1.0, 1.0, 1.0)
COARSE = (0.25, 0.25, 1.0)
HALF = 64
ROWS = 80
WIDE = 4


def shifted(value, by):
    peers = lax.axis_size("tm")
    return lax.ppermute(value, "tm", [(i, i + by) for i in range(peers) if 0 <= i + by < peers])


def flipped(value, mask):
    peers = lax.axis_size("tm")
    return lax.ppermute(value, "tm", [(i, i ^ mask) for i in range(peers)])


def crossed(value):
    peers = lax.axis_size("tm")
    pairs = [(i, i + (2 if i & 2 else 6)) for i in range(peers)]
    return lax.ppermute(value, "tm", [(i, j) for i, j in pairs if j < peers])


def faces(value, width, dim=0):
    peers, length = lax.axis_size("space"), value.shape[dim]
    up = [(i, i + 1) for i in range(peers - 1)]
    before = lax.ppermute(lax.slice_in_dim(value, length - width, length, axis=dim), "space", up)
    after = lax.ppermute(
        lax.slice_in_dim(value, 0, width, axis=dim), "space", [(j, i) for i, j in up]
    )
    return before, after


def framed(value, width, dim=0):
    before, after = faces(value, width, dim)
    return jnp.concatenate([before, value, after], axis=dim)


def stencil(v, weights=FINE):
    a, b, d = weights
    m = v[..., 1:-1, :, :]
    lead = [(0, 0)] * (v.ndim - 2)
    px = jnp.pad(m, lead + [(1, 1), (0, 0)])
    py = jnp.pad(m, lead + [(0, 0), (1, 1)])
    return (
        2.0 * (a + b + d) * m
        - a * (v[..., 2:, :, :] + v[..., :-2, :, :])
        - b * (px[..., 2:, :] + px[..., :-2, :])
        - d * (py[..., 2:] + py[..., :-2])
    )


def inner(v, n=1):
    return v[..., n:-n, :, :]


def applied(v, c, weights=FINE):
    return inner(v) + c * stencil(v, weights)


def pair_matrix(rows):
    i = lax.broadcasted_iota(jnp.int32, (rows // 2, rows), 0)
    j = lax.broadcasted_iota(jnp.int32, (rows // 2, rows), 1)
    return (j // 2 == i).astype(jnp.float32)


def coarsen(v):
    z = v[..., 0::2, :, :] + v[..., 1::2, :, :]
    rows = z.shape[-2]
    return 0.25 * jnp.einsum(
        "ij,...jy->...iy", pair_matrix(rows), z, precision=lax.Precision.HIGHEST
    )


def refine(v):
    rows = v.shape[-2] * 2
    wide = jnp.einsum(
        "ij,...iy->...jy", pair_matrix(rows), v, precision=lax.Precision.HIGHEST
    )
    return jnp.repeat(wide, 2, axis=-3)


def body(source, conductivity):
    me = lax.axis_index("tm")
    core = me % 2
    odd_chip = (me // 2) % 2 == 1
    low = core == 0
    planes, rows, _ = conductivity.shape
    k = WIDE

    def window(v, keep):
        return jnp.where(keep, v[:, :ROWS], v[:, rows - ROWS :])

    mine = window(source[0], low)
    got = flipped(window(source[0], ~low), 1)
    even, odd = jnp.where(low, mine, got), jnp.where(low, got, mine)
    bundle = framed(jnp.stack([even, odd, window(conductivity, low)]), k, 1)
    prior_odd = shifted(odd, 2)
    g, cond = bundle[:2], bundle[2]
    d0 = OMEGA / (1.0 + 6.0 * cond)
    d1 = OMEGA / (1.0 + 12.0 * cond)

    c14, c12 = inner(cond, 1), inner(cond, 2)
    u1 = d0 * g
    rest = inner(u1) + inner(d0) * (inner(g) - applied(u1, c14))
    hop = d0 * u1
    odd2 = rest[1] + inner(hop[0])
    w = inner(odd2) - c12 * stencil(inner(hop[1]))
    local = inner(g[0] + g[1], 2) + inner(rest[0]) - applied(rest[0] + odd2, c12)
    g1 = local + shifted(w, 2)

    c10, c8 = 2.0 * inner(cond, 3), 2.0 * inner(cond, 4)
    m1 = inner(d1, 2) * g1
    rest1 = inner(m1) + inner(d1, 3) * (inner(g1) - applied(m1, c10))
    hop1 = inner(d1, 3) * inner(m1)
    own = inner(g1, 2) - applied(rest1, c8)
    nxt = inner(rest1) - applied(hop1, c8)
    carry = inner(hop1)
    pair = coarsen(
        jnp.stack([own + jnp.where(odd_chip, 0.0, nxt), carry + jnp.where(odd_chip, nxt, 0.0)])
    )
    f0, f1 = pair[0], pair[1]
    g2 = (f0 + flipped(f0, 2)) + (shifted(f1, 4) + crossed(f1))

    c2 = 4.0 * coarsen(inner(cond, k))
    d2 = OMEGA / (1.0 + 3.0 * c2)
    coarse = d2 * g2
    for _ in range(3):
        prior = shifted(coarse, 4)
        coarse = coarse + d2 * (g2 + prior - applied(framed(coarse, 1), c2, COARSE))

    e1, b1 = inner(d1, k), inner(g1, 2)
    middle = inner(rest1) + e1 * shifted(inner(m1, 2), 2) + refine(coarse)
    for _ in range(2):
        prior = shifted(middle, 2)
        middle = middle + e1 * (b1 + prior - applied(framed(middle, 1), c8))

    e0, c0, b0 = inner(d0, k), inner(cond, k), inner(g, k)
    even2 = inner(rest[0], 3) + e0 * (e0 * prior_odd)
    state = jnp.stack([even2, inner(odd2, 3)]) + middle

    def residual(v):
        prior = shifted(v[1], 2)
        before = jnp.stack([prior, v[0]])
        return b0 + before - applied(framed(v, 1, 1), c0)

    for _ in range(2):
        state = state + e0 * residual(state)
    last = residual(state)

    def whole(v):
        part = jnp.where(low, v[:, :, :HALF], v[:, :, ROWS - HALF :])
        keep, give = jnp.where(low, part[0], part[1]), jnp.where(low, part[1], part[0])
        other = flipped(give, 1)
        return jnp.concatenate(
            [jnp.where(low, keep, other), jnp.where(low, other, keep)], axis=1
        )

    return whole(state)[None], whole(last)[None]


def solution(mesh):
    return jax.shard_map(
        body,
        mesh=mesh,
        in_specs=(P("tm", "space", None, None), P("space", None, None)),
        out_specs=(P("tm", "space", None, None), P("tm", "space", None, None)),
        check_vma=False,
    )
```

time: 258 us -> 181 us (0.70)
  the two profiles are of different devices: /device:TPU:32 before, /device:TPU:29 now
where the time goes in v1:
time: 181 us; the launch traced here: 180 us
  starting transfers between devices  116 us (64%)
  waiting for transfers between devices  43.7 us (24%)
  other arithmetic  15.5 us (9%)
  local copies, waits for them, and re-layouts  2.48 us (1%)
    ppermute x12, starting transfers between devices, shifted(): lax.ppermute(value, 'tm', [(i, i + by) for i in range(peers) if 0 <= i +...  38.5 us
    ppermute x9, starting transfers between devices, faces(): lax.ppermute(lax.slice_in_dim(value, length - width, length, axis=dim), '...  28.6 us
    ppermute x4, starting transfers between devices, flipped(): return lax.ppermute(value, 'tm', [(i, i ^ mask) for i in range(peers)])  25.5 us
    ppermute x12, waiting for transfers between devices, shifted(): lax.ppermute(value, 'tm', [(i, i + by) for i in range(peers) if 0 <= i +...  20.2 us
    ppermute x9, starting transfers between devices, faces(): lax.ppermute(lax.slice_in_dim(value, 0, width, axis=dim), 'space', [(j, i...  19 us
    ppermute x9, waiting for transfers between devices, faces(): lax.ppermute(lax.slice_in_dim(value, length - width, length, axis=dim), '...  16.3 us
    ppermute x4, waiting for transfers between devices, flipped(): return lax.ppermute(value, 'tm', [(i, i ^ mask) for i in range(peers)])  4.37 us
    ppermute x1, starting transfers between devices, crossed(): return lax.ppermute(value, 'tm', [(i, j) for i, j in pairs if j < peers])  4.35 us
  transfers between devices with their start and end apart: 35, of which 16 were waited for; matrix products, arithmetic and copies ran while one was open for 3% of the time, Pallas kernels for 0%

profile of v1, /device:TPU:29, one launch (start us, length us, event | category | flops | bytes accessed | tf_op | source)
XLA Modules:
  0.0 180.0 jit_solution(6255370117469993302)
XLA Ops:
  5.9 2.8 %collective-permute-start.1 = (f32[3,4,80,128]{3,2,1,0:T(8,128)S(1)}, f32[3,4,80,128]{3,2,1,0:T(8,128)S(1)}, u32[]{:S(2)}, u32[]{:S(2)}) collective-permute-start(f32[3,4,80,128]{3,2,1,0:T(8,128)S(1)} %get-tuple-element.19), channel_id=1, source_target_pairs={{0,1},{1,2},{2,3},{4,5},{5,6},{6,7},{8,9},{9,10},{10,11},{12,13},{... | collective-permute-start | bytes 1474568 | tf_op jit(solution)/shard_map/ppermute | solution.py:33
  11.2 9.0 %collective-permute-done.1 = f32[3,4,80,128]{3,2,1,0:T(8,128)S(1)} collective-permute-done((f32[3,4,80,128]{3,2,1,0:T(8,128)S(1)}, f32[3,4,80,128]{3,2,1,0:T(8,128)S(1)}, u32[]{:S(2)}, u32[]{:S(2)}) %collective-permute-start.1) | collective-permute-done | bytes 491552 | tf_op jit(solution)/shard_map/ppermute | solution.py:33
  28.5 4.0 %collective-permute-start.4 = (f32[12,80,128]{2,1,0:T(8,128)}, f32[12,80,128]{2,1,0:T(8,128)}, u32[]{:S(2)}, u32[]{:S(2)}) collective-permute-start(f32[12,80,128]{2,1,0:T(8,128)} %fusion.53), channel_id=1, source_target_pairs={{0,8},{4,12},{8,16},{12,20},{16,24},{20,28},{24,32},{28,36},{32,40... | collective-permute-start | bytes 1474568 | tf_op jit(solution)/shard_map/ppermute | solution.py:16
  33.7 15.7 %collective-permute-done.4 = f32[12,80,128]{2,1,0:T(8,128)} collective-permute-done((f32[12,80,128]{2,1,0:T(8,128)}, f32[12,80,128]{2,1,0:T(8,128)}, u32[]{:S(2)}, u32[]{:S(2)}) %collective-permute-start.4) | collective-permute-done | bytes 491552 | tf_op jit(solution)/shard_map/ppermute | solution.py:16
  55.3 4.3 %collective-permute-start.8 = (f32[4,40,128]{2,1,0:T(8,128)S(1)}, f32[4,40,128]{2,1,0:T(8,128)S(1)}, u32[]{:S(2)}, u32[]{:S(2)}) collective-permute-start(f32[4,40,128]{2,1,0:T(8,128)S(1)} %get-tuple-element.44), channel_id=1, source_target_pairs={{0,24},{4,28},{8,16},{12,20},{16,40},{20,44},{24,32},{28,36},{32,5... | collective-permute-start | bytes 245768 | tf_op jit(solution)/shard_map/ppermute | solution.py:27
  62.2 2.9 %collective-permute-done.6 = f32[4,40,128]{2,1,0:T(8,128)S(1)} collective-permute-done((f32[4,40,128]{2,1,0:T(8,128)S(1)}, f32[4,40,128]{2,1,0:T(8,128)S(1)}, u32[]{:S(2)}, u32[]{:S(2)}) %collective-permute-start.6) | collective-permute-done | bytes 81952 | tf_op jit(solution)/shard_map/ppermute | solution.py:21
  65.4 3.7 %collective-permute-start.9 = (f32[4,40,128]{2,1,0:T(8,128)S(1)}, f32[4,40,128]{2,1,0:T(8,128)S(1)}, u32[]{:S(2)}, u32[]{:S(2)}) collective-permute-start(f32[4,40,128]{2,1,0:T(8,128)S(1)} %get-tuple-element.2), channel_id=1, source_target_pairs={{0,16},{4,20},{8,24},{12,28},{16,32},{20,36},{24,40},{28,44},{32,4... | collective-permute-start | bytes 245768 | tf_op jit(solution)/shard_map/ppermute | solution.py:16
  71.6 2.8 %collective-permute-start.11 = (f32[1,40,128]{2,1,0:T(8,128)S(1)}, f32[1,40,128]{2,1,0:T(8,128)S(1)}, u32[]{:S(2)}, u32[]{:S(2)}) collective-permute-start(f32[1,40,128]{2,1,0:T(8,128)S(1)} %get-tuple-element.50), channel_id=1, source_target_pairs={{0,1},{1,2},{2,3},{4,5},{5,6},{6,7},{8,9},{9,10},{10,11},{12,13},{... | collective-permute-start | bytes 61448 | tf_op jit(solution)/shard_map/ppermute | solution.py:33
  76.2 4.3 %collective-permute-start.12 = (f32[4,40,128]{2,1,0:T(8,128)S(1)}, f32[4,40,128]{2,1,0:T(8,128)S(1)}, u32[]{:S(2)}, u32[]{:S(2)}) collective-permute-start(f32[4,40,128]{2,1,0:T(8,128)S(1)} %fusion.130), channel_id=1, source_target_pairs={{0,16},{4,20},{8,24},{12,28},{16,32},{20,36},{24,40},{28,44},{32,4... | collective-permute-start | bytes 245768 | tf_op jit(solution)/shard_map/ppermute | solution.py:16
  82.8 3.1 %collective-permute-start.14 = (f32[1,40,128]{2,1,0:T(8,128)S(1)}, f32[1,40,128]{2,1,0:T(8,128)S(1)}, u32[]{:S(2)}, u32[]{:S(2)}) collective-permute-start(f32[1,40,128]{2,1,0:T(8,128)S(1)} %get-tuple-element.48), channel_id=1, source_target_pairs={{0,1},{1,2},{2,3},{4,5},{5,6},{6,7},{8,9},{9,10},{10,11},{12,13},{... | collective-permute-start | bytes 61448 | tf_op jit(solution)/shard_map/ppermute | solution.py:33
  85.9 4.0 %collective-permute-start.5 = (f32[8,80,128]{2,1,0:T(8,128)S(1)}, f32[8,80,128]{2,1,0:T(8,128)S(1)}, u32[]{:S(2)}, u32[]{:S(2)}) collective-permute-start(f32[8,80,128]{2,1,0:T(8,128)S(1)} %slice.778), channel_id=1, source_target_pairs={{0,8},{4,12},{8,16},{12,20},{16,24},{20,28},{24,32},{28,36},{32,40... | collective-permute-start | bytes 983048 | tf_op jit(solution)/shard_map/ppermute | solution.py:16
  90.1 2.9 %collective-permute-start.15 = (f32[4,40,128]{2,1,0:T(8,128)S(1)}, f32[4,40,128]{2,1,0:T(8,128)S(1)}, u32[]{:S(2)}, u32[]{:S(2)}) collective-permute-start(f32[4,40,128]{2,1,0:T(8,128)S(1)} %fusion.139), channel_id=1, source_target_pairs={{0,16},{4,20},{8,24},{12,28},{16,32},{20,36},{24,40},{28,44},{32,4... | collective-permute-start | bytes 245768 | tf_op jit(solution)/shard_map/ppermute | solution.py:16
  95.2 3.1 %collective-permute-start.17 = (f32[1,40,128]{2,1,0:T(8,128)S(1)}, f32[1,40,128]{2,1,0:T(8,128)S(1)}, u32[]{:S(2)}, u32[]{:S(2)}) collective-permute-start(f32[1,40,128]{2,1,0:T(8,128)S(1)} %get-tuple-element.46), channel_id=1, source_target_pairs={{0,1},{1,2},{2,3},{4,5},{5,6},{6,7},{8,9},{9,10},{10,11},{12,13},{... | collective-permute-start | bytes 61448 | tf_op jit(solution)/shard_map/ppermute | solution.py:33
  100.4 3.0 %collective-permute-start.18 = (f32[8,80,128]{2,1,0:T(8,128)S(1)}, f32[8,80,128]{2,1,0:T(8,128)S(1)}, u32[]{:S(2)}, u32[]{:S(2)}) collective-permute-start(f32[8,80,128]{2,1,0:T(8,128)S(1)} %bitcast_add_fusion), channel_id=1, source_target_pairs={{0,8},{4,12},{8,16},{12,20},{16,24},{20,28},{24,32},{28,36},{32,40... | collective-permute-start | bytes 983048 | tf_op jit(solution)/shard_map/ppermute | solution.py:16
  105.5 3.4 %collective-permute-start.20 = (f32[1,80,128]{2,1,0:T(8,128)S(1)}, f32[1,80,128]{2,1,0:T(8,128)S(1)}, u32[]{:S(2)}, u32[]{:S(2)}) collective-permute-start(f32[1,80,128]{2,1,0:T(8,128)S(1)} %get-tuple-element.42), channel_id=1, source_target_pairs={{0,1},{1,2},{2,3},{4,5},{5,6},{6,7},{8,9},{9,10},{10,11},{12,13},{... | collective-permute-start | bytes 122888 | tf_op jit(solution)/shard_map/ppermute | solution.py:33
  108.9 3.4 %collective-permute-start.3 = (f32[8,80,128]{2,1,0:T(8,128)S(1)}, f32[8,80,128]{2,1,0:T(8,128)S(1)}, u32[]{:S(2)}, u32[]{:S(2)}) collective-permute-start(f32[8,80,128]{2,1,0:T(8,128)S(1)} %get-tuple-element.22), channel_id=1, source_target_pairs={{0,8},{4,12},{8,16},{12,20},{16,24},{20,28},{24,32},{28,36},{32,40... | collective-permute-start | bytes 983048 | tf_op jit(solution)/shard_map/ppermute | solution.py:16
  117.3 3.4 %collective-permute-start.23 = (f32[1,80,128]{2,1,0:T(8,128)S(1)}, f32[1,80,128]{2,1,0:T(8,128)S(1)}, u32[]{:S(2)}, u32[]{:S(2)}) collective-permute-start(f32[1,80,128]{2,1,0:T(8,128)S(1)} %get-tuple-element.40), channel_id=1, source_target_pairs={{0,1},{1,2},{2,3},{4,5},{5,6},{6,7},{8,9},{9,10},{10,11},{12,13},{... | collective-permute-start | bytes 122888 | tf_op jit(solution)/shard_map/ppermute | solution.py:33
  124.5 3.9 %collective-permute-start.24 = (f32[8,80,128]{2,1,0:T(8,128)S(1)}, f32[8,80,128]{2,1,0:T(8,128)S(1)}, u32[]{:S(2)}, u32[]{:S(2)}) collective-permute-start(f32[8,80,128]{2,1,0:T(8,128)S(1)} %get-tuple-element.35), channel_id=1, source_target_pairs={{0,8},{4,12},{8,16},{12,20},{16,24},{20,28},{24,32},{28,36},{32,40... | collective-permute-start | bytes 983048 | tf_op jit(solution)/shard_map/ppermute | solution.py:16
  130.4 3.4 %collective-permute-start.26 = (f32[2,1,80,128]{3,2,1,0:T(8,128)S(1)}, f32[2,1,80,128]{3,2,1,0:T(8,128)S(1)}, u32[]{:S(2)}, u32[]{:S(2)}) collective-permute-start(f32[2,1,80,128]{3,2,1,0:T(8,128)S(1)} %get-tuple-element.38), channel_id=1, source_target_pairs={{0,1},{1,2},{2,3},{4,5},{5,6},{6,7},{8,9},{9,10},{10,11},{12,13},{... | collective-permute-start | bytes 245768 | tf_op jit(solution)/shard_map/ppermute | solution.py:33
  136.6 2.7 %collective-permute-start.27 = (f32[8,80,128]{2,1,0:T(8,128)S(1)}, f32[8,80,128]{2,1,0:T(8,128)S(1)}, u32[]{:S(2)}, u32[]{:S(2)}) collective-permute-start(f32[8,80,128]{2,1,0:T(8,128)S(1)} %get-tuple-element.31), channel_id=1, source_target_pairs={{0,8},{4,12},{8,16},{12,20},{16,24},{20,28},{24,32},{28,36},{32,40... | collective-permute-start | bytes 983048 | tf_op jit(solution)/shard_map/ppermute | solution.py:16
  141.2 3.4 %collective-permute-start.29 = (f32[2,1,80,128]{3,2,1,0:T(8,128)S(1)}, f32[2,1,80,128]{3,2,1,0:T(8,128)S(1)}, u32[]{:S(2)}, u32[]{:S(2)}) collective-permute-start(f32[2,1,80,128]{3,2,1,0:T(8,128)S(1)} %get-tuple-element.34), channel_id=1, source_target_pairs={{0,1},{1,2},{2,3},{4,5},{5,6},{6,7},{8,9},{9,10},{10,11},{12,13},{... | collective-permute-start | bytes 245768 | tf_op jit(solution)/shard_map/ppermute | solution.py:33
  153.4 3.4 %collective-permute-start.33 = (f32[2,1,80,128]{3,2,1,0:T(8,128)S(1)}, f32[2,1,80,128]{3,2,1,0:T(8,128)S(1)}, u32[]{:S(2)}, u32[]{:S(2)}) collective-permute-start(f32[2,1,80,128]{3,2,1,0:T(8,128)S(1)} %get-tuple-element.30), channel_id=1, source_target_pairs={{0,1},{1,2},{2,3},{4,5},{5,6},{6,7},{8,9},{9,10},{10,11},{12,13},{... | collective-permute-start | bytes 245768 | tf_op jit(solution)/shard_map/ppermute | solution.py:33
  156.9 17.2 %collective-permute-start.30 = (f32[8,64,128]{2,1,0:T(8,128)S(1)}, f32[8,64,128]{2,1,0:T(8,128)S(1)}, u32[]{:S(2)}, u32[]{:S(2)}) collective-permute-start(f32[8,64,128]{2,1,0:T(8,128)S(1)} %select_bitcast_fusion.2), channel_id=1, source_target_pairs={{0,4},{4,0},{8,12},{12,8},{16,20},{20,16},{24,28},{28,24},{32,36},... | collective-permute-start | bytes 786440 | tf_op jit(solution)/shard_map/ppermute | solution.py:21
  174.7 3.2 %collective-permute-start.34 = (f32[8,64,128]{2,1,0:T(8,128)S(1)}, f32[8,64,128]{2,1,0:T(8,128)S(1)}, u32[]{:S(2)}, u32[]{:S(2)}) collective-permute-start(f32[8,64,128]{2,1,0:T(8,128)S(1)} %select_bitcast_fusion.1), channel_id=1, source_target_pairs={{0,4},{4,0},{8,12},{12,8},{16,20},{20,16},{24,28},{28,24},{32,36},... | collective-permute-start | bytes 786440 | tf_op jit(solution)/shard_map/ppermute | solution.py:21
  (124 shorter events, 65.5 us)
Async XLA Ops:
  5.9 14.3 %collective-permute-start.1 = (f32[3,4,80,128]{3,2,1,0:T(8,128)S(1)}, f32[3,4,80,128]{3,2,1,0:T(8,128)S(1)}, u32[]{:S(2)}, u32[]{:S(2)}) collective-permute-start(f32[3,4,80,128]{3,2,1,0:T(8,128)S(1)} %get-tuple-element.19), channel_id=1, source_target_pairs={{0,1},{1,2},{2,3},{4,5},{5,6},{6,7},{8,9},{9,10},{10,11},{12,13},{... | collective-permute-start | bytes 1474568 | tf_op jit(solution)/shard_map/ppermute | solution.py:33
  8.8 14.0 %collective-permute-start.2 = (f32[3,4,80,128]{3,2,1,0:T(8,128)S(1)}, f32[3,4,80,128]{3,2,1,0:T(8,128)S(1)}, u32[]{:S(2)}, u32[]{:S(2)}) collective-permute-start(f32[3,4,80,128]{3,2,1,0:T(8,128)S(1)} %get-tuple-element.20), channel_id=1, source_target_pairs={{1,0},{2,1},{3,2},{5,4},{6,5},{7,6},{9,8},{10,9},{11,10},{13,12},{... | collective-permute-start | bytes 1474568 | tf_op jit(solution)/shard_map/ppermute | solution.py:34
  28.5 20.9 %collective-permute-start.4 = (f32[12,80,128]{2,1,0:T(8,128)}, f32[12,80,128]{2,1,0:T(8,128)}, u32[]{:S(2)}, u32[]{:S(2)}) collective-permute-start(f32[12,80,128]{2,1,0:T(8,128)} %fusion.53), channel_id=1, source_target_pairs={{0,8},{4,12},{8,16},{12,20},{16,24},{20,28},{24,32},{28,36},{32,40... | collective-permute-start | bytes 1474568 | tf_op jit(solution)/shard_map/ppermute | solution.py:16
  53.4 11.8 %collective-permute-start.7 = (f32[4,40,128]{2,1,0:T(8,128)S(1)}, f32[4,40,128]{2,1,0:T(8,128)S(1)}, u32[]{:S(2)}, u32[]{:S(2)}) collective-permute-start(f32[4,40,128]{2,1,0:T(8,128)S(1)} %get-tuple-element.44), channel_id=1, source_target_pairs={{0,16},{4,20},{8,24},{12,28},{16,32},{20,36},{24,40},{28,44},{32,4... | collective-permute-start | bytes 245768 | tf_op jit(solution)/shard_map/ppermute | solution.py:16
  55.3 9.8 %collective-permute-start.8 = (f32[4,40,128]{2,1,0:T(8,128)S(1)}, f32[4,40,128]{2,1,0:T(8,128)S(1)}, u32[]{:S(2)}, u32[]{:S(2)}) collective-permute-start(f32[4,40,128]{2,1,0:T(8,128)S(1)} %get-tuple-element.44), channel_id=1, source_target_pairs={{0,24},{4,28},{8,16},{12,20},{16,40},{20,44},{24,32},{28,36},{32,5... | collective-permute-start | bytes 245768 | tf_op jit(solution)/shard_map/ppermute | solution.py:27
  59.6 5.5 %collective-permute-start.6 = (f32[4,40,128]{2,1,0:T(8,128)S(1)}, f32[4,40,128]{2,1,0:T(8,128)S(1)}, u32[]{:S(2)}, u32[]{:S(2)}) collective-permute-start(f32[4,40,128]{2,1,0:T(8,128)S(1)} %get-tuple-element.43), channel_id=1, source_target_pairs={{0,8},{4,12},{8,0},{12,4},{16,24},{20,28},{24,16},{28,20},{32,40},... | collective-permute-start | bytes 245768 | tf_op jit(solution)/shard_map/ppermute | solution.py:21
  65.4 10.7 %collective-permute-start.9 = (f32[4,40,128]{2,1,0:T(8,128)S(1)}, f32[4,40,128]{2,1,0:T(8,128)S(1)}, u32[]{:S(2)}, u32[]{:S(2)}) collective-permute-start(f32[4,40,128]{2,1,0:T(8,128)S(1)} %get-tuple-element.2), channel_id=1, source_target_pairs={{0,16},{4,20},{8,24},{12,28},{16,32},{20,36},{24,40},{28,44},{32,4... | collective-permute-start | bytes 245768 | tf_op jit(solution)/shard_map/ppermute | solution.py:16
  76.2 13.8 %collective-permute-start.12 = (f32[4,40,128]{2,1,0:T(8,128)S(1)}, f32[4,40,128]{2,1,0:T(8,128)S(1)}, u32[]{:S(2)}, u32[]{:S(2)}) collective-permute-start(f32[4,40,128]{2,1,0:T(8,128)S(1)} %fusion.130), channel_id=1, source_target_pairs={{0,16},{4,20},{8,24},{12,28},{16,32},{20,36},{24,40},{28,44},{32,4... | collective-permute-start | bytes 245768 | tf_op jit(solution)/shard_map/ppermute | solution.py:16
  80.6 9.4 %collective-permute-start.13 = (f32[1,40,128]{2,1,0:T(8,128)S(1)}, f32[1,40,128]{2,1,0:T(8,128)S(1)}, u32[]{:S(2)}, u32[]{:S(2)}) collective-permute-start(f32[1,40,128]{2,1,0:T(8,128)S(1)} %get-tuple-element.47), channel_id=1, source_target_pairs={{1,0},{2,1},{3,2},{5,4},{6,5},{7,6},{9,8},{10,9},{11,10},{13,12},{... | collective-permute-start | bytes 61448 | tf_op jit(solution)/shard_map/ppermute | solution.py:34
  82.8 7.2 %collective-permute-start.14 = (f32[1,40,128]{2,1,0:T(8,128)S(1)}, f32[1,40,128]{2,1,0:T(8,128)S(1)}, u32[]{:S(2)}, u32[]{:S(2)}) collective-permute-start(f32[1,40,128]{2,1,0:T(8,128)S(1)} %get-tuple-element.48), channel_id=1, source_target_pairs={{0,1},{1,2},{2,3},{4,5},{5,6},{6,7},{8,9},{9,10},{10,11},{12,13},{... | collective-permute-start | bytes 61448 | tf_op jit(solution)/shard_map/ppermute | solution.py:33
  85.9 14.4 %collective-permute-start.5 = (f32[8,80,128]{2,1,0:T(8,128)S(1)}, f32[8,80,128]{2,1,0:T(8,128)S(1)}, u32[]{:S(2)}, u32[]{:S(2)}) collective-permute-start(f32[8,80,128]{2,1,0:T(8,128)S(1)} %slice.778), channel_id=1, source_target_pairs={{0,8},{4,12},{8,16},{12,20},{16,24},{20,28},{24,32},{28,36},{32,40... | collective-permute-start | bytes 983048 | tf_op jit(solution)/shard_map/ppermute | solution.py:16
  90.1 9.9 %collective-permute-start.15 = (f32[4,40,128]{2,1,0:T(8,128)S(1)}, f32[4,40,128]{2,1,0:T(8,128)S(1)}, u32[]{:S(2)}, u32[]{:S(2)}) collective-permute-start(f32[4,40,128]{2,1,0:T(8,128)S(1)} %fusion.139), channel_id=1, source_target_pairs={{0,16},{4,20},{8,24},{12,28},{16,32},{20,36},{24,40},{28,44},{32,4... | collective-permute-start | bytes 245768 | tf_op jit(solution)/shard_map/ppermute | solution.py:16
  100.4 11.9 %collective-permute-start.18 = (f32[8,80,128]{2,1,0:T(8,128)S(1)}, f32[8,80,128]{2,1,0:T(8,128)S(1)}, u32[]{:S(2)}, u32[]{:S(2)}) collective-permute-start(f32[8,80,128]{2,1,0:T(8,128)S(1)} %bitcast_add_fusion), channel_id=1, source_target_pairs={{0,8},{4,12},{8,16},{12,20},{16,24},{20,28},{24,32},{28,36},{32,40... | collective-permute-start | bytes 983048 | tf_op jit(solution)/shard_map/ppermute | solution.py:16
  103.5 8.8 %collective-permute-start.19 = (f32[1,80,128]{2,1,0:T(8,128)S(1)}, f32[1,80,128]{2,1,0:T(8,128)S(1)}, u32[]{:S(2)}, u32[]{:S(2)}) collective-permute-start(f32[1,80,128]{2,1,0:T(8,128)S(1)} %get-tuple-element.41), channel_id=1, source_target_pairs={{1,0},{2,1},{3,2},{5,4},{6,5},{7,6},{9,8},{10,9},{11,10},{13,12},{... | collective-permute-start | bytes 122888 | tf_op jit(solution)/shard_map/ppermute | solution.py:34
  105.5 6.8 %collective-permute-start.20 = (f32[1,80,128]{2,1,0:T(8,128)S(1)}, f32[1,80,128]{2,1,0:T(8,128)S(1)}, u32[]{:S(2)}, u32[]{:S(2)}) collective-permute-start(f32[1,80,128]{2,1,0:T(8,128)S(1)} %get-tuple-element.42), channel_id=1, source_target_pairs={{0,1},{1,2},{2,3},{4,5},{5,6},{6,7},{8,9},{9,10},{10,11},{12,13},{... | collective-permute-start | bytes 122888 | tf_op jit(solution)/shard_map/ppermute | solution.py:33
  108.9 11.8 %collective-permute-start.3 = (f32[8,80,128]{2,1,0:T(8,128)S(1)}, f32[8,80,128]{2,1,0:T(8,128)S(1)}, u32[]{:S(2)}, u32[]{:S(2)}) collective-permute-start(f32[8,80,128]{2,1,0:T(8,128)S(1)} %get-tuple-element.22), channel_id=1, source_target_pairs={{0,8},{4,12},{8,16},{12,20},{16,24},{20,28},{24,32},{28,36},{32,40... | collective-permute-start | bytes 983048 | tf_op jit(solution)/shard_map/ppermute | solution.py:16
  112.7 11.4 %collective-permute-start.21 = (f32[8,80,128]{2,1,0:T(8,128)S(1)}, f32[8,80,128]{2,1,0:T(8,128)S(1)}, u32[]{:S(2)}, u32[]{:S(2)}) collective-permute-start(f32[8,80,128]{2,1,0:T(8,128)S(1)} %fusion.95), channel_id=1, source_target_pairs={{0,8},{4,12},{8,16},{12,20},{16,24},{20,28},{24,32},{28,36},{32,40... | collective-permute-start | bytes 983048 | tf_op jit(solution)/shard_map/ppermute | solution.py:16
  115.4 6.4 %collective-permute-start.22 = (f32[1,80,128]{2,1,0:T(8,128)S(1)}, f32[1,80,128]{2,1,0:T(8,128)S(1)}, u32[]{:S(2)}, u32[]{:S(2)}) collective-permute-start(f32[1,80,128]{2,1,0:T(8,128)S(1)} %get-tuple-element.39), channel_id=1, source_target_pairs={{1,0},{2,1},{3,2},{5,4},{6,5},{7,6},{9,8},{10,9},{11,10},{13,12},{... | collective-permute-start | bytes 122888 | tf_op jit(solution)/shard_map/ppermute | solution.py:34
  124.5 11.4 %collective-permute-start.24 = (f32[8,80,128]{2,1,0:T(8,128)S(1)}, f32[8,80,128]{2,1,0:T(8,128)S(1)}, u32[]{:S(2)}, u32[]{:S(2)}) collective-permute-start(f32[8,80,128]{2,1,0:T(8,128)S(1)} %get-tuple-element.35), channel_id=1, source_target_pairs={{0,8},{4,12},{8,16},{12,20},{16,24},{20,28},{24,32},{28,36},{32,40... | collective-permute-start | bytes 983048 | tf_op jit(solution)/shard_map/ppermute | solution.py:16
  136.6 12.3 %collective-permute-start.27 = (f32[8,80,128]{2,1,0:T(8,128)S(1)}, f32[8,80,128]{2,1,0:T(8,128)S(1)}, u32[]{:S(2)}, u32[]{:S(2)}) collective-permute-start(f32[8,80,128]{2,1,0:T(8,128)S(1)} %get-tuple-element.31), channel_id=1, source_target_pairs={{0,8},{4,12},{8,16},{12,20},{16,24},{20,28},{24,32},{28,36},{32,40... | collective-permute-start | bytes 983048 | tf_op jit(solution)/shard_map/ppermute | solution.py:16
  149.6 24.6 %collective-permute-start.31 = (f32[8,80,128]{2,1,0:T(8,128)S(1)}, f32[8,80,128]{2,1,0:T(8,128)S(1)}, u32[]{:S(2)}, u32[]{:S(2)}) collective-permute-start(f32[8,80,128]{2,1,0:T(8,128)S(1)} %get-tuple-element.27), channel_id=1, source_target_pairs={{0,8},{4,12},{8,16},{12,20},{16,24},{20,28},{24,32},{28,36},{32,40... | collective-permute-start | bytes 983048 | tf_op jit(solution)/shard_map/ppermute | solution.py:16
  151.5 22.6 %collective-permute-start.32 = (f32[2,1,80,128]{3,2,1,0:T(8,128)S(1)}, f32[2,1,80,128]{3,2,1,0:T(8,128)S(1)}, u32[]{:S(2)}, u32[]{:S(2)}) collective-permute-start(f32[2,1,80,128]{3,2,1,0:T(8,128)S(1)} %get-tuple-element.29), channel_id=1, source_target_pairs={{1,0},{2,1},{3,2},{5,4},{6,5},{7,6},{9,8},{10,9},{11,10},{13,12},{... | collective-permute-start | bytes 245768 | tf_op jit(solution)/shard_map/ppermute | solution.py:34
  153.4 20.7 %collective-permute-start.33 = (f32[2,1,80,128]{3,2,1,0:T(8,128)S(1)}, f32[2,1,80,128]{3,2,1,0:T(8,128)S(1)}, u32[]{:S(2)}, u32[]{:S(2)}) collective-permute-start(f32[2,1,80,128]{3,2,1,0:T(8,128)S(1)} %get-tuple-element.30), channel_id=1, source_target_pairs={{0,1},{1,2},{2,3},{4,5},{5,6},{6,7},{8,9},{9,10},{10,11},{12,13},{... | collective-permute-start | bytes 245768 | tf_op jit(solution)/shard_map/ppermute | solution.py:33
  156.9 21.1 %collective-permute-start.30 = (f32[8,64,128]{2,1,0:T(8,128)S(1)}, f32[8,64,128]{2,1,0:T(8,128)S(1)}, u32[]{:S(2)}, u32[]{:S(2)}) collective-permute-start(f32[8,64,128]{2,1,0:T(8,128)S(1)} %select_bitcast_fusion.2), channel_id=1, source_target_pairs={{0,4},{4,0},{8,12},{12,8},{16,20},{20,16},{24,28},{28,24},{32,36},... | collective-permute-start | bytes 786440 | tf_op jit(solution)/shard_map/ppermute | solution.py:21
  (19 other events, 109.7 us)

commit v2 on v1

v2 whole, which is shorter than its diff:
```python
import jax
import jax.numpy as jnp
from jax import lax
from jax.sharding import PartitionSpec as P

OMEGA = 0.8
FINE = (1.0, 1.0, 1.0)
COARSE = (0.25, 0.25, 1.0)
HALF = 64
ROWS = 80
NARROW = 72


def shifted(value, by):
    peers = lax.axis_size("tm")
    return lax.ppermute(value, "tm", [(i, i + by) for i in range(peers) if 0 <= i + by < peers])


def flipped(value, mask):
    peers = lax.axis_size("tm")
    return lax.ppermute(value, "tm", [(i, i ^ mask) for i in range(peers)])


def exchanged(upward, downward):
    peers = lax.axis_size("space")
    up = [(i, i + 1) for i in range(peers - 1)]
    below = lax.ppermute(upward, "space", up)
    above = lax.ppermute(downward, "space", [(j, i) for i, j in up])
    return below, above


def framed(value, width, dim=0):
    length = value.shape[dim]
    before, after = exchanged(
        lax.slice_in_dim(value, length - width, length, axis=dim),
        lax.slice_in_dim(value, 0, width, axis=dim),
    )
    return jnp.concatenate([before, value, after], axis=dim)


def stencil(v, weights=FINE):
    a, b, d = weights
    m = v[..., 1:-1, :, :]
    lead = [(0, 0)] * (v.ndim - 2)
    px = jnp.pad(m, lead + [(1, 1), (0, 0)])
    py = jnp.pad(m, lead + [(0, 0), (1, 1)])
    return (
        2.0 * (a + b + d) * m
        - a * (v[..., 2:, :, :] + v[..., :-2, :, :])
        - b * (px[..., 2:, :] + px[..., :-2, :])
        - d * (py[..., 2:] + py[..., :-2])
    )


def inner(v, n=1):
    return v[..., n:-n, :, :]


def applied(v, c, weights=FINE):
    return inner(v) + c * stencil(v, weights)


def pair_matrix(rows):
    i = lax.broadcasted_iota(jnp.int32, (rows // 2, rows), 0)
    j = lax.broadcasted_iota(jnp.int32, (rows // 2, rows), 1)
    return (j // 2 == i).astype(jnp.float32)


def coarsen(v):
    z = v[..., 0::2, :, :] + v[..., 1::2, :, :]
    rows = z.shape[-2]
    return 0.25 * jnp.einsum(
        "ij,...jy->...iy", pair_matrix(rows), z, precision=lax.Precision.HIGHEST
    )


def refine(v):
    rows = v.shape[-2] * 2
    wide = jnp.einsum(
        "ij,...iy->...jy", pair_matrix(rows), v, precision=lax.Precision.HIGHEST
    )
    return jnp.repeat(wide, 2, axis=-3)


def body(source, conductivity):
    me = lax.axis_index("tm")
    odd_chip = (me // 2) % 2 == 1
    low = me % 2 == 0
    planes, rows, _ = conductivity.shape

    def window(v, keep):
        return jnp.where(keep, v[:, :ROWS], v[:, rows - ROWS :])

    def narrow(v):
        return jnp.where(low, v[..., :NARROW, :], v[..., ROWS - NARROW :, :])

    mine = window(source[0], low)
    got = flipped(window(source[0], ~low), 1)
    even, odd = jnp.where(low, mine, got), jnp.where(low, got, mine)
    prior_odd = shifted(odd, 2)
    bundle = framed(jnp.stack([even, odd, window(conductivity, low)]), 2, 1)
    bundle, prior_odd = lax.optimization_barrier((bundle, prior_odd))
    g, cond = bundle[:2], bundle[2]
    d0 = OMEGA / (1.0 + 6.0 * cond)
    d1 = OMEGA / (1.0 + 12.0 * cond)

    c10, c8 = inner(cond, 1), inner(cond, 2)
    u1 = d0 * g
    rest = inner(u1) + inner(d0) * (inner(g) - applied(u1, c10))
    hop = inner(d0) * inner(u1)
    odd2 = rest[1] + hop[0]
    w = inner(odd2) - c8 * stencil(hop[1])
    local = inner(g[0] + g[1], 2) + inner(rest[0]) - applied(rest[0] + odd2, c8)
    g1 = local + shifted(w, 2)

    def spill(v, n):
        return jnp.pad(v, ((n, n), (0, 0), (0, 0)))

    m1 = inner(d1, 2) * g1
    rest1 = spill(m1, 1) + inner(d1) * (spill(g1, 1) - applied(spill(m1, 2), 2.0 * c10))
    hop1 = inner(d1, 2) * m1
    own = spill(g1, 2) - applied(spill(rest1, 2), 2.0 * cond)
    nxt = spill(rest1, 1) - applied(spill(hop1, 3), 2.0 * cond)
    carry = spill(hop1, 2)
    pair = coarsen(
        jnp.stack([own + jnp.where(odd_chip, 0.0, nxt), carry + jnp.where(odd_chip, nxt, 0.0)])
    )
    pair = pair + flipped(pair, 2)

    c2 = 4.0 * coarsen(inner(cond, 2))
    split = g1.reshape(planes, 2, ROWS // 2, g1.shape[-1])
    below, above = exchanged(
        jnp.concatenate([pair[0, -5:], pair[1, -5:], c2[-3:], split[-1]]),
        jnp.concatenate([pair[0, :5], pair[1, :5], c2[:3], split[0]]),
    )

    def joined(part, lower, upper):
        first = part[1:2] + lower[4:5]
        last = part[-2:-1] + upper[0:1]
        before = jnp.concatenate([lower[1:3], lower[3:4] + part[0:1]])
        after = jnp.concatenate([upper[1:2] + part[-1:], upper[2:4]])
        return jnp.concatenate([before, first, part[2:-2], last, after])

    right = [
        joined(pair[i], below[5 * i : 5 * i + 5], above[5 * i : 5 * i + 5]) for i in range(2)
    ]
    c2 = jnp.concatenate([below[10:13], c2, above[10:13]])
    g1_wide = jnp.concatenate(
        [below[13:15].reshape(1, ROWS, -1), g1, above[13:15].reshape(1, ROWS, -1)]
    )
    d2 = OMEGA / (1.0 + 3.0 * c2)
    base = [d2 * v for v in right]
    share = list(base)
    for _ in range(3):
        c2 = inner(c2)
        d2 = inner(d2)
        base = [inner(v) for v in base]
        kept = [inner(v) - d2 * applied(v, c2, COARSE) for v in share]
        moved = [d2 * inner(v) for v in share]
        share = [
            sum(
                ([kept[j]] if j < len(kept) else [])
                + ([moved[j - 1]] if j else [])
                + ([base[j]] if j < 2 else [])
            )
            for j in range(len(kept) + 1)
        ]
    coarse = share[0]
    arrived = [shifted(share[j], 4 * j) for j in range(1, 5)]
    coarse = coarse + (arrived[0] + arrived[1]) + (arrived[2] + arrived[3])

    e1, b1, cc = narrow(inner(d1, 2)), narrow(g1), narrow(2.0 * c8)
    m1_wide = inner(d1) * g1_wide
    rest1 = m1 + inner(d1, 2) * (g1 - applied(m1_wide, 2.0 * c8))
    middle = narrow(rest1 + inner(d1, 2) * shifted(m1, 2) + refine(coarse))
    for _ in range(2):
        prior = shifted(middle, 2)
        middle = middle + e1 * (b1 + prior - applied(framed(middle, 1), cc))

    def half(v):
        return jnp.where(low, v[..., :HALF, :], v[..., v.shape[-2] - HALF :, :])

    e0 = half(inner(d0, 2))
    pre = [half(inner(rest[0])) + e0 * (e0 * half(prior_odd)), half(inner(odd2))]
    top = half(middle)
    keep = jnp.where(low, pre[0], pre[1]) + top
    other = flipped(jnp.where(low, pre[1], pre[0]) + top, 1)
    state = jnp.concatenate([jnp.where(low, keep, other), jnp.where(low, other, keep)], axis=1)
    b0 = source[0]
    d0 = OMEGA / (1.0 + 6.0 * conductivity)
    for _ in range(2):
        prior = shifted(state, 1)
        state = state + d0 * (b0 + prior - applied(framed(state, 1), conductivity))
    prior = shifted(state, 1)
    last = b0 + prior - applied(framed(state, 1), conductivity)
    return state[None], last[None]


def solution(mesh):
    return jax.shard_map(
        body,
        mesh=mesh,
        in_specs=(P("tm", "space", None, None), P("space", None, None)),
        out_specs=(P("tm", "space", None, None), P("tm", "space", None, None)),
        check_vma=False,
    )
```

time: 181 us -> 164 us (0.906)
  the two profiles are of different devices: /device:TPU:29 before, /device:TPU:38 now
where the time goes in v2:
time: 164 us; the launch traced here: 163 us
  waiting for transfers between devices  75.9 us (46%)
  starting transfers between devices  73.6 us (45%)
  other arithmetic  10.4 us (6%)
    ppermute x12, waiting for transfers between devices, shifted(): lax.ppermute(value, 'tm', [(i, i + by) for i in range(peers) if 0 <= i +...  38.6 us
    ppermute x12, starting transfers between devices, shifted(): lax.ppermute(value, 'tm', [(i, i + by) for i in range(peers) if 0 <= i +...  35.1 us
    ppermute x7, starting transfers between devices, exchanged(): above = lax.ppermute(downward, 'space', [(j, i) for i, j in up])  23.6 us
    ppermute x7, waiting for transfers between devices, exchanged(): below = lax.ppermute(upward, 'space', up)  22.6 us
    ppermute x7, starting transfers between devices, exchanged(): below = lax.ppermute(upward, 'space', up)  9.04 us
    ppermute x3, waiting for transfers between devices, flipped(): return lax.ppermute(value, 'tm', [(i, i ^ mask) for i in range(peers)])  8.1 us
    ppermute x7, waiting for transfers between devices, exchanged(): above = lax.ppermute(downward, 'space', [(j, i) for i, j in up])  6.54 us
    ppermute x3, starting transfers between devices, flipped(): return lax.ppermute(value, 'tm', [(i, i ^ mask) for i in range(peers)])  5.76 us
  transfers between devices with their start and end apart: 29, of which 24 were waited for; matrix products, arithmetic and copies ran while one was open for 2% of the time, Pallas kernels for 0%

profile of v2, /device:TPU:38, one launch (start us, length us, event | category | flops | bytes accessed | tf_op | source)
XLA Modules:
  0.0 162.7 jit_solution(11145076609656242834)
XLA Ops:
  6.8 4.6 %collective-permute-start.2 = (f32[3,2,80,128]{3,2,1,0:T(8,128)S(1)}, f32[3,2,80,128]{3,2,1,0:T(8,128)S(1)}, u32[]{:S(2)}, u32[]{:S(2)}) collective-permute-start(f32[3,2,80,128]{3,2,1,0:T(8,128)S(1)} %get-tuple-element.27), channel_id=1, source_target_pairs={{1,0},{2,1},{3,2},{5,4},{6,5},{7,6},{9,8},{10,9},{11,10},{13,12},{... | collective-permute-start | bytes 737288 | tf_op jit(solution)/shard_map/ppermute | solution.py:28
  11.4 4.3 %collective-permute-start.3 = (f32[8,80,128]{2,1,0:T(8,128)S(1)}, f32[8,80,128]{2,1,0:T(8,128)S(1)}, u32[]{:S(2)}, u32[]{:S(2)}) collective-permute-start(f32[8,80,128]{2,1,0:T(8,128)S(1)} %get-tuple-element.29), channel_id=1, source_target_pairs={{0,8},{4,12},{8,16},{12,20},{16,24},{20,28},{24,32},{28,36},{32,40... | collective-permute-start | bytes 983048 | tf_op jit(solution)/shard_map/ppermute | solution.py:16
  16.6 13.0 %collective-permute-done.3 = f32[8,80,128]{2,1,0:T(8,128)S(1)} collective-permute-done((f32[8,80,128]{2,1,0:T(8,128)S(1)}, f32[8,80,128]{2,1,0:T(8,128)S(1)}, u32[]{:S(2)}, u32[]{:S(2)}) %collective-permute-start.3) | collective-permute-done | bytes 327712 | tf_op jit(solution)/shard_map/ppermute | solution.py:16
  33.3 11.6 %collective-permute-done.4 = f32[8,80,128]{2,1,0:T(8,128)S(1)} collective-permute-done((f32[8,80,128]{2,1,0:T(8,128)S(1)}, f32[8,80,128]{2,1,0:T(8,128)S(1)}, u32[]{:S(2)}, u32[]{:S(2)}) %collective-permute-start.4) | collective-permute-done | bytes 327712 | tf_op jit(solution)/shard_map/ppermute | solution.py:16
  49.3 6.1 %collective-permute-done.5 = f32[2,6,40,128]{3,2,1,0:T(8,128)S(1)} collective-permute-done((f32[2,6,40,128]{3,2,1,0:T(8,128)S(1)}, f32[2,6,40,128]{3,2,1,0:T(8,128)S(1)}, u32[]{:S(2)}, u32[]{:S(2)}) %collective-permute-start.5) | collective-permute-done | bytes 245792 | tf_op jit(solution)/shard_map/ppermute | solution.py:21
  58.8 4.6 %collective-permute-start.7 = (f32[15,40,128]{2,1,0:T(8,128)S(1)}, f32[15,40,128]{2,1,0:T(8,128)S(1)}, u32[]{:S(2)}, u32[]{:S(2)}) collective-permute-start(f32[15,40,128]{2,1,0:T(8,128)S(1)} %pad_maximum_fusion.12), channel_id=1, source_target_pairs={{1,0},{2,1},{3,2},{5,4},{6,5},{7,6},{9,8},{10,9},{11,10},{13,12},{... | collective-permute-start | bytes 921608 | tf_op jit(solution)/shard_map/ppermute | solution.py:28
  64.3 3.4 %collective-permute-done.7 = f32[15,40,128]{2,1,0:T(8,128)S(1)} collective-permute-done((f32[15,40,128]{2,1,0:T(8,128)S(1)}, f32[15,40,128]{2,1,0:T(8,128)S(1)}, u32[]{:S(2)}, u32[]{:S(2)}) %collective-permute-start.7) | collective-permute-done | bytes 307232 | tf_op jit(solution)/shard_map/ppermute | solution.py:28
  70.8 4.1 %collective-permute-start.10 = (f32[4,40,128]{2,1,0:T(8,128)S(1)}, f32[4,40,128]{2,1,0:T(8,128)S(1)}, u32[]{:S(2)}, u32[]{:S(2)}) collective-permute-start(f32[4,40,128]{2,1,0:T(8,128)S(1)} %get-tuple-element.48), channel_id=1, source_target_pairs={{0,32},{4,36},{8,40},{12,44},{16,48},{20,52},{24,56},{28,60},{32,6... | collective-permute-start | bytes 245768 | tf_op jit(solution)/shard_map/ppermute | solution.py:16
  75.0 4.5 %collective-permute-start.11 = (f32[4,40,128]{2,1,0:T(8,128)S(1)}, f32[4,40,128]{2,1,0:T(8,128)S(1)}, u32[]{:S(2)}, u32[]{:S(2)}) collective-permute-start(f32[4,40,128]{2,1,0:T(8,128)S(1)} %get-tuple-element.49), channel_id=1, source_target_pairs={{0,48},{4,52},{8,56},{12,60},{16,64},{20,68},{24,72},{28,76},{32,8... | collective-permute-start | bytes 245768 | tf_op jit(solution)/shard_map/ppermute | solution.py:16
  79.5 2.6 %collective-permute-start.12 = (f32[4,40,128]{2,1,0:T(8,128)S(1)}, f32[4,40,128]{2,1,0:T(8,128)S(1)}, u32[]{:S(2)}, u32[]{:S(2)}) collective-permute-start(f32[4,40,128]{2,1,0:T(8,128)S(1)} %get-tuple-element.53), channel_id=1, source_target_pairs={{0,64},{4,68},{8,72},{12,76},{16,80},{20,84},{24,88},{28,92},{32,9... | collective-permute-start | bytes 245768 | tf_op jit(solution)/shard_map/ppermute | solution.py:16
  87.8 3.9 %collective-permute-start.13 = (f32[8,72,128]{2,1,0:T(8,128)S(1)}, f32[8,72,128]{2,1,0:T(8,128)S(1)}, u32[]{:S(2)}, u32[]{:S(2)}) collective-permute-start(f32[8,72,128]{2,1,0:T(8,128)S(1)} %slice_select_fusion.5), channel_id=1, source_target_pairs={{0,8},{4,12},{8,16},{12,20},{16,24},{20,28},{24,32},{28,36},{32,40... | collective-permute-start | bytes 884744 | tf_op jit(solution)/shard_map/ppermute | solution.py:16
  91.8 4.4 %collective-permute-start.14 = (f32[1,72,128]{2,1,0:T(8,128)S(1)}, f32[1,72,128]{2,1,0:T(8,128)S(1)}, u32[]{:S(2)}, u32[]{:S(2)}) collective-permute-start(f32[1,72,128]{2,1,0:T(8,128)S(1)} %get-tuple-element.64), channel_id=1, source_target_pairs={{1,0},{2,1},{3,2},{5,4},{6,5},{7,6},{9,8},{10,9},{11,10},{13,12},{... | collective-permute-start | bytes 110600 | tf_op jit(solution)/shard_map/ppermute | solution.py:28
  97.8 4.2 %collective-permute-done.15 = f32[1,72,128]{2,1,0:T(8,128)S(1)} collective-permute-done((f32[1,72,128]{2,1,0:T(8,128)S(1)}, f32[1,72,128]{2,1,0:T(8,128)S(1)}, u32[]{:S(2)}, u32[]{:S(2)}) %collective-permute-start.15) | collective-permute-done | bytes 36896 | tf_op jit(solution)/shard_map/ppermute | solution.py:27
  102.3 3.9 %collective-permute-start.16 = (f32[8,72,128]{2,1,0:T(8,128)S(1)}, f32[8,72,128]{2,1,0:T(8,128)S(1)}, u32[]{:S(2)}, u32[]{:S(2)}) collective-permute-start(f32[8,72,128]{2,1,0:T(8,128)S(1)} %fusion.116), channel_id=1, source_target_pairs={{0,8},{4,12},{8,16},{12,20},{16,24},{20,28},{24,32},{28,36},{32,40... | collective-permute-start | bytes 884744 | tf_op jit(solution)/shard_map/ppermute | solution.py:16
  106.2 2.7 %collective-permute-start.17 = (f32[1,72,128]{2,1,0:T(8,128)S(1)}, f32[1,72,128]{2,1,0:T(8,128)S(1)}, u32[]{:S(2)}, u32[]{:S(2)}) collective-permute-start(f32[1,72,128]{2,1,0:T(8,128)S(1)} %get-tuple-element.62), channel_id=1, source_target_pairs={{1,0},{2,1},{3,2},{5,4},{6,5},{7,6},{9,8},{10,9},{11,10},{13,12},{... | collective-permute-start | bytes 110600 | tf_op jit(solution)/shard_map/ppermute | solution.py:28
  110.6 4.2 %collective-permute-done.18 = f32[1,72,128]{2,1,0:T(8,128)S(1)} collective-permute-done((f32[1,72,128]{2,1,0:T(8,128)S(1)}, f32[1,72,128]{2,1,0:T(8,128)S(1)}, u32[]{:S(2)}, u32[]{:S(2)}) %collective-permute-start.18) | collective-permute-done | bytes 36896 | tf_op jit(solution)/shard_map/ppermute | solution.py:27
  121.1 2.5 %collective-permute-start.21 = (f32[1,128,128]{2,1,0:T(8,128)S(1)}, f32[1,128,128]{2,1,0:T(8,128)S(1)}, u32[]{:S(2)}, u32[]{:S(2)}) collective-permute-start(f32[1,128,128]{2,1,0:T(8,128)S(1)} %get-tuple-element.46), channel_id=1, source_target_pairs={{1,0},{2,1},{3,2},{5,4},{6,5},{7,6},{9,8},{10,9},{11,10},{13,12},{... | collective-permute-start | bytes 196616 | tf_op jit(solution)/shard_map/ppermute | solution.py:28
  125.5 4.7 %collective-permute-done.22 = f32[1,128,128]{2,1,0:T(8,128)S(1)} collective-permute-done((f32[1,128,128]{2,1,0:T(8,128)S(1)}, f32[1,128,128]{2,1,0:T(8,128)S(1)}, u32[]{:S(2)}, u32[]{:S(2)}) %collective-permute-start.22) | collective-permute-done | bytes 65568 | tf_op jit(solution)/shard_map/ppermute | solution.py:27
  130.2 2.7 %collective-permute-done.20 = f32[8,128,128]{2,1,0:T(8,128)S(1)} collective-permute-done((f32[8,128,128]{2,1,0:T(8,128)S(1)}, f32[8,128,128]{2,1,0:T(8,128)S(1)}, u32[]{:S(2)}, u32[]{:S(2)}) %collective-permute-start.20) | collective-permute-done | bytes 524320 | tf_op jit(solution)/shard_map/ppermute | solution.py:16
  139.7 4.3 %collective-permute-done.25 = f32[1,128,128]{2,1,0:T(8,128)S(1)} collective-permute-done((f32[1,128,128]{2,1,0:T(8,128)S(1)}, f32[1,128,128]{2,1,0:T(8,128)S(1)}, u32[]{:S(2)}, u32[]{:S(2)}) %collective-permute-start.25) | collective-permute-done | bytes 65568 | tf_op jit(solution)/shard_map/ppermute | solution.py:27
  143.9 3.2 %collective-permute-done.23 = f32[8,128,128]{2,1,0:T(8,128)S(1)} collective-permute-done((f32[8,128,128]{2,1,0:T(8,128)S(1)}, f32[8,128,128]{2,1,0:T(8,128)S(1)}, u32[]{:S(2)}, u32[]{:S(2)}) %collective-permute-start.23) | collective-permute-done | bytes 524320 | tf_op jit(solution)/shard_map/ppermute | solution.py:16
  149.6 2.5 %collective-permute-start.27 = (f32[1,128,128]{2,1,0:T(8,128)S(1)}, f32[1,128,128]{2,1,0:T(8,128)S(1)}, u32[]{:S(2)}, u32[]{:S(2)}) collective-permute-start(f32[1,128,128]{2,1,0:T(8,128)S(1)} %get-tuple-element.42), channel_id=1, source_target_pairs={{1,0},{2,1},{3,2},{5,4},{6,5},{7,6},{9,8},{10,9},{11,10},{13,12},{... | collective-permute-start | bytes 196616 | tf_op jit(solution)/shard_map/ppermute | solution.py:28
  154.0 4.3 %collective-permute-done.28 = f32[1,128,128]{2,1,0:T(8,128)S(1)} collective-permute-done((f32[1,128,128]{2,1,0:T(8,128)S(1)}, f32[1,128,128]{2,1,0:T(8,128)S(1)}, u32[]{:S(2)}, u32[]{:S(2)}) %collective-permute-start.28) | collective-permute-done | bytes 65568 | tf_op jit(solution)/shard_map/ppermute | solution.py:27
  158.3 3.2 %collective-permute-done.26 = f32[8,128,128]{2,1,0:T(8,128)S(1)} collective-permute-done((f32[8,128,128]{2,1,0:T(8,128)S(1)}, f32[8,128,128]{2,1,0:T(8,128)S(1)}, u32[]{:S(2)}, u32[]{:S(2)}) %collective-permute-start.26) | collective-permute-done | bytes 524320 | tf_op jit(solution)/shard_map/ppermute | solution.py:16
  (115 shorter events, 51.8 us)
Async XLA Ops:
  5.5 10.2 %collective-permute-start.1 = (f32[3,2,80,128]{3,2,1,0:T(8,128)S(1)}, f32[3,2,80,128]{3,2,1,0:T(8,128)S(1)}, u32[]{:S(2)}, u32[]{:S(2)}) collective-permute-start(f32[3,2,80,128]{3,2,1,0:T(8,128)S(1)} %get-tuple-element.26), channel_id=1, source_target_pairs={{0,1},{1,2},{2,3},{4,5},{5,6},{6,7},{8,9},{9,10},{10,11},{12,13},{... | collective-permute-start | bytes 737288 | tf_op jit(solution)/shard_map/ppermute | solution.py:27
  6.8 9.8 %collective-permute-start.2 = (f32[3,2,80,128]{3,2,1,0:T(8,128)S(1)}, f32[3,2,80,128]{3,2,1,0:T(8,128)S(1)}, u32[]{:S(2)}, u32[]{:S(2)}) collective-permute-start(f32[3,2,80,128]{3,2,1,0:T(8,128)S(1)} %get-tuple-element.27), channel_id=1, source_target_pairs={{1,0},{2,1},{3,2},{5,4},{6,5},{7,6},{9,8},{10,9},{11,10},{13,12},{... | collective-permute-start | bytes 737288 | tf_op jit(solution)/shard_map/ppermute | solution.py:28
  11.4 18.3 %collective-permute-start.3 = (f32[8,80,128]{2,1,0:T(8,128)S(1)}, f32[8,80,128]{2,1,0:T(8,128)S(1)}, u32[]{:S(2)}, u32[]{:S(2)}) collective-permute-start(f32[8,80,128]{2,1,0:T(8,128)S(1)} %get-tuple-element.29), channel_id=1, source_target_pairs={{0,8},{4,12},{8,16},{12,20},{16,24},{20,28},{24,32},{28,36},{32,40... | collective-permute-start | bytes 983048 | tf_op jit(solution)/shard_map/ppermute | solution.py:16
  31.1 13.8 %collective-permute-start.4 = (f32[8,80,128]{2,1,0:T(8,128)S(1)}, f32[8,80,128]{2,1,0:T(8,128)S(1)}, u32[]{:S(2)}, u32[]{:S(2)}) collective-permute-start(f32[8,80,128]{2,1,0:T(8,128)S(1)} %fusion.89), channel_id=1, source_target_pairs={{0,8},{4,12},{8,16},{12,20},{16,24},{20,28},{24,32},{28,36},{32,40... | collective-permute-start | bytes 983048 | tf_op jit(solution)/shard_map/ppermute | solution.py:16
  47.3 8.1 %collective-permute-start.5 = (f32[2,6,40,128]{3,2,1,0:T(8,128)S(1)}, f32[2,6,40,128]{3,2,1,0:T(8,128)S(1)}, u32[]{:S(2)}, u32[]{:S(2)}) collective-permute-start(f32[2,6,40,128]{3,2,1,0:T(8,128)S(1)} %fusion), channel_id=1, source_target_pairs={{0,8},{4,12},{8,0},{12,4},{16,24},{20,28},{24,16},{28,20},{32,40},... | collective-permute-start | bytes 737288 | tf_op jit(solution)/shard_map/ppermute | solution.py:21
  55.5 8.7 %collective-permute-start.6 = (f32[15,40,128]{2,1,0:T(8,128)S(1)}, f32[15,40,128]{2,1,0:T(8,128)S(1)}, u32[]{:S(2)}, u32[]{:S(2)}) collective-permute-start(f32[15,40,128]{2,1,0:T(8,128)S(1)} %pad_maximum_fusion.11), channel_id=1, source_target_pairs={{0,1},{1,2},{2,3},{4,5},{5,6},{6,7},{8,9},{9,10},{10,11},{12,13},{... | collective-permute-start | bytes 921608 | tf_op jit(solution)/shard_map/ppermute | solution.py:27
  56.8 30.6 %collective-permute-start.8 = (f32[8,80,128]{2,1,0:T(8,128)S(1)}, f32[8,80,128]{2,1,0:T(8,128)S(1)}, u32[]{:S(2)}, u32[]{:S(2)}) collective-permute-start(f32[8,80,128]{2,1,0:T(8,128)S(1)} %get-tuple-element.13), channel_id=1, source_target_pairs={{0,8},{4,12},{8,16},{12,20},{16,24},{20,28},{24,32},{28,36},{32,40... | collective-permute-start | bytes 983048 | tf_op jit(solution)/shard_map/ppermute | solution.py:16
  58.8 8.9 %collective-permute-start.7 = (f32[15,40,128]{2,1,0:T(8,128)S(1)}, f32[15,40,128]{2,1,0:T(8,128)S(1)}, u32[]{:S(2)}, u32[]{:S(2)}) collective-permute-start(f32[15,40,128]{2,1,0:T(8,128)S(1)} %pad_maximum_fusion.12), channel_id=1, source_target_pairs={{1,0},{2,1},{3,2},{5,4},{6,5},{7,6},{9,8},{10,9},{11,10},{13,12},{... | collective-permute-start | bytes 921608 | tf_op jit(solution)/shard_map/ppermute | solution.py:28
  68.9 13.3 %collective-permute-start.9 = (f32[4,40,128]{2,1,0:T(8,128)S(1)}, f32[4,40,128]{2,1,0:T(8,128)S(1)}, u32[]{:S(2)}, u32[]{:S(2)}) collective-permute-start(f32[4,40,128]{2,1,0:T(8,128)S(1)} %get-tuple-element.78), channel_id=1, source_target_pairs={{0,16},{4,20},{8,24},{12,28},{16,32},{20,36},{24,40},{28,44},{32,4... | collective-permute-start | bytes 245768 | tf_op jit(solution)/shard_map/ppermute | solution.py:16
  70.8 13.4 %collective-permute-start.10 = (f32[4,40,128]{2,1,0:T(8,128)S(1)}, f32[4,40,128]{2,1,0:T(8,128)S(1)}, u32[]{:S(2)}, u32[]{:S(2)}) collective-permute-start(f32[4,40,128]{2,1,0:T(8,128)S(1)} %get-tuple-element.48), channel_id=1, source_target_pairs={{0,32},{4,36},{8,40},{12,44},{16,48},{20,52},{24,56},{28,60},{32,6... | collective-permute-start | bytes 245768 | tf_op jit(solution)/shard_map/ppermute | solution.py:16
  75.0 11.4 %collective-permute-start.11 = (f32[4,40,128]{2,1,0:T(8,128)S(1)}, f32[4,40,128]{2,1,0:T(8,128)S(1)}, u32[]{:S(2)}, u32[]{:S(2)}) collective-permute-start(f32[4,40,128]{2,1,0:T(8,128)S(1)} %get-tuple-element.49), channel_id=1, source_target_pairs={{0,48},{4,52},{8,56},{12,60},{16,64},{20,68},{24,72},{28,76},{32,8... | collective-permute-start | bytes 245768 | tf_op jit(solution)/shard_map/ppermute | solution.py:16
  79.5 7.5 %collective-permute-start.12 = (f32[4,40,128]{2,1,0:T(8,128)S(1)}, f32[4,40,128]{2,1,0:T(8,128)S(1)}, u32[]{:S(2)}, u32[]{:S(2)}) collective-permute-start(f32[4,40,128]{2,1,0:T(8,128)S(1)} %get-tuple-element.53), channel_id=1, source_target_pairs={{0,64},{4,68},{8,72},{12,76},{16,80},{20,84},{24,88},{28,92},{32,9... | collective-permute-start | bytes 245768 | tf_op jit(solution)/shard_map/ppermute | solution.py:16
  87.8 14.2 %collective-permute-start.13 = (f32[8,72,128]{2,1,0:T(8,128)S(1)}, f32[8,72,128]{2,1,0:T(8,128)S(1)}, u32[]{:S(2)}, u32[]{:S(2)}) collective-permute-start(f32[8,72,128]{2,1,0:T(8,128)S(1)} %slice_select_fusion.5), channel_id=1, source_target_pairs={{0,8},{4,12},{8,16},{12,20},{16,24},{20,28},{24,32},{28,36},{32,40... | collective-permute-start | bytes 884744 | tf_op jit(solution)/shard_map/ppermute | solution.py:16
  91.8 6.0 %collective-permute-start.14 = (f32[1,72,128]{2,1,0:T(8,128)S(1)}, f32[1,72,128]{2,1,0:T(8,128)S(1)}, u32[]{:S(2)}, u32[]{:S(2)}) collective-permute-start(f32[1,72,128]{2,1,0:T(8,128)S(1)} %get-tuple-element.64), channel_id=1, source_target_pairs={{1,0},{2,1},{3,2},{5,4},{6,5},{7,6},{9,8},{10,9},{11,10},{13,12},{... | collective-permute-start | bytes 110600 | tf_op jit(solution)/shard_map/ppermute | solution.py:28
  96.1 5.9 %collective-permute-start.15 = (f32[1,72,128]{2,1,0:T(8,128)S(1)}, f32[1,72,128]{2,1,0:T(8,128)S(1)}, u32[]{:S(2)}, u32[]{:S(2)}) collective-permute-start(f32[1,72,128]{2,1,0:T(8,128)S(1)} %get-tuple-element.65), channel_id=1, source_target_pairs={{0,1},{1,2},{2,3},{4,5},{5,6},{6,7},{8,9},{9,10},{10,11},{12,13},{... | collective-permute-start | bytes 110600 | tf_op jit(solution)/shard_map/ppermute | solution.py:27
  102.3 12.5 %collective-permute-start.16 = (f32[8,72,128]{2,1,0:T(8,128)S(1)}, f32[8,72,128]{2,1,0:T(8,128)S(1)}, u32[]{:S(2)}, u32[]{:S(2)}) collective-permute-start(f32[8,72,128]{2,1,0:T(8,128)S(1)} %fusion.116), channel_id=1, source_target_pairs={{0,8},{4,12},{8,16},{12,20},{16,24},{20,28},{24,32},{28,36},{32,40... | collective-permute-start | bytes 884744 | tf_op jit(solution)/shard_map/ppermute | solution.py:16
  108.9 5.9 %collective-permute-start.18 = (f32[1,72,128]{2,1,0:T(8,128)S(1)}, f32[1,72,128]{2,1,0:T(8,128)S(1)}, u32[]{:S(2)}, u32[]{:S(2)}) collective-permute-start(f32[1,72,128]{2,1,0:T(8,128)S(1)} %get-tuple-element.63), channel_id=1, source_target_pairs={{0,1},{1,2},{2,3},{4,5},{5,6},{6,7},{8,9},{9,10},{10,11},{12,13},{... | collective-permute-start | bytes 110600 | tf_op jit(solution)/shard_map/ppermute | solution.py:27
  118.9 14.0 %collective-permute-start.20 = (f32[8,128,128]{2,1,0:T(8,128)S(1)}, f32[8,128,128]{2,1,0:T(8,128)S(1)}, u32[]{:S(2)}, u32[]{:S(2)}) collective-permute-start(f32[8,128,128]{2,1,0:T(8,128)S(1)} %pad_maximum_fusion.2), channel_id=1, source_target_pairs={{0,4},{4,8},{8,12},{12,16},{16,20},{20,24},{24,28},{28,32},{32,36}... | collective-permute-start | bytes 1572872 | tf_op jit(solution)/shard_map/ppermute | solution.py:16
  121.1 4.4 %collective-permute-start.21 = (f32[1,128,128]{2,1,0:T(8,128)S(1)}, f32[1,128,128]{2,1,0:T(8,128)S(1)}, u32[]{:S(2)}, u32[]{:S(2)}) collective-permute-start(f32[1,128,128]{2,1,0:T(8,128)S(1)} %get-tuple-element.46), channel_id=1, source_target_pairs={{1,0},{2,1},{3,2},{5,4},{6,5},{7,6},{9,8},{10,9},{11,10},{13,12},{... | collective-permute-start | bytes 196616 | tf_op jit(solution)/shard_map/ppermute | solution.py:28
  123.6 6.6 %collective-permute-start.22 = (f32[1,128,128]{2,1,0:T(8,128)S(1)}, f32[1,128,128]{2,1,0:T(8,128)S(1)}, u32[]{:S(2)}, u32[]{:S(2)}) collective-permute-start(f32[1,128,128]{2,1,0:T(8,128)S(1)} %get-tuple-element.47), channel_id=1, source_target_pairs={{0,1},{1,2},{2,3},{4,5},{5,6},{6,7},{8,9},{9,10},{10,11},{12,13},{... | collective-permute-start | bytes 196616 | tf_op jit(solution)/shard_map/ppermute | solution.py:27
  133.3 13.8 %collective-permute-start.23 = (f32[8,128,128]{2,1,0:T(8,128)S(1)}, f32[8,128,128]{2,1,0:T(8,128)S(1)}, u32[]{:S(2)}, u32[]{:S(2)}) collective-permute-start(f32[8,128,128]{2,1,0:T(8,128)S(1)} %fusion.18), channel_id=1, source_target_pairs={{0,4},{4,8},{8,12},{12,16},{16,20},{20,24},{24,28},{28,32},{32,36}... | collective-permute-start | bytes 1572872 | tf_op jit(solution)/shard_map/ppermute | solution.py:16
  137.8 6.2 %collective-permute-start.25 = (f32[1,128,128]{2,1,0:T(8,128)S(1)}, f32[1,128,128]{2,1,0:T(8,128)S(1)}, u32[]{:S(2)}, u32[]{:S(2)}) collective-permute-start(f32[1,128,128]{2,1,0:T(8,128)S(1)} %get-tuple-element.45), channel_id=1, source_target_pairs={{0,1},{1,2},{2,3},{4,5},{5,6},{6,7},{8,9},{9,10},{10,11},{12,13},{... | collective-permute-start | bytes 196616 | tf_op jit(solution)/shard_map/ppermute | solution.py:27
  147.7 13.8 %collective-permute-start.26 = (f32[8,128,128]{2,1,0:T(8,128)S(1)}, f32[8,128,128]{2,1,0:T(8,128)S(1)}, u32[]{:S(2)}, u32[]{:S(2)}) collective-permute-start(f32[8,128,128]{2,1,0:T(8,128)S(1)} %fusion.26), channel_id=1, source_target_pairs={{0,4},{4,8},{8,12},{12,16},{16,20},{20,24},{24,28},{28,32},{32,36}... | collective-permute-start | bytes 1572872 | tf_op jit(solution)/shard_map/ppermute | solution.py:16
  152.1 6.2 %collective-permute-start.28 = (f32[1,128,128]{2,1,0:T(8,128)S(1)}, f32[1,128,128]{2,1,0:T(8,128)S(1)}, u32[]{:S(2)}, u32[]{:S(2)}) collective-permute-start(f32[1,128,128]{2,1,0:T(8,128)S(1)} %get-tuple-element.43), channel_id=1, source_target_pairs={{0,1},{1,2},{2,3},{4,5},{5,6},{6,7},{8,9},{9,10},{10,11},{12,13},{... | collective-permute-start | bytes 196616 | tf_op jit(solution)/shard_map/ppermute | solution.py:27
  (8 other events, 53.8 us)

commit v3 on v2

--- a/solution.py
+++ b/solution.py
@@ -27,6 +27,15 @@
     below = lax.ppermute(upward, "space", up)
     above = lax.ppermute(downward, "space", [(j, i) for i, j in up])
     return below, above
+
+
+def slanted(upward, downward):
+    times, peers = lax.axis_size("tm"), lax.axis_size("space")
+    axes = ("tm", "space")
+    steps = [(t * peers, (t + 2) * peers) for t in range(times - 2)]
+    up = [(a + i, b + i + 1) for a, b in steps for i in range(peers - 1)]
+    down = [(a + i + 1, b + i) for a, b in steps for i in range(peers - 1)]
+    return lax.ppermute(upward, axes, up), lax.ppermute(downward, axes, down)
 
 
 def framed(value, width, dim=0):
@@ -97,9 +106,7 @@
     mine = window(source[0], low)
     got = flipped(window(source[0], ~low), 1)
     even, odd = jnp.where(low, mine, got), jnp.where(low, got, mine)
-    prior_odd = shifted(odd, 2)
     bundle = framed(jnp.stack([even, odd, window(conductivity, low)]), 2, 1)
-    bundle, prior_odd = lax.optimization_barrier((bundle, prior_odd))
     g, cond = bundle[:2], bundle[2]
     d0 = OMEGA / (1.0 + 6.0 * cond)
     d1 = OMEGA / (1.0 + 12.0 * cond)
@@ -177,22 +184,30 @@
         prior = shifted(middle, 2)
         middle = middle + e1 * (b1 + prior - applied(framed(middle, 1), cc))
 
-    def half(v):
-        return jnp.where(low, v[..., :HALF, :], v[..., v.shape[-2] - HALF :, :])
-
-    e0 = half(inner(d0, 2))
-    pre = [half(inner(rest[0])) + e0 * (e0 * half(prior_odd)), half(inner(odd2))]
-    top = half(middle)
-    keep = jnp.where(low, pre[0], pre[1]) + top
-    other = flipped(jnp.where(low, pre[1], pre[0]) + top, 1)
+    g, d0, cond = narrow(g), narrow(d0), narrow(cond)
+    e0 = inner(d0, 2)
+    prior_odd = shifted(inner(g[1], 2), 2)
+    pre = jnp.stack([narrow(inner(rest[0])) + e0 * (e0 * prior_odd), narrow(inner(odd2))])
+    state = pre + middle
+    sent = shifted(jnp.stack([state[1], e0 * (inner(g[1], 2) + state[0])]), 2)
+    state = framed(state, 2, 1)
+    lower, upper = slanted(state[1, -3:-2], state[1, 2:3])
+    earlier = jnp.concatenate([lower, sent[0], upper])
+
+    def swept(v, width):
+        return inner(v) - inner(d0, width) * applied(v, inner(cond, width))
+
+    before = jnp.stack([earlier, inner(state[0])])
+    state = swept(state, 1) + inner(d0) * (inner(g) + before)
+    earlier = swept(earlier, 2) + sent[1]
+    before = jnp.stack([earlier, inner(state[0])])
+    state = swept(state, 2) + e0 * (inner(g, 2) + before)
+
+    half = jnp.where(low, state[:, :, :HALF], state[:, :, NARROW - HALF :])
+    keep = jnp.where(low, half[0], half[1])
+    other = flipped(jnp.where(low, half[1], half[0]), 1)
     state = jnp.concatenate([jnp.where(low, keep, other), jnp.where(low, other, keep)], axis=1)
-    b0 = source[0]
-    d0 = OMEGA / (1.0 + 6.0 * conductivity)
-    for _ in range(2):
-        prior = shifted(state, 1)
-        state = state + d0 * (b0 + prior - applied(framed(state, 1), conductivity))
-    prior = shifted(state, 1)
-    last = b0 + prior - applied(framed(state, 1), conductivity)
+    last = source[0] + shifted(state, 1) - applied(framed(state, 1), conductivity)
     return state[None], last[None]
 
 

time: 164 us -> 156 us (0.951)
  the two profiles are of different devices: /device:TPU:38 before, /device:TPU:34 now
where the time goes in v3:
time: 156 us; the launch traced here: 155 us
  starting transfers between devices  84.4 us (54%)
  waiting for transfers between devices  54.9 us (35%)
  other arithmetic  11.5 us (7%)
  local copies, waits for them, and re-layouts  1.76 us (1%)
  between operations  1.62 us (1%)
    ppermute x11, starting transfers between devices, shifted(): lax.ppermute(value, 'tm', [(i, i + by) for i in range(peers) if 0 <= i +...  36.8 us
    ppermute x6, starting transfers between devices, exchanged(): below = lax.ppermute(upward, 'space', up)  21.3 us
    ppermute x11, waiting for transfers between devices, shifted(): lax.ppermute(value, 'tm', [(i, i + by) for i in range(peers) if 0 <= i +...  19.3 us
    ppermute x6, starting transfers between devices, exchanged(): above = lax.ppermute(downward, 'space', [(j, i) for i, j in up])  13.8 us
    ppermute x6, waiting for transfers between devices, exchanged(): below = lax.ppermute(upward, 'space', up)  10.8 us
    ppermute x6, waiting for transfers between devices, exchanged(): above = lax.ppermute(downward, 'space', [(j, i) for i, j in up])  8.74 us
    ppermute x3, waiting for transfers between devices, flipped(): return lax.ppermute(value, 'tm', [(i, i ^ mask) for i in range(peers)])  8.07 us
    ppermute x2, waiting for transfers between devices, slanted(): return (lax.ppermute(upward, axes, up), lax.ppermute(downward, axes, down))  7.93 us
  transfers between devices with their start and end apart: 28, of which 17 were waited for; matrix products, arithmetic and copies ran while one was open for 3% of the time, Pallas kernels for 0%

profile of v3, /device:TPU:34, one launch (start us, length us, event | category | flops | bytes accessed | tf_op | source)
XLA Modules:
  0.0 155.1 jit_solution(4399918637712357925)
XLA Ops:
  5.5 3.4 %collective-permute-start.1 = (f32[3,2,80,128]{3,2,1,0:T(8,128)S(1)}, f32[3,2,80,128]{3,2,1,0:T(8,128)S(1)}, u32[]{:S(2)}, u32[]{:S(2)}) collective-permute-start(f32[3,2,80,128]{3,2,1,0:T(8,128)S(1)} %get-tuple-element.19), channel_id=1, source_target_pairs={{0,1},{1,2},{2,3},{4,5},{5,6},{6,7},{8,9},{9,10},{10,11},{12,13},{... | collective-permute-start | bytes 737288 | tf_op jit(solution)/shard_map/ppermute | solution.py:27
  11.6 3.8 %collective-permute-done.1 = f32[3,2,80,128]{3,2,1,0:T(8,128)S(1)} collective-permute-done((f32[3,2,80,128]{3,2,1,0:T(8,128)S(1)}, f32[3,2,80,128]{3,2,1,0:T(8,128)S(1)}, u32[]{:S(2)}, u32[]{:S(2)}) %collective-permute-start.1) | collective-permute-done | bytes 245792 | tf_op jit(solution)/shard_map/ppermute | solution.py:27
  15.3 3.1 %collective-permute-done.2 = f32[3,2,80,128]{3,2,1,0:T(8,128)S(1)} collective-permute-done((f32[3,2,80,128]{3,2,1,0:T(8,128)S(1)}, f32[3,2,80,128]{3,2,1,0:T(8,128)S(1)}, u32[]{:S(2)}, u32[]{:S(2)}) %collective-permute-start.2) | collective-permute-done | bytes 245792 | tf_op jit(solution)/shard_map/ppermute | solution.py:28
  20.2 4.3 %collective-permute-start.4 = (f32[8,80,128]{2,1,0:T(8,128)S(1)}, f32[8,80,128]{2,1,0:T(8,128)S(1)}, u32[]{:S(2)}, u32[]{:S(2)}) collective-permute-start(f32[8,80,128]{2,1,0:T(8,128)S(1)} %fusion.91), channel_id=1, source_target_pairs={{0,8},{4,12},{8,16},{12,20},{16,24},{20,28},{24,32},{28,36},{32,40... | collective-permute-start | bytes 983048 | tf_op jit(solution)/shard_map/ppermute | solution.py:16
  24.6 13.2 %collective-permute-done.4 = f32[8,80,128]{2,1,0:T(8,128)S(1)} collective-permute-done((f32[8,80,128]{2,1,0:T(8,128)S(1)}, f32[8,80,128]{2,1,0:T(8,128)S(1)}, u32[]{:S(2)}, u32[]{:S(2)}) %collective-permute-start.4) | collective-permute-done | bytes 327712 | tf_op jit(solution)/shard_map/ppermute | solution.py:16
  42.2 6.1 %collective-permute-done.5 = f32[2,6,40,128]{3,2,1,0:T(8,128)S(1)} collective-permute-done((f32[2,6,40,128]{3,2,1,0:T(8,128)S(1)}, f32[2,6,40,128]{3,2,1,0:T(8,128)S(1)}, u32[]{:S(2)}, u32[]{:S(2)}) %collective-permute-start.5) | collective-permute-done | bytes 245792 | tf_op jit(solution)/shard_map/ppermute | solution.py:21
  48.5 3.1 %collective-permute-start.6 = (f32[15,40,128]{2,1,0:T(8,128)S(1)}, f32[15,40,128]{2,1,0:T(8,128)S(1)}, u32[]{:S(2)}, u32[]{:S(2)}) collective-permute-start(f32[15,40,128]{2,1,0:T(8,128)S(1)} %pad_maximum_fusion.11), channel_id=1, source_target_pairs={{0,1},{1,2},{2,3},{4,5},{5,6},{6,7},{8,9},{9,10},{10,11},{12,13},{... | collective-permute-start | bytes 921608 | tf_op jit(solution)/shard_map/ppermute | solution.py:27
  53.8 2.8 %collective-permute-start.7 = (f32[15,40,128]{2,1,0:T(8,128)S(1)}, f32[15,40,128]{2,1,0:T(8,128)S(1)}, u32[]{:S(2)}, u32[]{:S(2)}) collective-permute-start(f32[15,40,128]{2,1,0:T(8,128)S(1)} %pad_maximum_fusion.12), channel_id=1, source_target_pairs={{1,0},{2,1},{3,2},{5,4},{6,5},{7,6},{9,8},{10,9},{11,10},{13,12},{... | collective-permute-start | bytes 921608 | tf_op jit(solution)/shard_map/ppermute | solution.py:28
  57.3 5.3 %collective-permute-done.7 = f32[15,40,128]{2,1,0:T(8,128)S(1)} collective-permute-done((f32[15,40,128]{2,1,0:T(8,128)S(1)}, f32[15,40,128]{2,1,0:T(8,128)S(1)}, u32[]{:S(2)}, u32[]{:S(2)}) %collective-permute-start.7) | collective-permute-done | bytes 307232 | tf_op jit(solution)/shard_map/ppermute | solution.py:28
  65.9 7.1 %collective-permute-start.10 = (f32[4,40,128]{2,1,0:T(8,128)S(1)}, f32[4,40,128]{2,1,0:T(8,128)S(1)}, u32[]{:S(2)}, u32[]{:S(2)}) collective-permute-start(f32[4,40,128]{2,1,0:T(8,128)S(1)} %get-tuple-element.48), channel_id=1, source_target_pairs={{0,32},{4,36},{8,40},{12,44},{16,48},{20,52},{24,56},{28,60},{32,6... | collective-permute-start | bytes 245768 | tf_op jit(solution)/shard_map/ppermute | solution.py:16
  73.0 3.8 %collective-permute-start.11 = (f32[4,40,128]{2,1,0:T(8,128)S(1)}, f32[4,40,128]{2,1,0:T(8,128)S(1)}, u32[]{:S(2)}, u32[]{:S(2)}) collective-permute-start(f32[4,40,128]{2,1,0:T(8,128)S(1)} %get-tuple-element.49), channel_id=1, source_target_pairs={{0,48},{4,52},{8,56},{12,60},{16,64},{20,68},{24,72},{28,76},{32,8... | collective-permute-start | bytes 245768 | tf_op jit(solution)/shard_map/ppermute | solution.py:16
  79.5 3.4 %collective-permute-start.3 = (f32[8,72,128]{2,1,0:T(8,128)S(1)}, f32[8,72,128]{2,1,0:T(8,128)S(1)}, u32[]{:S(2)}, u32[]{:S(2)}) collective-permute-start(f32[8,72,128]{2,1,0:T(8,128)S(1)} %slice_bitcast_fusion.9), channel_id=1, source_target_pairs={{0,8},{4,12},{8,16},{12,20},{16,24},{20,28},{24,32},{28,36},{32,40... | collective-permute-start | bytes 884744 | tf_op jit(solution)/shard_map/ppermute | solution.py:16
  85.1 3.4 %collective-permute-start.13 = (f32[8,72,128]{2,1,0:T(8,128)S(1)}, f32[8,72,128]{2,1,0:T(8,128)S(1)}, u32[]{:S(2)}, u32[]{:S(2)}) collective-permute-start(f32[8,72,128]{2,1,0:T(8,128)S(1)} %slice_select_fusion.10), channel_id=1, source_target_pairs={{0,8},{4,12},{8,16},{12,20},{16,24},{20,28},{24,32},{28,36},{32,40... | collective-permute-start | bytes 884744 | tf_op jit(solution)/shard_map/ppermute | solution.py:16
  88.5 2.8 %collective-permute-start.14 = (f32[1,72,128]{2,1,0:T(8,128)S(1)}, f32[1,72,128]{2,1,0:T(8,128)S(1)}, u32[]{:S(2)}, u32[]{:S(2)}) collective-permute-start(f32[1,72,128]{2,1,0:T(8,128)S(1)} %get-tuple-element.64), channel_id=1, source_target_pairs={{1,0},{2,1},{3,2},{5,4},{6,5},{7,6},{9,8},{10,9},{11,10},{13,12},{... | collective-permute-start | bytes 110600 | tf_op jit(solution)/shard_map/ppermute | solution.py:28
  91.3 3.1 %collective-permute-start.15 = (f32[1,72,128]{2,1,0:T(8,128)S(1)}, f32[1,72,128]{2,1,0:T(8,128)S(1)}, u32[]{:S(2)}, u32[]{:S(2)}) collective-permute-start(f32[1,72,128]{2,1,0:T(8,128)S(1)} %get-tuple-element.65), channel_id=1, source_target_pairs={{0,1},{1,2},{2,3},{4,5},{5,6},{6,7},{8,9},{9,10},{10,11},{12,13},{... | collective-permute-start | bytes 110600 | tf_op jit(solution)/shard_map/ppermute | solution.py:27
  97.4 3.2 %collective-permute-start.16 = (f32[8,72,128]{2,1,0:T(8,128)S(1)}, f32[8,72,128]{2,1,0:T(8,128)S(1)}, u32[]{:S(2)}, u32[]{:S(2)}) collective-permute-start(f32[8,72,128]{2,1,0:T(8,128)S(1)} %fusion.118), channel_id=1, source_target_pairs={{0,8},{4,12},{8,16},{12,20},{16,24},{20,28},{24,32},{28,36},{32,40... | collective-permute-start | bytes 884744 | tf_op jit(solution)/shard_map/ppermute | solution.py:16
  102.6 3.9 %collective-permute-start.18 = (f32[1,72,128]{2,1,0:T(8,128)S(1)}, f32[1,72,128]{2,1,0:T(8,128)S(1)}, u32[]{:S(2)}, u32[]{:S(2)}) collective-permute-start(f32[1,72,128]{2,1,0:T(8,128)S(1)} %get-tuple-element.63), channel_id=1, source_target_pairs={{0,1},{1,2},{2,3},{4,5},{5,6},{6,7},{8,9},{9,10},{10,11},{12,13},{... | collective-permute-start | bytes 110600 | tf_op jit(solution)/shard_map/ppermute | solution.py:27
  109.9 2.8 %collective-permute-start.22 = (f32[2,8,72,128]{3,2,1,0:T(8,128)S(1)}, f32[2,8,72,128]{3,2,1,0:T(8,128)S(1)}, u32[]{:S(2)}, u32[]{:S(2)}) collective-permute-start(f32[2,8,72,128]{3,2,1,0:T(8,128)S(1)} %pad_maximum_fusion.6), channel_id=1, source_target_pairs={{0,8},{4,12},{8,16},{12,20},{16,24},{20,28},{24,32},{28,36},{32,40... | collective-permute-start | bytes 1769480 | tf_op jit(solution)/shard_map/ppermute | solution.py:16
  112.7 3.9 %collective-permute-start.19 = (f32[2,2,72,128]{3,2,1,0:T(8,128)S(1)}, f32[2,2,72,128]{3,2,1,0:T(8,128)S(1)}, u32[]{:S(2)}, u32[]{:S(2)}) collective-permute-start(f32[2,2,72,128]{3,2,1,0:T(8,128)S(1)} %get-tuple-element.29), channel_id=1, source_target_pairs={{0,1},{1,2},{2,3},{4,5},{5,6},{6,7},{8,9},{9,10},{10,11},{12,13},{... | collective-permute-start | bytes 442376 | tf_op jit(solution)/shard_map/ppermute | solution.py:27
  118.6 4.8 %collective-permute-start.21 = (f32[1,72,128]{2,1,0:T(8,128)S(1)}, f32[1,72,128]{2,1,0:T(8,128)S(1)}, u32[]{:S(2)}, u32[]{:S(2)}) collective-permute-start(f32[1,72,128]{2,1,0:T(8,128)S(1)} %get-tuple-element.27), channel_id=1, source_target_pairs={{0,9},{1,10},{2,11},{4,13},{5,14},{6,15},{8,17},{9,18},{10,19},{12... | collective-permute-start | bytes 110600 | tf_op jit(solution)/shard_map/ppermute | solution.py:38
  125.5 3.1 %collective-permute-done.21 = f32[1,72,128]{2,1,0:T(8,128)S(1)} collective-permute-done((f32[1,72,128]{2,1,0:T(8,128)S(1)}, f32[1,72,128]{2,1,0:T(8,128)S(1)}, u32[]{:S(2)}, u32[]{:S(2)}) %collective-permute-start.21) | collective-permute-done | bytes 36896 | tf_op jit(solution)/shard_map/ppermute | solution.py:38
  128.6 4.8 %collective-permute-done.23 = f32[1,72,128]{2,1,0:T(8,128)S(1)} collective-permute-done((f32[1,72,128]{2,1,0:T(8,128)S(1)}, f32[1,72,128]{2,1,0:T(8,128)S(1)}, u32[]{:S(2)}, u32[]{:S(2)}) %collective-permute-start.23) | collective-permute-done | bytes 36896 | tf_op jit(solution)/shard_map/ppermute | solution.py:38
  143.9 3.9 %collective-permute-start.27 = (f32[1,128,128]{2,1,0:T(8,128)S(1)}, f32[1,128,128]{2,1,0:T(8,128)S(1)}, u32[]{:S(2)}, u32[]{:S(2)}) collective-permute-start(f32[1,128,128]{2,1,0:T(8,128)S(1)} %get-tuple-element.44), channel_id=1, source_target_pairs={{0,1},{1,2},{2,3},{4,5},{5,6},{6,7},{8,9},{9,10},{10,11},{12,13},{... | collective-permute-start | bytes 196616 | tf_op jit(solution)/shard_map/ppermute | solution.py:27
  150.1 3.7 %collective-permute-done.25 = f32[8,128,128]{2,1,0:T(8,128)S(1)} collective-permute-done((f32[8,128,128]{2,1,0:T(8,128)S(1)}, f32[8,128,128]{2,1,0:T(8,128)S(1)}, u32[]{:S(2)}, u32[]{:S(2)}) %collective-permute-start.25) | collective-permute-done | bytes 524320 | tf_op jit(solution)/shard_map/ppermute | solution.py:16
  (140 shorter events, 50.9 us)
Async XLA Ops:
  5.5 9.9 %collective-permute-start.1 = (f32[3,2,80,128]{3,2,1,0:T(8,128)S(1)}, f32[3,2,80,128]{3,2,1,0:T(8,128)S(1)}, u32[]{:S(2)}, u32[]{:S(2)}) collective-permute-start(f32[3,2,80,128]{3,2,1,0:T(8,128)S(1)} %get-tuple-element.19), channel_id=1, source_target_pairs={{0,1},{1,2},{2,3},{4,5},{5,6},{6,7},{8,9},{9,10},{10,11},{12,13},{... | collective-permute-start | bytes 737288 | tf_op jit(solution)/shard_map/ppermute | solution.py:27
  8.9 9.6 %collective-permute-start.2 = (f32[3,2,80,128]{3,2,1,0:T(8,128)S(1)}, f32[3,2,80,128]{3,2,1,0:T(8,128)S(1)}, u32[]{:S(2)}, u32[]{:S(2)}) collective-permute-start(f32[3,2,80,128]{3,2,1,0:T(8,128)S(1)} %get-tuple-element.20), channel_id=1, source_target_pairs={{1,0},{2,1},{3,2},{5,4},{6,5},{7,6},{9,8},{10,9},{11,10},{13,12},{... | collective-permute-start | bytes 737288 | tf_op jit(solution)/shard_map/ppermute | solution.py:28
  20.2 17.7 %collective-permute-start.4 = (f32[8,80,128]{2,1,0:T(8,128)S(1)}, f32[8,80,128]{2,1,0:T(8,128)S(1)}, u32[]{:S(2)}, u32[]{:S(2)}) collective-permute-start(f32[8,80,128]{2,1,0:T(8,128)S(1)} %fusion.91), channel_id=1, source_target_pairs={{0,8},{4,12},{8,16},{12,20},{16,24},{20,28},{24,32},{28,36},{32,40... | collective-permute-start | bytes 983048 | tf_op jit(solution)/shard_map/ppermute | solution.py:16
  40.3 8.1 %collective-permute-start.5 = (f32[2,6,40,128]{3,2,1,0:T(8,128)S(1)}, f32[2,6,40,128]{3,2,1,0:T(8,128)S(1)}, u32[]{:S(2)}, u32[]{:S(2)}) collective-permute-start(f32[2,6,40,128]{3,2,1,0:T(8,128)S(1)} %fusion), channel_id=1, source_target_pairs={{0,8},{4,12},{8,0},{12,4},{16,24},{20,28},{24,16},{28,20},{32,40},... | collective-permute-start | bytes 737288 | tf_op jit(solution)/shard_map/ppermute | solution.py:21
  48.5 8.7 %collective-permute-start.6 = (f32[15,40,128]{2,1,0:T(8,128)S(1)}, f32[15,40,128]{2,1,0:T(8,128)S(1)}, u32[]{:S(2)}, u32[]{:S(2)}) collective-permute-start(f32[15,40,128]{2,1,0:T(8,128)S(1)} %pad_maximum_fusion.11), channel_id=1, source_target_pairs={{0,1},{1,2},{2,3},{4,5},{5,6},{6,7},{8,9},{9,10},{10,11},{12,13},{... | collective-permute-start | bytes 921608 | tf_op jit(solution)/shard_map/ppermute | solution.py:27
  51.6 33.1 %collective-permute-start.8 = (f32[8,80,128]{2,1,0:T(8,128)S(1)}, f32[8,80,128]{2,1,0:T(8,128)S(1)}, u32[]{:S(2)}, u32[]{:S(2)}) collective-permute-start(f32[8,80,128]{2,1,0:T(8,128)S(1)} %get-tuple-element.7), channel_id=1, source_target_pairs={{0,8},{4,12},{8,16},{12,20},{16,24},{20,28},{24,32},{28,36},{32,40... | collective-permute-start | bytes 983048 | tf_op jit(solution)/shard_map/ppermute | solution.py:16
  53.8 8.7 %collective-permute-start.7 = (f32[15,40,128]{2,1,0:T(8,128)S(1)}, f32[15,40,128]{2,1,0:T(8,128)S(1)}, u32[]{:S(2)}, u32[]{:S(2)}) collective-permute-start(f32[15,40,128]{2,1,0:T(8,128)S(1)} %pad_maximum_fusion.12), channel_id=1, source_target_pairs={{1,0},{2,1},{3,2},{5,4},{6,5},{7,6},{9,8},{10,9},{11,10},{13,12},{... | collective-permute-start | bytes 921608 | tf_op jit(solution)/shard_map/ppermute | solution.py:28
  63.8 15.7 %collective-permute-start.9 = (f32[4,40,128]{2,1,0:T(8,128)S(1)}, f32[4,40,128]{2,1,0:T(8,128)S(1)}, u32[]{:S(2)}, u32[]{:S(2)}) collective-permute-start(f32[4,40,128]{2,1,0:T(8,128)S(1)} %get-tuple-element.78), channel_id=1, source_target_pairs={{0,16},{4,20},{8,24},{12,28},{16,32},{20,36},{24,40},{28,44},{32,4... | collective-permute-start | bytes 245768 | tf_op jit(solution)/shard_map/ppermute | solution.py:16
  65.9 17.0 %collective-permute-start.10 = (f32[4,40,128]{2,1,0:T(8,128)S(1)}, f32[4,40,128]{2,1,0:T(8,128)S(1)}, u32[]{:S(2)}, u32[]{:S(2)}) collective-permute-start(f32[4,40,128]{2,1,0:T(8,128)S(1)} %get-tuple-element.48), channel_id=1, source_target_pairs={{0,32},{4,36},{8,40},{12,44},{16,48},{20,52},{24,56},{28,60},{32,6... | collective-permute-start | bytes 245768 | tf_op jit(solution)/shard_map/ppermute | solution.py:16
  73.0 9.9 %collective-permute-start.11 = (f32[4,40,128]{2,1,0:T(8,128)S(1)}, f32[4,40,128]{2,1,0:T(8,128)S(1)}, u32[]{:S(2)}, u32[]{:S(2)}) collective-permute-start(f32[4,40,128]{2,1,0:T(8,128)S(1)} %get-tuple-element.49), channel_id=1, source_target_pairs={{0,48},{4,52},{8,56},{12,60},{16,64},{20,68},{24,72},{28,76},{32,8... | collective-permute-start | bytes 245768 | tf_op jit(solution)/shard_map/ppermute | solution.py:16
  76.8 7.5 %collective-permute-start.12 = (f32[4,40,128]{2,1,0:T(8,128)S(1)}, f32[4,40,128]{2,1,0:T(8,128)S(1)}, u32[]{:S(2)}, u32[]{:S(2)}) collective-permute-start(f32[4,40,128]{2,1,0:T(8,128)S(1)} %get-tuple-element.53), channel_id=1, source_target_pairs={{0,64},{4,68},{8,72},{12,76},{16,80},{20,84},{24,88},{28,92},{32,9... | collective-permute-start | bytes 245768 | tf_op jit(solution)/shard_map/ppermute | solution.py:16
  79.5 27.0 %collective-permute-start.3 = (f32[8,72,128]{2,1,0:T(8,128)S(1)}, f32[8,72,128]{2,1,0:T(8,128)S(1)}, u32[]{:S(2)}, u32[]{:S(2)}) collective-permute-start(f32[8,72,128]{2,1,0:T(8,128)S(1)} %slice_bitcast_fusion.9), channel_id=1, source_target_pairs={{0,8},{4,12},{8,16},{12,20},{16,24},{20,28},{24,32},{28,36},{32,40... | collective-permute-start | bytes 884744 | tf_op jit(solution)/shard_map/ppermute | solution.py:16
  85.1 12.0 %collective-permute-start.13 = (f32[8,72,128]{2,1,0:T(8,128)S(1)}, f32[8,72,128]{2,1,0:T(8,128)S(1)}, u32[]{:S(2)}, u32[]{:S(2)}) collective-permute-start(f32[8,72,128]{2,1,0:T(8,128)S(1)} %slice_select_fusion.10), channel_id=1, source_target_pairs={{0,8},{4,12},{8,16},{12,20},{16,24},{20,28},{24,32},{28,36},{32,40... | collective-permute-start | bytes 884744 | tf_op jit(solution)/shard_map/ppermute | solution.py:16
  88.5 5.9 %collective-permute-start.14 = (f32[1,72,128]{2,1,0:T(8,128)S(1)}, f32[1,72,128]{2,1,0:T(8,128)S(1)}, u32[]{:S(2)}, u32[]{:S(2)}) collective-permute-start(f32[1,72,128]{2,1,0:T(8,128)S(1)} %get-tuple-element.64), channel_id=1, source_target_pairs={{1,0},{2,1},{3,2},{5,4},{6,5},{7,6},{9,8},{10,9},{11,10},{13,12},{... | collective-permute-start | bytes 110600 | tf_op jit(solution)/shard_map/ppermute | solution.py:28
  97.4 11.9 %collective-permute-start.16 = (f32[8,72,128]{2,1,0:T(8,128)S(1)}, f32[8,72,128]{2,1,0:T(8,128)S(1)}, u32[]{:S(2)}, u32[]{:S(2)}) collective-permute-start(f32[8,72,128]{2,1,0:T(8,128)S(1)} %fusion.118), channel_id=1, source_target_pairs={{0,8},{4,12},{8,16},{12,20},{16,24},{20,28},{24,32},{28,36},{32,40... | collective-permute-start | bytes 884744 | tf_op jit(solution)/shard_map/ppermute | solution.py:16
  100.7 5.9 %collective-permute-start.17 = (f32[1,72,128]{2,1,0:T(8,128)S(1)}, f32[1,72,128]{2,1,0:T(8,128)S(1)}, u32[]{:S(2)}, u32[]{:S(2)}) collective-permute-start(f32[1,72,128]{2,1,0:T(8,128)S(1)} %get-tuple-element.62), channel_id=1, source_target_pairs={{1,0},{2,1},{3,2},{5,4},{6,5},{7,6},{9,8},{10,9},{11,10},{13,12},{... | collective-permute-start | bytes 110600 | tf_op jit(solution)/shard_map/ppermute | solution.py:28
  109.9 15.6 %collective-permute-start.22 = (f32[2,8,72,128]{3,2,1,0:T(8,128)S(1)}, f32[2,8,72,128]{3,2,1,0:T(8,128)S(1)}, u32[]{:S(2)}, u32[]{:S(2)}) collective-permute-start(f32[2,8,72,128]{3,2,1,0:T(8,128)S(1)} %pad_maximum_fusion.6), channel_id=1, source_target_pairs={{0,8},{4,12},{8,16},{12,20},{16,24},{20,28},{24,32},{28,36},{32,40... | collective-permute-start | bytes 1769480 | tf_op jit(solution)/shard_map/ppermute | solution.py:16
  112.7 12.6 %collective-permute-start.19 = (f32[2,2,72,128]{3,2,1,0:T(8,128)S(1)}, f32[2,2,72,128]{3,2,1,0:T(8,128)S(1)}, u32[]{:S(2)}, u32[]{:S(2)}) collective-permute-start(f32[2,2,72,128]{3,2,1,0:T(8,128)S(1)} %get-tuple-element.29), channel_id=1, source_target_pairs={{0,1},{1,2},{2,3},{4,5},{5,6},{6,7},{8,9},{9,10},{10,11},{12,13},{... | collective-permute-start | bytes 442376 | tf_op jit(solution)/shard_map/ppermute | solution.py:27
  116.5 8.7 %collective-permute-start.20 = (f32[2,2,72,128]{3,2,1,0:T(8,128)S(1)}, f32[2,2,72,128]{3,2,1,0:T(8,128)S(1)}, u32[]{:S(2)}, u32[]{:S(2)}) collective-permute-start(f32[2,2,72,128]{3,2,1,0:T(8,128)S(1)} %get-tuple-element.30), channel_id=1, source_target_pairs={{1,0},{2,1},{3,2},{5,4},{6,5},{7,6},{9,8},{10,9},{11,10},{13,12},{... | collective-permute-start | bytes 442376 | tf_op jit(solution)/shard_map/ppermute | solution.py:28
  118.6 10.1 %collective-permute-start.21 = (f32[1,72,128]{2,1,0:T(8,128)S(1)}, f32[1,72,128]{2,1,0:T(8,128)S(1)}, u32[]{:S(2)}, u32[]{:S(2)}) collective-permute-start(f32[1,72,128]{2,1,0:T(8,128)S(1)} %get-tuple-element.27), channel_id=1, source_target_pairs={{0,9},{1,10},{2,11},{4,13},{5,14},{6,15},{8,17},{9,18},{10,19},{12... | collective-permute-start | bytes 110600 | tf_op jit(solution)/shard_map/ppermute | solution.py:38
  123.4 10.1 %collective-permute-start.23 = (f32[1,72,128]{2,1,0:T(8,128)S(1)}, f32[1,72,128]{2,1,0:T(8,128)S(1)}, u32[]{:S(2)}, u32[]{:S(2)}) collective-permute-start(f32[1,72,128]{2,1,0:T(8,128)S(1)} %get-tuple-element.28), channel_id=1, source_target_pairs={{1,8},{2,9},{3,10},{5,12},{6,13},{7,14},{9,16},{10,17},{11,18},{13... | collective-permute-start | bytes 110600 | tf_op jit(solution)/shard_map/ppermute | solution.py:38
  139.9 13.8 %collective-permute-start.25 = (f32[8,128,128]{2,1,0:T(8,128)S(1)}, f32[8,128,128]{2,1,0:T(8,128)S(1)}, u32[]{:S(2)}, u32[]{:S(2)}) collective-permute-start(f32[8,128,128]{2,1,0:T(8,128)S(1)} %pad_maximum_fusion.5), channel_id=1, source_target_pairs={{0,4},{4,8},{8,12},{12,16},{16,20},{20,24},{24,28},{28,32},{32,36}... | collective-permute-start | bytes 1572872 | tf_op jit(solution)/shard_map/ppermute | solution.py:16
  142.0 6.2 %collective-permute-start.26 = (f32[1,128,128]{2,1,0:T(8,128)S(1)}, f32[1,128,128]{2,1,0:T(8,128)S(1)}, u32[]{:S(2)}, u32[]{:S(2)}) collective-permute-start(f32[1,128,128]{2,1,0:T(8,128)S(1)} %get-tuple-element.43), channel_id=1, source_target_pairs={{1,0},{2,1},{3,2},{5,4},{6,5},{7,6},{9,8},{10,9},{11,10},{13,12},{... | collective-permute-start | bytes 196616 | tf_op jit(solution)/shard_map/ppermute | solution.py:28
  143.9 6.2 %collective-permute-start.27 = (f32[1,128,128]{2,1,0:T(8,128)S(1)}, f32[1,128,128]{2,1,0:T(8,128)S(1)}, u32[]{:S(2)}, u32[]{:S(2)}) collective-permute-start(f32[1,128,128]{2,1,0:T(8,128)S(1)} %get-tuple-element.44), channel_id=1, source_target_pairs={{0,1},{1,2},{2,3},{4,5},{5,6},{6,7},{8,9},{9,10},{10,11},{12,13},{... | collective-permute-start | bytes 196616 | tf_op jit(solution)/shard_map/ppermute | solution.py:27
  (12 other events, 220.0 us)

commit v4 on v3

v4 whole, which is shorter than its diff:
```python
import jax
import jax.numpy as jnp
from jax import lax
from jax.sharding import PartitionSpec as P

OMEGA = 0.8
FINE = (1.0, 1.0, 1.0)
COARSE = (0.25, 0.25, 1.0)
HALF = 64
ROWS = 80
NARROW = 72


def shifted(value, by):
    peers = lax.axis_size("tm")
    return lax.ppermute(value, "tm", [(i, i + by) for i in range(peers) if 0 <= i + by < peers])


def flipped(value, mask):
    peers = lax.axis_size("tm")
    return lax.ppermute(value, "tm", [(i, i ^ mask) for i in range(peers)])


def exchanged(upward, downward):
    peers = lax.axis_size("space")
    up = [(i, i + 1) for i in range(peers - 1)]
    below = lax.ppermute(upward, "space", up)
    above = lax.ppermute(downward, "space", [(j, i) for i, j in up])
    return below, above


def framed(value, width, dim=0):
    length = value.shape[dim]
    before, after = exchanged(
        lax.slice_in_dim(value, length - width, length, axis=dim),
        lax.slice_in_dim(value, 0, width, axis=dim),
    )
    return jnp.concatenate([before, value, after], axis=dim)


def stencil(v, weights=FINE):
    a, b, d = weights
    m = v[..., 1:-1, :, :]
    lead = [(0, 0)] * (v.ndim - 2)
    px = jnp.pad(m, lead + [(1, 1), (0, 0)])
    py = jnp.pad(m, lead + [(0, 0), (1, 1)])
    return (
        2.0 * (a + b + d) * m
        - a * (v[..., 2:, :, :] + v[..., :-2, :, :])
        - b * (px[..., 2:, :] + px[..., :-2, :])
        - d * (py[..., 2:] + py[..., :-2])
    )


def inner(v, n=1):
    return v[..., n:-n, :, :]


def applied(v, c, weights=FINE):
    return inner(v) + c * stencil(v, weights)


def pair_matrix(rows):
    i = lax.broadcasted_iota(jnp.int32, (rows // 2, rows), 0)
    j = lax.broadcasted_iota(jnp.int32, (rows // 2, rows), 1)
    return (j // 2 == i).astype(jnp.float32)


def coarsen(v):
    z = v[..., 0::2, :, :] + v[..., 1::2, :, :]
    rows = z.shape[-2]
    return 0.25 * jnp.einsum(
        "ij,...jy->...iy", pair_matrix(rows), z, precision=lax.Precision.HIGHEST
    )


def refine(v):
    rows = v.shape[-2] * 2
    wide = jnp.einsum(
        "ij,...iy->...jy", pair_matrix(rows), v, precision=lax.Precision.HIGHEST
    )
    return jnp.repeat(wide, 2, axis=-3)


def body(source, conductivity):
    me = lax.axis_index("tm")
    odd_chip = (me // 2) % 2 == 1
    low = me % 2 == 0
    planes, rows, _ = conductivity.shape

    def window(v, keep):
        return jnp.where(keep, v[:, :ROWS], v[:, rows - ROWS :])

    def narrow(v):
        return jnp.where(low, v[..., :NARROW, :], v[..., ROWS - NARROW :, :])

    mine = window(source[0], low)
    got = flipped(window(source[0], ~low), 1)
    even, odd = jnp.where(low, mine, got), jnp.where(low, got, mine)
    bundle = framed(jnp.stack([even, odd, window(conductivity, low)]), 3, 1)
    g, cond = bundle[:2], bundle[2]
    d0 = OMEGA / (1.0 + 6.0 * cond)
    d1 = OMEGA / (1.0 + 12.0 * cond)

    c12, c10, c8 = inner(cond, 1), inner(cond, 2), inner(cond, 3)
    u1 = d0 * g
    rest = inner(u1) + inner(d0) * (inner(g) - applied(u1, c12))
    hop = inner(d0) * inner(u1)
    odd2 = rest[1] + hop[0]
    w = inner(odd2) - c10 * stencil(hop[1])
    local = inner(g[0] + g[1], 2) + inner(rest[0]) - applied(rest[0] + odd2, c10)
    before_w = shifted(narrow(w), 2)

    def spill(v, n):
        return jnp.pad(v, ((0, 0), (n, n), (0, 0), (0, 0)))

    part = jnp.stack([inner(local), inner(w)])
    first = inner(d1, 3) * part
    swept1 = spill(first, 1) + inner(d1, 2) * (
        spill(part, 1) - applied(spill(first, 2), 2.0 * c10)
    )
    hop1 = inner(d1, 3) * first
    own = spill(part, 2) - applied(spill(swept1, 2), 2.0 * c12)
    nxt = spill(swept1, 1) - applied(spill(hop1, 3), 2.0 * c12)
    carry = spill(hop1, 2)
    share = coarsen(
        jnp.stack(
            [
                own[0] + jnp.where(odd_chip, 0.0, nxt[0] + own[1]),
                carry[0]
                + nxt[1]
                + jnp.where(odd_chip, nxt[0] + own[1], carry[1]),
                jnp.where(odd_chip, carry[1], 0.0),
            ]
        )
    )

    c2 = 4.0 * coarsen(c8)
    below, above = exchanged(
        jnp.concatenate([share[0, -5:], share[1, -5:], share[2, -5:], c2[-3:]]),
        jnp.concatenate([share[0, :5], share[1, :5], share[2, :5], c2[:3]]),
    )

    def joined(v, lower, upper):
        head, tail = v[1:2] + lower[4:5], v[-2:-1] + upper[0:1]
        before = jnp.concatenate([lower[1:3], lower[3:4] + v[0:1]])
        after = jnp.concatenate([upper[1:2] + v[-1:], upper[2:4]])
        return jnp.concatenate([before, head, v[2:-2], tail, after])

    right = [
        joined(share[i], below[5 * i : 5 * i + 5], above[5 * i : 5 * i + 5]) for i in range(3)
    ]
    c2 = jnp.concatenate([below[15:], c2, above[15:]])
    d2 = OMEGA / (1.0 + 3.0 * c2)
    base = [d2 * v for v in right]
    terms = list(base)
    for _ in range(3):
        c2, d2 = inner(c2), inner(d2)
        base = [inner(v) for v in base]
        kept = [inner(v) - d2 * applied(v, c2, COARSE) for v in terms]
        moved = [d2 * inner(v) for v in terms]
        count = len(terms)
        terms = [
            sum(
                ([kept[j]] if j < count else [])
                + ([moved[j - 1]] if j else [])
                + ([base[j]] if j < 3 else [])
            )
            for j in range(count + 1)
        ]
    coarse = terms[0]
    for j in range(1, 6):
        coarse = coarse + shifted(terms[j], 4 * j)
    coarse = coarse + flipped(coarse, 2)

    g, cond, d0, d1 = narrow(g), narrow(cond), narrow(d0), narrow(d1)
    g1 = narrow(local) + before_w
    m1 = inner(d1, 2) * g1
    prior = shifted(jnp.stack([inner(m1), inner(g[1], 3)]), 2)
    e1, b1, cc = inner(d1, 3), inner(g1), 2.0 * inner(cond, 3)
    rest1 = inner(m1) + e1 * (b1 - applied(m1, cc))
    middle = rest1 + e1 * prior[0] + narrow(refine(coarse))
    for _ in range(2):
        earlier = shifted(middle, 2)
        middle = middle + e1 * (b1 + earlier - applied(framed(middle, 1), cc))

    g, cond, d0 = inner(g), inner(cond), inner(d0)
    e0 = inner(d0, 2)
    pre = jnp.stack(
        [narrow(inner(rest[0], 2)) + e0 * (e0 * prior[1]), narrow(inner(odd2, 2))]
    )
    state = pre + middle
    sent = shifted(jnp.stack([state[1], e0 * (inner(g[1], 2) + state[0])]), 2)
    state = framed(state, 2, 1)
    ghost = jnp.pad(sent[0], ((1, 1), (0, 0), (0, 0)))

    def swept(v, width):
        return inner(v) - inner(d0, width) * applied(v, inner(cond, width))

    before = jnp.stack([ghost, inner(state[0])])
    state = swept(state, 1) + inner(d0) * (inner(g) + before)
    before = jnp.stack([swept(ghost, 2) + sent[1], inner(state[0])])
    state = swept(state, 2) + e0 * (inner(g, 2) + before)

    def half(v):
        return jnp.where(low, v[..., :HALF, :], v[..., NARROW - HALF :, :])

    both = half(state)
    faces = half(
        jnp.concatenate([sent[0][:1], sent[0][-1:], cond[1:2], cond[-2:-1]])
    )
    keep = jnp.concatenate([jnp.where(low, both[0], both[1]), faces])
    other = flipped(jnp.concatenate([jnp.where(low, both[1], both[0]), faces]), 1)
    full = jnp.concatenate([jnp.where(low, keep, other), jnp.where(low, other, keep)], axis=1)
    state, lead, beyond = full[:planes], full[planes : planes + 2], full[planes + 2 :]
    earlier = shifted(state, 1)
    below, above = exchanged(
        jnp.concatenate([state[-1:], lead[1:]]), jnp.concatenate([state[:1], lead[:1]])
    )
    edge = jnp.concatenate([conductivity[:1], conductivity[-1:]])
    de, db = OMEGA / (1.0 + 6.0 * edge), OMEGA / (1.0 + 6.0 * beyond)
    inside = de * edge * (de + db) * jnp.concatenate([below[1:], above[1:]])
    outside = db * beyond * (de + db) * lead
    outside = jnp.where(low, outside, 0.0)

    def mended(v, keep):
        fix = jnp.where(keep, inside, 0.0)
        return jnp.concatenate([v[:1] + fix[:1], v[1:-1], v[-1:] + fix[1:]])

    state, earlier = mended(state, low), mended(earlier, ~low)
    wide = jnp.concatenate([below[:1] + outside[:1], state, above[:1] + outside[1:]])
    last = source[0] + earlier - applied(wide, conductivity)
    return state[None], last[None]


def solution(mesh):
    return jax.shard_map(
        body,
        mesh=mesh,
        in_specs=(P("tm", "space", None, None), P("space", None, None)),
        out_specs=(P("tm", "space", None, None), P("tm", "space", None, None)),
        check_vma=False,
    )
```

time: 156 us -> 157 us (level)
  other arithmetic: 11.5 us -> 14.7 us
  waiting for transfers between devices: 54.9 us -> 52.3 us
    ppermute x2 -> x0, waiting for transfers between devices: 7.93 us -> none  [slanted(): return (lax.ppermute(upward, axes, up), lax.ppermute(downward, axes, down))]
    ppermute x2 -> x0, starting transfers between devices: 6.7 us -> none  [slanted(): return (lax.ppermute(upward, axes, up), lax.ppermute(downward, axes, down))]
    ppermute x11, starting transfers between devices: 36.8 us -> 41.7 us  [shifted(): lax.ppermute(value, 'tm', [(i, i + by) for i in range(peers) if 0 <= i +...]
    ppermute x6, starting transfers between devices: 13.8 us -> 18.2 us  [exchanged(): above = lax.ppermute(downward, 'space', [(j, i) for i, j in up])]
    ppermute x6, starting transfers between devices: 21.3 us -> 17.1 us  [exchanged(): below = lax.ppermute(upward, 'space', up)]
    ppermute x6, waiting for transfers between devices: 10.8 us -> 14 us  [exchanged(): below = lax.ppermute(upward, 'space', up)]
    sub x1 -> x2, other arithmetic: 0.28 us -> 2.78 us  [the longest x1 2.04 us: body(): own = spill(part, 2) - applied(spill(swept1, 2), 2.0 * c12)]
    ppermute x3, waiting for transfers between devices: 8.07 us -> 9.81 us  [flipped(): return lax.ppermute(value, 'tm', [(i, i ^ mask) for i in range(peers)])]
  transfers between devices with their start and end apart: 28 -> 26, of which waited for: 17 -> 18; matrix products, arithmetic and copies ran while one was open for 3% -> 3% of each run, Pallas kernels for 0% -> 0%
where the time goes in v4:
time: 157 us; the launch traced here: 156 us
  starting transfers between devices  84.1 us (54%)
  waiting for transfers between devices  52.3 us (33%)
  other arithmetic  14.7 us (9%)
  local copies, waits for them, and re-layouts  2.14 us (1%)
  between operations  1.78 us (1%)
    ppermute x11, starting transfers between devices, shifted(): lax.ppermute(value, 'tm', [(i, i + by) for i in range(peers) if 0 <= i +...  41.7 us
    ppermute x11, waiting for transfers between devices, shifted(): lax.ppermute(value, 'tm', [(i, i + by) for i in range(peers) if 0 <= i +...  18.9 us
    ppermute x6, starting transfers between devices, exchanged(): above = lax.ppermute(downward, 'space', [(j, i) for i, j in up])  18.2 us
    ppermute x6, starting transfers between devices, exchanged(): below = lax.ppermute(upward, 'space', up)  17.1 us
    ppermute x6, waiting for transfers between devices, exchanged(): below = lax.ppermute(upward, 'space', up)  14 us
    ppermute x3, waiting for transfers between devices, flipped(): return lax.ppermute(value, 'tm', [(i, i ^ mask) for i in range(peers)])  9.81 us
    ppermute x6, waiting for transfers between devices, exchanged(): above = lax.ppermute(downward, 'space', [(j, i) for i, j in up])  9.59 us
    ppermute x3, starting transfers between devices, flipped(): return lax.ppermute(value, 'tm', [(i, i ^ mask) for i in range(peers)])  7.05 us
  transfers between devices with their start and end apart: 26, of which 18 were waited for; matrix products, arithmetic and copies ran while one was open for 3% of the time, Pallas kernels for 0%

profile of v4, /device:TPU:34, one launch (start us, length us, event | category | flops | bytes accessed | tf_op | source)
XLA Modules:
  0.0 155.9 jit_solution(18245392295761771697)
XLA Ops:
  5.5 3.4 %collective-permute-start.1 = (f32[3,3,80,128]{3,2,1,0:T(8,128)S(1)}, f32[3,3,80,128]{3,2,1,0:T(8,128)S(1)}, u32[]{:S(2)}, u32[]{:S(2)}) collective-permute-start(f32[3,3,80,128]{3,2,1,0:T(8,128)S(1)} %get-tuple-element.26), channel_id=1, source_target_pairs={{0,1},{1,2},{2,3},{4,5},{5,6},{6,7},{8,9},{9,10},{10,11},{12,13},{... | collective-permute-start | bytes 1105928 | tf_op jit(solution)/shard_map/ppermute | solution.py:27
  11.6 6.4 %collective-permute-done.1 = f32[3,3,80,128]{3,2,1,0:T(8,128)S(1)} collective-permute-done((f32[3,3,80,128]{3,2,1,0:T(8,128)S(1)}, f32[3,3,80,128]{3,2,1,0:T(8,128)S(1)}, u32[]{:S(2)}, u32[]{:S(2)}) %collective-permute-start.1) | collective-permute-done | bytes 368672 | tf_op jit(solution)/shard_map/ppermute | solution.py:27
  18.1 3.1 %collective-permute-done.2 = f32[3,3,80,128]{3,2,1,0:T(8,128)S(1)} collective-permute-done((f32[3,3,80,128]{3,2,1,0:T(8,128)S(1)}, f32[3,3,80,128]{3,2,1,0:T(8,128)S(1)}, u32[]{:S(2)}, u32[]{:S(2)}) %collective-permute-start.2) | collective-permute-done | bytes 368672 | tf_op jit(solution)/shard_map/ppermute | solution.py:28
  28.0 3.1 %collective-permute-start.5 = (f32[18,40,128]{2,1,0:T(8,128)S(1)}, f32[18,40,128]{2,1,0:T(8,128)S(1)}, u32[]{:S(2)}, u32[]{:S(2)}) collective-permute-start(f32[18,40,128]{2,1,0:T(8,128)S(1)} %pad_maximum_fusion.14), channel_id=1, source_target_pairs={{0,1},{1,2},{2,3},{4,5},{5,6},{6,7},{8,9},{9,10},{10,11},{12,13},{... | collective-permute-start | bytes 1105928 | tf_op jit(solution)/shard_map/ppermute | solution.py:27
  31.1 2.8 %collective-permute-start.6 = (f32[18,40,128]{2,1,0:T(8,128)S(1)}, f32[18,40,128]{2,1,0:T(8,128)S(1)}, u32[]{:S(2)}, u32[]{:S(2)}) collective-permute-start(f32[18,40,128]{2,1,0:T(8,128)S(1)} %pad_maximum_fusion.15), channel_id=1, source_target_pairs={{1,0},{2,1},{3,2},{5,4},{6,5},{7,6},{9,8},{10,9},{11,10},{13,12},{... | collective-permute-start | bytes 1105928 | tf_op jit(solution)/shard_map/ppermute | solution.py:28
  33.9 4.3 %collective-permute-start.3 = (f32[10,72,128]{2,1,0:T(8,128)S(1)}, f32[10,72,128]{2,1,0:T(8,128)S(1)}, u32[]{:S(2)}, u32[]{:S(2)}) collective-permute-start(f32[10,72,128]{2,1,0:T(8,128)S(1)} %slice_select_fusion.5), channel_id=1, source_target_pairs={{0,8},{4,12},{8,16},{12,20},{16,24},{20,28},{24,32},{28,36},{32,40... | collective-permute-start | bytes 1105928 | tf_op jit(solution)/shard_map/ppermute | solution.py:16
  39.4 2.8 %collective-permute-done.6 = f32[18,40,128]{2,1,0:T(8,128)S(1)} collective-permute-done((f32[18,40,128]{2,1,0:T(8,128)S(1)}, f32[18,40,128]{2,1,0:T(8,128)S(1)}, u32[]{:S(2)}, u32[]{:S(2)}) %collective-permute-start.6) | collective-permute-done | bytes 368672 | tf_op jit(solution)/shard_map/ppermute | solution.py:28
  43.8 6.1 %collective-permute-start.7 = (f32[4,40,128]{2,1,0:T(8,128)S(1)}, f32[4,40,128]{2,1,0:T(8,128)S(1)}, u32[]{:S(2)}, u32[]{:S(2)}) collective-permute-start(f32[4,40,128]{2,1,0:T(8,128)S(1)} %get-tuple-element.75), channel_id=1, source_target_pairs={{0,16},{4,20},{8,24},{12,28},{16,32},{20,36},{24,40},{28,44},{32,4... | collective-permute-start | bytes 245768 | tf_op jit(solution)/shard_map/ppermute | solution.py:16
  49.9 9.1 %collective-permute-start.8 = (f32[4,40,128]{2,1,0:T(8,128)S(1)}, f32[4,40,128]{2,1,0:T(8,128)S(1)}, u32[]{:S(2)}, u32[]{:S(2)}) collective-permute-start(f32[4,40,128]{2,1,0:T(8,128)S(1)} %get-tuple-element.76), channel_id=1, source_target_pairs={{0,32},{4,36},{8,40},{12,44},{16,48},{20,52},{24,56},{28,60},{32,6... | collective-permute-start | bytes 245768 | tf_op jit(solution)/shard_map/ppermute | solution.py:16
  59.0 2.6 %collective-permute-start.10 = (f32[4,40,128]{2,1,0:T(8,128)S(1)}, f32[4,40,128]{2,1,0:T(8,128)S(1)}, u32[]{:S(2)}, u32[]{:S(2)}) collective-permute-start(f32[4,40,128]{2,1,0:T(8,128)S(1)} %get-tuple-element.78), channel_id=1, source_target_pairs={{0,64},{4,68},{8,72},{12,76},{16,80},{20,84},{24,88},{28,92},{32,9... | collective-permute-start | bytes 245768 | tf_op jit(solution)/shard_map/ppermute | solution.py:16
  63.7 6.1 %collective-permute-start.9 = (f32[4,40,128]{2,1,0:T(8,128)S(1)}, f32[4,40,128]{2,1,0:T(8,128)S(1)}, u32[]{:S(2)}, u32[]{:S(2)}) collective-permute-start(f32[4,40,128]{2,1,0:T(8,128)S(1)} %get-tuple-element.77), channel_id=1, source_target_pairs={{0,48},{4,52},{8,56},{12,60},{16,64},{20,68},{24,72},{28,76},{32,8... | collective-permute-start | bytes 245768 | tf_op jit(solution)/shard_map/ppermute | solution.py:16
  70.0 3.4 %collective-permute-start.4 = (f32[2,8,72,128]{3,2,1,0:T(8,128)S(1)}, f32[2,8,72,128]{3,2,1,0:T(8,128)S(1)}, u32[]{:S(2)}, u32[]{:S(2)}) collective-permute-start(f32[2,8,72,128]{3,2,1,0:T(8,128)S(1)} %pad_maximum_fusion.6), channel_id=1, source_target_pairs={{0,8},{4,12},{8,16},{12,20},{16,24},{20,28},{24,32},{28,36},{32,40... | collective-permute-start | bytes 1769480 | tf_op jit(solution)/shard_map/ppermute | solution.py:16
  74.2 3.2 %collective-permute-start.12 = (f32[4,40,128]{2,1,0:T(8,128)S(1)}, f32[4,40,128]{2,1,0:T(8,128)S(1)}, u32[]{:S(2)}, u32[]{:S(2)}) collective-permute-start(f32[4,40,128]{2,1,0:T(8,128)S(1)} %fusion.261), channel_id=1, source_target_pairs={{0,8},{4,12},{8,0},{12,4},{16,24},{20,28},{24,16},{28,20},{32,40},... | collective-permute-start | bytes 245768 | tf_op jit(solution)/shard_map/ppermute | solution.py:21
  77.4 7.8 %collective-permute-done.12 = f32[4,40,128]{2,1,0:T(8,128)S(1)} collective-permute-done((f32[4,40,128]{2,1,0:T(8,128)S(1)}, f32[4,40,128]{2,1,0:T(8,128)S(1)}, u32[]{:S(2)}, u32[]{:S(2)}) %collective-permute-start.12) | collective-permute-done | bytes 81952 | tf_op jit(solution)/shard_map/ppermute | solution.py:21
  90.4 2.8 %collective-permute-start.14 = (f32[1,72,128]{2,1,0:T(8,128)S(1)}, f32[1,72,128]{2,1,0:T(8,128)S(1)}, u32[]{:S(2)}, u32[]{:S(2)}) collective-permute-start(f32[1,72,128]{2,1,0:T(8,128)S(1)} %get-tuple-element.102), channel_id=1, source_target_pairs={{1,0},{2,1},{3,2},{5,4},{6,5},{7,6},{9,8},{10,9},{11,10},{13,12},{... | collective-permute-start | bytes 110600 | tf_op jit(solution)/shard_map/ppermute | solution.py:28
  93.1 3.1 %collective-permute-start.15 = (f32[1,72,128]{2,1,0:T(8,128)S(1)}, f32[1,72,128]{2,1,0:T(8,128)S(1)}, u32[]{:S(2)}, u32[]{:S(2)}) collective-permute-start(f32[1,72,128]{2,1,0:T(8,128)S(1)} %get-tuple-element.103), channel_id=1, source_target_pairs={{0,1},{1,2},{2,3},{4,5},{5,6},{6,7},{8,9},{9,10},{10,11},{12,13},{... | collective-permute-start | bytes 110600 | tf_op jit(solution)/shard_map/ppermute | solution.py:27
  96.2 2.7 %collective-permute-done.15 = f32[1,72,128]{2,1,0:T(8,128)S(1)} collective-permute-done((f32[1,72,128]{2,1,0:T(8,128)S(1)}, f32[1,72,128]{2,1,0:T(8,128)S(1)}, u32[]{:S(2)}, u32[]{:S(2)}) %collective-permute-start.15) | collective-permute-done | bytes 36896 | tf_op jit(solution)/shard_map/ppermute | solution.py:27
  102.2 2.8 %collective-permute-start.17 = (f32[1,72,128]{2,1,0:T(8,128)S(1)}, f32[1,72,128]{2,1,0:T(8,128)S(1)}, u32[]{:S(2)}, u32[]{:S(2)}) collective-permute-start(f32[1,72,128]{2,1,0:T(8,128)S(1)} %get-tuple-element.100), channel_id=1, source_target_pairs={{1,0},{2,1},{3,2},{5,4},{6,5},{7,6},{9,8},{10,9},{11,10},{13,12},{... | collective-permute-start | bytes 110600 | tf_op jit(solution)/shard_map/ppermute | solution.py:28
  105.0 3.1 %collective-permute-start.18 = (f32[1,72,128]{2,1,0:T(8,128)S(1)}, f32[1,72,128]{2,1,0:T(8,128)S(1)}, u32[]{:S(2)}, u32[]{:S(2)}) collective-permute-start(f32[1,72,128]{2,1,0:T(8,128)S(1)} %get-tuple-element.101), channel_id=1, source_target_pairs={{0,1},{1,2},{2,3},{4,5},{5,6},{6,7},{8,9},{9,10},{10,11},{12,13},{... | collective-permute-start | bytes 110600 | tf_op jit(solution)/shard_map/ppermute | solution.py:27
  108.1 2.7 %collective-permute-done.18 = f32[1,72,128]{2,1,0:T(8,128)S(1)} collective-permute-done((f32[1,72,128]{2,1,0:T(8,128)S(1)}, f32[1,72,128]{2,1,0:T(8,128)S(1)}, u32[]{:S(2)}, u32[]{:S(2)}) %collective-permute-start.18) | collective-permute-done | bytes 36896 | tf_op jit(solution)/shard_map/ppermute | solution.py:27
  117.0 3.8 %collective-permute-start.20 = (f32[2,2,72,128]{3,2,1,0:T(8,128)S(1)}, f32[2,2,72,128]{3,2,1,0:T(8,128)S(1)}, u32[]{:S(2)}, u32[]{:S(2)}) collective-permute-start(f32[2,2,72,128]{3,2,1,0:T(8,128)S(1)} %get-tuple-element.56), channel_id=1, source_target_pairs={{1,0},{2,1},{3,2},{5,4},{6,5},{7,6},{9,8},{10,9},{11,10},{13,12},{... | collective-permute-start | bytes 442376 | tf_op jit(solution)/shard_map/ppermute | solution.py:28
  124.2 3.7 %collective-permute-done.21 = f32[2,8,72,128]{3,2,1,0:T(8,128)S(1)} collective-permute-done((f32[2,8,72,128]{3,2,1,0:T(8,128)S(1)}, f32[2,8,72,128]{3,2,1,0:T(8,128)S(1)}, u32[]{:S(2)}, u32[]{:S(2)}) %collective-permute-start.21) | collective-permute-done | bytes 589856 | tf_op jit(solution)/shard_map/ppermute | solution.py:16
  136.9 3.6 %collective-permute-start.24 = (f32[2,128,128]{2,1,0:T(8,128)S(1)}, f32[2,128,128]{2,1,0:T(8,128)S(1)}, u32[]{:S(2)}, u32[]{:S(2)}) collective-permute-start(f32[2,128,128]{2,1,0:T(8,128)S(1)} %pad_maximum_fusion.25), channel_id=1, source_target_pairs={{1,0},{2,1},{3,2},{5,4},{6,5},{7,6},{9,8},{10,9},{11,10},{13,12},{... | collective-permute-start | bytes 393224 | tf_op jit(solution)/shard_map/ppermute | solution.py:28
  144.2 10.2 %collective-permute-done.25 = f32[8,128,128]{2,1,0:T(8,128)S(1)} collective-permute-done((f32[8,128,128]{2,1,0:T(8,128)S(1)}, f32[8,128,128]{2,1,0:T(8,128)S(1)}, u32[]{:S(2)}, u32[]{:S(2)}) %collective-permute-start.25) | collective-permute-done | bytes 524320 | tf_op jit(solution)/shard_map/ppermute | solution.py:16
  (163 shorter events, 51.4 us)
Async XLA Ops:
  5.5 12.5 %collective-permute-start.1 = (f32[3,3,80,128]{3,2,1,0:T(8,128)S(1)}, f32[3,3,80,128]{3,2,1,0:T(8,128)S(1)}, u32[]{:S(2)}, u32[]{:S(2)}) collective-permute-start(f32[3,3,80,128]{3,2,1,0:T(8,128)S(1)} %get-tuple-element.26), channel_id=1, source_target_pairs={{0,1},{1,2},{2,3},{4,5},{5,6},{6,7},{8,9},{9,10},{10,11},{12,13},{... | collective-permute-start | bytes 1105928 | tf_op jit(solution)/shard_map/ppermute | solution.py:27
  8.9 12.3 %collective-permute-start.2 = (f32[3,3,80,128]{3,2,1,0:T(8,128)S(1)}, f32[3,3,80,128]{3,2,1,0:T(8,128)S(1)}, u32[]{:S(2)}, u32[]{:S(2)}) collective-permute-start(f32[3,3,80,128]{3,2,1,0:T(8,128)S(1)} %get-tuple-element.27), channel_id=1, source_target_pairs={{1,0},{2,1},{3,2},{5,4},{6,5},{7,6},{9,8},{10,9},{11,10},{13,12},{... | collective-permute-start | bytes 1105928 | tf_op jit(solution)/shard_map/ppermute | solution.py:28
  28.0 11.4 %collective-permute-start.5 = (f32[18,40,128]{2,1,0:T(8,128)S(1)}, f32[18,40,128]{2,1,0:T(8,128)S(1)}, u32[]{:S(2)}, u32[]{:S(2)}) collective-permute-start(f32[18,40,128]{2,1,0:T(8,128)S(1)} %pad_maximum_fusion.14), channel_id=1, source_target_pairs={{0,1},{1,2},{2,3},{4,5},{5,6},{6,7},{8,9},{9,10},{10,11},{12,13},{... | collective-permute-start | bytes 1105928 | tf_op jit(solution)/shard_map/ppermute | solution.py:27
  31.1 11.1 %collective-permute-start.6 = (f32[18,40,128]{2,1,0:T(8,128)S(1)}, f32[18,40,128]{2,1,0:T(8,128)S(1)}, u32[]{:S(2)}, u32[]{:S(2)}) collective-permute-start(f32[18,40,128]{2,1,0:T(8,128)S(1)} %pad_maximum_fusion.15), channel_id=1, source_target_pairs={{1,0},{2,1},{3,2},{5,4},{6,5},{7,6},{9,8},{10,9},{11,10},{13,12},{... | collective-permute-start | bytes 1105928 | tf_op jit(solution)/shard_map/ppermute | solution.py:28
  33.9 29.8 %collective-permute-start.3 = (f32[10,72,128]{2,1,0:T(8,128)S(1)}, f32[10,72,128]{2,1,0:T(8,128)S(1)}, u32[]{:S(2)}, u32[]{:S(2)}) collective-permute-start(f32[10,72,128]{2,1,0:T(8,128)S(1)} %slice_select_fusion.5), channel_id=1, source_target_pairs={{0,8},{4,12},{8,16},{12,20},{16,24},{20,28},{24,32},{28,36},{32,40... | collective-permute-start | bytes 1105928 | tf_op jit(solution)/shard_map/ppermute | solution.py:16
  43.8 26.2 %collective-permute-start.7 = (f32[4,40,128]{2,1,0:T(8,128)S(1)}, f32[4,40,128]{2,1,0:T(8,128)S(1)}, u32[]{:S(2)}, u32[]{:S(2)}) collective-permute-start(f32[4,40,128]{2,1,0:T(8,128)S(1)} %get-tuple-element.75), channel_id=1, source_target_pairs={{0,16},{4,20},{8,24},{12,28},{16,32},{20,36},{24,40},{28,44},{32,4... | collective-permute-start | bytes 245768 | tf_op jit(solution)/shard_map/ppermute | solution.py:16
  49.9 23.5 %collective-permute-start.8 = (f32[4,40,128]{2,1,0:T(8,128)S(1)}, f32[4,40,128]{2,1,0:T(8,128)S(1)}, u32[]{:S(2)}, u32[]{:S(2)}) collective-permute-start(f32[4,40,128]{2,1,0:T(8,128)S(1)} %get-tuple-element.76), channel_id=1, source_target_pairs={{0,32},{4,36},{8,40},{12,44},{16,48},{20,52},{24,56},{28,60},{32,6... | collective-permute-start | bytes 245768 | tf_op jit(solution)/shard_map/ppermute | solution.py:16
  59.0 14.4 %collective-permute-start.10 = (f32[4,40,128]{2,1,0:T(8,128)S(1)}, f32[4,40,128]{2,1,0:T(8,128)S(1)}, u32[]{:S(2)}, u32[]{:S(2)}) collective-permute-start(f32[4,40,128]{2,1,0:T(8,128)S(1)} %get-tuple-element.78), channel_id=1, source_target_pairs={{0,64},{4,68},{8,72},{12,76},{16,80},{20,84},{24,88},{28,92},{32,9... | collective-permute-start | bytes 245768 | tf_op jit(solution)/shard_map/ppermute | solution.py:16
  61.6 12.4 %collective-permute-start.11 = (f32[4,40,128]{2,1,0:T(8,128)S(1)}, f32[4,40,128]{2,1,0:T(8,128)S(1)}, u32[]{:S(2)}, u32[]{:S(2)}) collective-permute-start(f32[4,40,128]{2,1,0:T(8,128)S(1)} %get-tuple-element.99), channel_id=1, source_target_pairs={{0,80},{4,84},{8,88},{12,92},{16,96},{20,100},{24,104},{28,108},{3... | collective-permute-start | bytes 245768 | tf_op jit(solution)/shard_map/ppermute | solution.py:16
  63.7 10.4 %collective-permute-start.9 = (f32[4,40,128]{2,1,0:T(8,128)S(1)}, f32[4,40,128]{2,1,0:T(8,128)S(1)}, u32[]{:S(2)}, u32[]{:S(2)}) collective-permute-start(f32[4,40,128]{2,1,0:T(8,128)S(1)} %get-tuple-element.77), channel_id=1, source_target_pairs={{0,48},{4,52},{8,56},{12,60},{16,64},{20,68},{24,72},{28,76},{32,8... | collective-permute-start | bytes 245768 | tf_op jit(solution)/shard_map/ppermute | solution.py:16
  70.0 17.5 %collective-permute-start.4 = (f32[2,8,72,128]{3,2,1,0:T(8,128)S(1)}, f32[2,8,72,128]{3,2,1,0:T(8,128)S(1)}, u32[]{:S(2)}, u32[]{:S(2)}) collective-permute-start(f32[2,8,72,128]{3,2,1,0:T(8,128)S(1)} %pad_maximum_fusion.6), channel_id=1, source_target_pairs={{0,8},{4,12},{8,16},{12,20},{16,24},{20,28},{24,32},{28,36},{32,40... | collective-permute-start | bytes 1769480 | tf_op jit(solution)/shard_map/ppermute | solution.py:16
  74.2 11.0 %collective-permute-start.12 = (f32[4,40,128]{2,1,0:T(8,128)S(1)}, f32[4,40,128]{2,1,0:T(8,128)S(1)}, u32[]{:S(2)}, u32[]{:S(2)}) collective-permute-start(f32[4,40,128]{2,1,0:T(8,128)S(1)} %fusion.261), channel_id=1, source_target_pairs={{0,8},{4,12},{8,0},{12,4},{16,24},{20,28},{24,16},{28,20},{32,40},... | collective-permute-start | bytes 245768 | tf_op jit(solution)/shard_map/ppermute | solution.py:21
  88.0 11.9 %collective-permute-start.13 = (f32[8,72,128]{2,1,0:T(8,128)S(1)}, f32[8,72,128]{2,1,0:T(8,128)S(1)}, u32[]{:S(2)}, u32[]{:S(2)}) collective-permute-start(f32[8,72,128]{2,1,0:T(8,128)S(1)} %get-tuple-element.59), channel_id=1, source_target_pairs={{0,8},{4,12},{8,16},{12,20},{16,24},{20,28},{24,32},{28,36},{32,40... | collective-permute-start | bytes 884744 | tf_op jit(solution)/shard_map/ppermute | solution.py:16
  90.4 5.9 %collective-permute-start.14 = (f32[1,72,128]{2,1,0:T(8,128)S(1)}, f32[1,72,128]{2,1,0:T(8,128)S(1)}, u32[]{:S(2)}, u32[]{:S(2)}) collective-permute-start(f32[1,72,128]{2,1,0:T(8,128)S(1)} %get-tuple-element.102), channel_id=1, source_target_pairs={{1,0},{2,1},{3,2},{5,4},{6,5},{7,6},{9,8},{10,9},{11,10},{13,12},{... | collective-permute-start | bytes 110600 | tf_op jit(solution)/shard_map/ppermute | solution.py:28
  93.1 5.9 %collective-permute-start.15 = (f32[1,72,128]{2,1,0:T(8,128)S(1)}, f32[1,72,128]{2,1,0:T(8,128)S(1)}, u32[]{:S(2)}, u32[]{:S(2)}) collective-permute-start(f32[1,72,128]{2,1,0:T(8,128)S(1)} %get-tuple-element.103), channel_id=1, source_target_pairs={{0,1},{1,2},{2,3},{4,5},{5,6},{6,7},{8,9},{9,10},{10,11},{12,13},{... | collective-permute-start | bytes 110600 | tf_op jit(solution)/shard_map/ppermute | solution.py:27
  100.3 11.9 %collective-permute-start.16 = (f32[8,72,128]{2,1,0:T(8,128)S(1)}, f32[8,72,128]{2,1,0:T(8,128)S(1)}, u32[]{:S(2)}, u32[]{:S(2)}) collective-permute-start(f32[8,72,128]{2,1,0:T(8,128)S(1)} %fusion.119), channel_id=1, source_target_pairs={{0,8},{4,12},{8,16},{12,20},{16,24},{20,28},{24,32},{28,36},{32,40... | collective-permute-start | bytes 884744 | tf_op jit(solution)/shard_map/ppermute | solution.py:16
  102.2 5.9 %collective-permute-start.17 = (f32[1,72,128]{2,1,0:T(8,128)S(1)}, f32[1,72,128]{2,1,0:T(8,128)S(1)}, u32[]{:S(2)}, u32[]{:S(2)}) collective-permute-start(f32[1,72,128]{2,1,0:T(8,128)S(1)} %get-tuple-element.100), channel_id=1, source_target_pairs={{1,0},{2,1},{3,2},{5,4},{6,5},{7,6},{9,8},{10,9},{11,10},{13,12},{... | collective-permute-start | bytes 110600 | tf_op jit(solution)/shard_map/ppermute | solution.py:28
  105.0 5.9 %collective-permute-start.18 = (f32[1,72,128]{2,1,0:T(8,128)S(1)}, f32[1,72,128]{2,1,0:T(8,128)S(1)}, u32[]{:S(2)}, u32[]{:S(2)}) collective-permute-start(f32[1,72,128]{2,1,0:T(8,128)S(1)} %get-tuple-element.101), channel_id=1, source_target_pairs={{0,1},{1,2},{2,3},{4,5},{5,6},{6,7},{8,9},{9,10},{10,11},{12,13},{... | collective-permute-start | bytes 110600 | tf_op jit(solution)/shard_map/ppermute | solution.py:27
  112.8 15.1 %collective-permute-start.21 = (f32[2,8,72,128]{3,2,1,0:T(8,128)S(1)}, f32[2,8,72,128]{3,2,1,0:T(8,128)S(1)}, u32[]{:S(2)}, u32[]{:S(2)}) collective-permute-start(f32[2,8,72,128]{3,2,1,0:T(8,128)S(1)} %pad_maximum_fusion.7), channel_id=1, source_target_pairs={{0,8},{4,12},{8,16},{12,20},{16,24},{20,28},{24,32},{28,36},{32,40... | collective-permute-start | bytes 1769480 | tf_op jit(solution)/shard_map/ppermute | solution.py:16
  114.8 7.0 %collective-permute-start.19 = (f32[2,2,72,128]{3,2,1,0:T(8,128)S(1)}, f32[2,2,72,128]{3,2,1,0:T(8,128)S(1)}, u32[]{:S(2)}, u32[]{:S(2)}) collective-permute-start(f32[2,2,72,128]{3,2,1,0:T(8,128)S(1)} %get-tuple-element.55), channel_id=1, source_target_pairs={{0,1},{1,2},{2,3},{4,5},{5,6},{6,7},{8,9},{9,10},{10,11},{12,13},{... | collective-permute-start | bytes 442376 | tf_op jit(solution)/shard_map/ppermute | solution.py:27
  117.0 7.0 %collective-permute-start.20 = (f32[2,2,72,128]{3,2,1,0:T(8,128)S(1)}, f32[2,2,72,128]{3,2,1,0:T(8,128)S(1)}, u32[]{:S(2)}, u32[]{:S(2)}) collective-permute-start(f32[2,2,72,128]{3,2,1,0:T(8,128)S(1)} %get-tuple-element.56), channel_id=1, source_target_pairs={{1,0},{2,1},{3,2},{5,4},{6,5},{7,6},{9,8},{10,9},{11,10},{13,12},{... | collective-permute-start | bytes 442376 | tf_op jit(solution)/shard_map/ppermute | solution.py:28
  134.6 7.9 %collective-permute-start.23 = (f32[2,128,128]{2,1,0:T(8,128)S(1)}, f32[2,128,128]{2,1,0:T(8,128)S(1)}, u32[]{:S(2)}, u32[]{:S(2)}) collective-permute-start(f32[2,128,128]{2,1,0:T(8,128)S(1)} %pad_maximum_fusion.24), channel_id=1, source_target_pairs={{0,1},{1,2},{2,3},{4,5},{5,6},{6,7},{8,9},{9,10},{10,11},{12,13},{... | collective-permute-start | bytes 393224 | tf_op jit(solution)/shard_map/ppermute | solution.py:27
  136.9 7.2 %collective-permute-start.24 = (f32[2,128,128]{2,1,0:T(8,128)S(1)}, f32[2,128,128]{2,1,0:T(8,128)S(1)}, u32[]{:S(2)}, u32[]{:S(2)}) collective-permute-start(f32[2,128,128]{2,1,0:T(8,128)S(1)} %pad_maximum_fusion.25), channel_id=1, source_target_pairs={{1,0},{2,1},{3,2},{5,4},{6,5},{7,6},{9,8},{10,9},{11,10},{13,12},{... | collective-permute-start | bytes 393224 | tf_op jit(solution)/shard_map/ppermute | solution.py:28
  140.6 13.8 %collective-permute-start.25 = (f32[8,128,128]{2,1,0:T(8,128)S(1)}, f32[8,128,128]{2,1,0:T(8,128)S(1)}, u32[]{:S(2)}, u32[]{:S(2)}) collective-permute-start(f32[8,128,128]{2,1,0:T(8,128)S(1)} %fusion.75), channel_id=1, source_target_pairs={{0,4},{4,8},{8,12},{12,16},{16,20},{20,24},{24,28},{28,32},{32,36}... | collective-permute-start | bytes 1572872 | tf_op jit(solution)/shard_map/ppermute | solution.py:16
  (10 other events, 199.4 us)

commit v5 on v4

--- a/solution.py
+++ b/solution.py
@@ -27,6 +27,15 @@
     below = lax.ppermute(upward, "space", up)
     above = lax.ppermute(downward, "space", [(j, i) for i, j in up])
     return below, above
+
+
+def slanted(upward, downward):
+    times, peers = lax.axis_size("tm"), lax.axis_size("space")
+    axes = ("tm", "space")
+    steps = [(t * peers, (t + 2) * peers) for t in range(times - 2)]
+    up = [(a + i, b + i + 1) for a, b in steps for i in range(peers - 1)]
+    down = [(a + i + 1, b + i) for a, b in steps for i in range(peers - 1)]
+    return lax.ppermute(upward, axes, up), lax.ppermute(downward, axes, down)
 
 
 def framed(value, width, dim=0):
@@ -97,48 +106,46 @@
     mine = window(source[0], low)
     got = flipped(window(source[0], ~low), 1)
     even, odd = jnp.where(low, mine, got), jnp.where(low, got, mine)
-    bundle = framed(jnp.stack([even, odd, window(conductivity, low)]), 3, 1)
+    bundle = framed(jnp.stack([even, odd, window(conductivity, low)]), 2, 1)
     g, cond = bundle[:2], bundle[2]
     d0 = OMEGA / (1.0 + 6.0 * cond)
     d1 = OMEGA / (1.0 + 12.0 * cond)
 
-    c12, c10, c8 = inner(cond, 1), inner(cond, 2), inner(cond, 3)
+    def spill(v, n):
+        return jnp.pad(v, ((n, n), (0, 0), (0, 0)))
+
+    cw = window(conductivity, low)
+    dw = OMEGA / (1.0 + 6.0 * cw)
+    u1 = dw * odd
+    w = u1 + dw * (odd - applied(spill(u1, 1), cw)) + dw * (dw * even)
+    w = w - cw * stencil(spill(dw * u1, 1))
+    before_w = shifted(w, 2)
+    lower, upper = slanted(odd[-1:], odd[:1])
+
+    c10, c8 = inner(cond, 1), inner(cond, 2)
     u1 = d0 * g
-    rest = inner(u1) + inner(d0) * (inner(g) - applied(u1, c12))
-    hop = inner(d0) * inner(u1)
-    odd2 = rest[1] + hop[0]
-    w = inner(odd2) - c10 * stencil(hop[1])
-    local = inner(g[0] + g[1], 2) + inner(rest[0]) - applied(rest[0] + odd2, c10)
-    before_w = shifted(narrow(w), 2)
-
-    def spill(v, n):
-        return jnp.pad(v, ((0, 0), (n, n), (0, 0), (0, 0)))
-
-    part = jnp.stack([inner(local), inner(w)])
-    first = inner(d1, 3) * part
-    swept1 = spill(first, 1) + inner(d1, 2) * (
-        spill(part, 1) - applied(spill(first, 2), 2.0 * c10)
-    )
-    hop1 = inner(d1, 3) * first
-    own = spill(part, 2) - applied(spill(swept1, 2), 2.0 * c12)
-    nxt = spill(swept1, 1) - applied(spill(hop1, 3), 2.0 * c12)
+    rest = inner(u1) + inner(d0) * (inner(g) - applied(u1, c10))
+    odd2 = rest[1] + inner(d0[None] * u1)[0]
+    local = inner(g[0] + g[1], 2) + inner(rest[0]) - applied(rest[0] + odd2, c8)
+    lower = c8[:1] * (d0[2:3] + d0[1:2]) * (d0[1:2] * lower)
+    upper = c8[-1:] * (d0[-3:-2] + d0[-2:-1]) * (d0[-2:-1] * upper)
+    g1 = local + jnp.concatenate([before_w[:1] + lower, before_w[1:-1], before_w[-1:] + upper])
+
+    m1 = inner(d1, 2) * g1
+    rest1 = spill(m1, 1) + inner(d1) * (spill(g1, 1) - applied(spill(m1, 2), 2.0 * c10))
+    hop1 = inner(d1, 2) * m1
+    own = spill(g1, 2) - applied(spill(rest1, 2), 2.0 * cond)
+    nxt = spill(rest1, 1) - applied(spill(hop1, 3), 2.0 * cond)
     carry = spill(hop1, 2)
     share = coarsen(
-        jnp.stack(
-            [
-                own[0] + jnp.where(odd_chip, 0.0, nxt[0] + own[1]),
-                carry[0]
-                + nxt[1]
-                + jnp.where(odd_chip, nxt[0] + own[1], carry[1]),
-                jnp.where(odd_chip, carry[1], 0.0),
-            ]
-        )
+        jnp.stack([own + jnp.where(odd_chip, 0.0, nxt), carry + jnp.where(odd_chip, nxt, 0.0)])
     )
 
     c2 = 4.0 * coarsen(c8)
+    split = g1.reshape(planes, 2, ROWS // 2, g1.shape[-1])
     below, above = exchanged(
-        jnp.concatenate([share[0, -5:], share[1, -5:], share[2, -5:], c2[-3:]]),
-        jnp.concatenate([share[0, :5], share[1, :5], share[2, :5], c2[:3]]),
+        jnp.concatenate([share[0, -5:], share[1, -5:], c2[-3:], split[-1]]),
+        jnp.concatenate([share[0, :5], share[1, :5], c2[:3], split[0]]),
     )
 
     def joined(v, lower, upper):
@@ -148,9 +155,12 @@
         return jnp.concatenate([before, head, v[2:-2], tail, after])
 
     right = [
-        joined(share[i], below[5 * i : 5 * i + 5], above[5 * i : 5 * i + 5]) for i in range(3)
+        joined(share[i], below[5 * i : 5 * i + 5], above[5 * i : 5 * i + 5]) for i in range(2)
     ]
-    c2 = jnp.concatenate([below[15:], c2, above[15:]])
+    c2 = jnp.concatenate([below[10:13], c2, above[10:13]])
+    g1_wide = jnp.concatenate(
+        [below[13:].reshape(1, ROWS, -1), g1, above[13:].reshape(1, ROWS, -1)]
+    )
     d2 = OMEGA / (1.0 + 3.0 * c2)
     base = [d2 * v for v in right]
     terms = list(base)
@@ -164,31 +174,27 @@
             sum(
                 ([kept[j]] if j < count else [])
                 + ([moved[j - 1]] if j else [])
-                + ([base[j]] if j < 3 else [])
+                + ([base[j]] if j < 2 else [])
             )
             for j in range(count + 1)
         ]
-    coarse = terms[0]
-    for j in range(1, 6):
-        coarse = coarse + shifted(terms[j], 4 * j)
+    arrived = [shifted(terms[j], 4 * j) for j in range(1, 5)]
+    coarse = terms[0] + (arrived[0] + arrived[1]) + (arrived[2] + arrived[3])
     coarse = coarse + flipped(coarse, 2)
 
+    prior_m1, prior_odd = shifted(jnp.stack([narrow(m1), narrow(odd)]), 2)
     g, cond, d0, d1 = narrow(g), narrow(cond), narrow(d0), narrow(d1)
-    g1 = narrow(local) + before_w
-    m1 = inner(d1, 2) * g1
-    prior = shifted(jnp.stack([inner(m1), inner(g[1], 3)]), 2)
-    e1, b1, cc = inner(d1, 3), inner(g1), 2.0 * inner(cond, 3)
+    g1 = narrow(g1_wide)
+    m1 = inner(d1) * g1
+    e1, b1, cc = inner(d1, 2), inner(g1), 2.0 * inner(cond, 2)
     rest1 = inner(m1) + e1 * (b1 - applied(m1, cc))
-    middle = rest1 + e1 * prior[0] + narrow(refine(coarse))
+    middle = rest1 + e1 * prior_m1 + narrow(refine(coarse))
     for _ in range(2):
         earlier = shifted(middle, 2)
         middle = middle + e1 * (b1 + earlier - applied(framed(middle, 1), cc))
 
-    g, cond, d0 = inner(g), inner(cond), inner(d0)
     e0 = inner(d0, 2)
-    pre = jnp.stack(
-        [narrow(inner(rest[0], 2)) + e0 * (e0 * prior[1]), narrow(inner(odd2, 2))]
-    )
+    pre = jnp.stack([narrow(inner(rest[0])) + e0 * (e0 * prior_odd), narrow(inner(odd2))])
     state = pre + middle
     sent = shifted(jnp.stack([state[1], e0 * (inner(g[1], 2) + state[0])]), 2)
     state = framed(state, 2, 1)
@@ -217,6 +223,7 @@
     below, above = exchanged(
         jnp.concatenate([state[-1:], lead[1:]]), jnp.concatenate([state[:1], lead[:1]])
     )
+    below, above, earlier = lax.optimization_barrier((below, above, earlier))
     edge = jnp.concatenate([conductivity[:1], conductivity[-1:]])
     de, db = OMEGA / (1.0 + 6.0 * edge), OMEGA / (1.0 + 6.0 * beyond)
     inside = de * edge * (de + db) * jnp.concatenate([below[1:], above[1:]])

time: 157 us -> 141 us (0.90)
  waiting for transfers between devices: 52.3 us -> 41.8 us
  other arithmetic: 14.7 us -> 11.6 us
  starting transfers between devices: 84.1 us -> 81.3 us
    ppermute x11 -> x10, starting transfers between devices: 41.7 us -> 30.7 us  [shifted(): lax.ppermute(value, 'tm', [(i, i + by) for i in range(peers) if 0 <= i +...]
    ppermute x0 -> x2, starting transfers between devices: none -> 9.46 us  [slanted(): return (lax.ppermute(upward, axes, up), lax.ppermute(downward, axes, down))]
    ppermute x6, starting transfers between devices: 18.2 us -> 13.1 us  [exchanged(): above = lax.ppermute(downward, 'space', [(j, i) for i, j in up])]
    ppermute x6, starting transfers between devices: 17.1 us -> 21.9 us  [exchanged(): below = lax.ppermute(upward, 'space', up)]
    ppermute x6, waiting for transfers between devices: 9.59 us -> 4.94 us  [exchanged(): above = lax.ppermute(downward, 'space', [(j, i) for i, j in up])]
    ppermute x6, waiting for transfers between devices: 14 us -> 10.7 us  [exchanged(): below = lax.ppermute(upward, 'space', up)]
    ppermute x3, waiting for transfers between devices: 9.81 us -> 7.28 us  [flipped(): return lax.ppermute(value, 'tm', [(i, i ^ mask) for i in range(peers)])]
    sub x2, other arithmetic: 2.78 us -> 0.54 us  [the longest x1 0.53 us: body(): w = w - cw * stencil(spill(dw * u1, 1))]
  transfers between devices with their start and end apart: 26 -> 27, of which waited for: 18 -> 19; matrix products, arithmetic and copies ran while one was open for 3% -> 3% of each run, Pallas kernels for 0% -> 0%
where the time goes in v5:
time: 141 us; the launch traced here: 140 us
  starting transfers between devices  81.3 us (58%)
  waiting for transfers between devices  41.8 us (30%)
  other arithmetic  11.6 us (8%)
  local copies, waits for them, and re-layouts  3.27 us (2%)
  between operations  1.71 us (1%)
    ppermute x10, starting transfers between devices, shifted(): lax.ppermute(value, 'tm', [(i, i + by) for i in range(peers) if 0 <= i +...  30.7 us
    ppermute x6, starting transfers between devices, exchanged(): below = lax.ppermute(upward, 'space', up)  21.9 us
    ppermute x10, waiting for transfers between devices, shifted(): lax.ppermute(value, 'tm', [(i, i + by) for i in range(peers) if 0 <= i +...  17.1 us
    ppermute x6, starting transfers between devices, exchanged(): above = lax.ppermute(downward, 'space', [(j, i) for i, j in up])  13.1 us
    ppermute x6, waiting for transfers between devices, exchanged(): below = lax.ppermute(upward, 'space', up)  10.7 us
    ppermute x2, starting transfers between devices, slanted(): return (lax.ppermute(upward, axes, up), lax.ppermute(downward, axes, down))  9.46 us
    ppermute x3, waiting for transfers between devices, flipped(): return lax.ppermute(value, 'tm', [(i, i ^ mask) for i in range(peers)])  7.28 us
    ppermute x3, starting transfers between devices, flipped(): return lax.ppermute(value, 'tm', [(i, i ^ mask) for i in range(peers)])  6.01 us
  transfers between devices with their start and end apart: 27, of which 19 were waited for; matrix products, arithmetic and copies ran while one was open for 3% of the time, Pallas kernels for 0%

profile of v5, /device:TPU:34, one launch (start us, length us, event | category | flops | bytes accessed | tf_op | source)
XLA Modules:
  0.0 140.4 jit_solution(9520496817422033704)
XLA Ops:
  6.2 3.4 %collective-permute-start.1 = (f32[3,2,80,128]{3,2,1,0:T(8,128)S(1)}, f32[3,2,80,128]{3,2,1,0:T(8,128)S(1)}, u32[]{:S(2)}, u32[]{:S(2)}) collective-permute-start(f32[3,2,80,128]{3,2,1,0:T(8,128)S(1)} %get-tuple-element.30), channel_id=1, source_target_pairs={{0,1},{1,2},{2,3},{4,5},{5,6},{6,7},{8,9},{9,10},{10,11},{12,13},{... | collective-permute-start | bytes 737288 | tf_op jit(solution)/shard_map/ppermute | solution.py:27
  9.6 2.5 %collective-permute-start.2 = (f32[3,2,80,128]{3,2,1,0:T(8,128)S(1)}, f32[3,2,80,128]{3,2,1,0:T(8,128)S(1)}, u32[]{:S(2)}, u32[]{:S(2)}) collective-permute-start(f32[3,2,80,128]{3,2,1,0:T(8,128)S(1)} %get-tuple-element.31), channel_id=1, source_target_pairs={{1,0},{2,1},{3,2},{5,4},{6,5},{7,6},{9,8},{10,9},{11,10},{13,12},{... | collective-permute-start | bytes 737288 | tf_op jit(solution)/shard_map/ppermute | solution.py:28
  12.0 4.3 %collective-permute-start.3 = (f32[8,80,128]{2,1,0:T(8,128)S(1)}, f32[8,80,128]{2,1,0:T(8,128)S(1)}, u32[]{:S(2)}, u32[]{:S(2)}) collective-permute-start(f32[8,80,128]{2,1,0:T(8,128)S(1)} %get-tuple-element.33), channel_id=1, source_target_pairs={{0,8},{4,12},{8,16},{12,20},{16,24},{20,28},{24,32},{28,36},{32,40... | collective-permute-start | bytes 983048 | tf_op jit(solution)/shard_map/ppermute | solution.py:16
  16.3 5.2 %collective-permute-start.4 = (f32[1,80,128]{2,1,0:T(8,128)S(1)}, f32[1,80,128]{2,1,0:T(8,128)S(1)}, u32[]{:S(2)}, u32[]{:S(2)}) collective-permute-start(f32[1,80,128]{2,1,0:T(8,128)S(1)} %get-tuple-element.79), channel_id=1, source_target_pairs={{0,9},{1,10},{2,11},{4,13},{5,14},{6,15},{8,17},{9,18},{10,19},{12... | collective-permute-start | bytes 122888 | tf_op jit(solution)/shard_map/ppermute | solution.py:38
  21.5 4.3 %collective-permute-start.5 = (f32[1,80,128]{2,1,0:T(8,128)S(1)}, f32[1,80,128]{2,1,0:T(8,128)S(1)}, u32[]{:S(2)}, u32[]{:S(2)}) collective-permute-start(f32[1,80,128]{2,1,0:T(8,128)S(1)} %get-tuple-element.80), channel_id=1, source_target_pairs={{1,8},{2,9},{3,10},{5,12},{6,13},{7,14},{9,16},{10,17},{11,18},{13... | collective-permute-start | bytes 122888 | tf_op jit(solution)/shard_map/ppermute | solution.py:38
  27.7 3.4 %collective-permute-done.3 = f32[8,80,128]{2,1,0:T(8,128)S(1)} collective-permute-done((f32[8,80,128]{2,1,0:T(8,128)S(1)}, f32[8,80,128]{2,1,0:T(8,128)S(1)}, u32[]{:S(2)}, u32[]{:S(2)}) %collective-permute-start.3) | collective-permute-done | bytes 327712 | tf_op jit(solution)/shard_map/ppermute | solution.py:16
  35.5 2.5 %collective-permute-start.8 = (f32[15,40,128]{2,1,0:T(8,128)S(1)}, f32[15,40,128]{2,1,0:T(8,128)S(1)}, u32[]{:S(2)}, u32[]{:S(2)}) collective-permute-start(f32[15,40,128]{2,1,0:T(8,128)S(1)} %pad_maximum_fusion.12), channel_id=1, source_target_pairs={{1,0},{2,1},{3,2},{5,4},{6,5},{7,6},{9,8},{10,9},{11,10},{13,12},{... | collective-permute-start | bytes 921608 | tf_op jit(solution)/shard_map/ppermute | solution.py:28
  38.0 3.4 %collective-permute-start.7 = (f32[15,40,128]{2,1,0:T(8,128)S(1)}, f32[15,40,128]{2,1,0:T(8,128)S(1)}, u32[]{:S(2)}, u32[]{:S(2)}) collective-permute-start(f32[15,40,128]{2,1,0:T(8,128)S(1)} %pad_maximum_fusion.11), channel_id=1, source_target_pairs={{0,1},{1,2},{2,3},{4,5},{5,6},{6,7},{8,9},{9,10},{10,11},{12,13},{... | collective-permute-start | bytes 921608 | tf_op jit(solution)/shard_map/ppermute | solution.py:27
  43.4 4.1 %collective-permute-done.7 = f32[15,40,128]{2,1,0:T(8,128)S(1)} collective-permute-done((f32[15,40,128]{2,1,0:T(8,128)S(1)}, f32[15,40,128]{2,1,0:T(8,128)S(1)}, u32[]{:S(2)}, u32[]{:S(2)}) %collective-permute-start.7) | collective-permute-done | bytes 307232 | tf_op jit(solution)/shard_map/ppermute | solution.py:27
  50.7 5.8 %collective-permute-start.10 = (f32[4,40,128]{2,1,0:T(8,128)S(1)}, f32[4,40,128]{2,1,0:T(8,128)S(1)}, u32[]{:S(2)}, u32[]{:S(2)}) collective-permute-start(f32[4,40,128]{2,1,0:T(8,128)S(1)} %get-tuple-element.71), channel_id=1, source_target_pairs={{0,32},{4,36},{8,40},{12,44},{16,48},{20,52},{24,56},{28,60},{32,6... | collective-permute-start | bytes 245768 | tf_op jit(solution)/shard_map/ppermute | solution.py:16
  56.5 5.7 %collective-permute-start.11 = (f32[4,40,128]{2,1,0:T(8,128)S(1)}, f32[4,40,128]{2,1,0:T(8,128)S(1)}, u32[]{:S(2)}, u32[]{:S(2)}) collective-permute-start(f32[4,40,128]{2,1,0:T(8,128)S(1)} %get-tuple-element.72), channel_id=1, source_target_pairs={{0,48},{4,52},{8,56},{12,60},{16,64},{20,68},{24,72},{28,76},{32,8... | collective-permute-start | bytes 245768 | tf_op jit(solution)/shard_map/ppermute | solution.py:16
  62.2 2.6 %collective-permute-start.12 = (f32[4,40,128]{2,1,0:T(8,128)S(1)}, f32[4,40,128]{2,1,0:T(8,128)S(1)}, u32[]{:S(2)}, u32[]{:S(2)}) collective-permute-start(f32[4,40,128]{2,1,0:T(8,128)S(1)} %get-tuple-element.76), channel_id=1, source_target_pairs={{0,64},{4,68},{8,72},{12,76},{16,80},{20,84},{24,88},{28,92},{32,9... | collective-permute-start | bytes 245768 | tf_op jit(solution)/shard_map/ppermute | solution.py:16
  66.1 3.7 %collective-permute-done.12 = f32[4,40,128]{2,1,0:T(8,128)S(1)} collective-permute-done((f32[4,40,128]{2,1,0:T(8,128)S(1)}, f32[4,40,128]{2,1,0:T(8,128)S(1)}, u32[]{:S(2)}, u32[]{:S(2)}) %collective-permute-start.12) | collective-permute-done | bytes 81952 | tf_op jit(solution)/shard_map/ppermute | solution.py:16
  72.2 4.1 %collective-permute-done.13 = f32[4,40,128]{2,1,0:T(8,128)S(1)} collective-permute-done((f32[4,40,128]{2,1,0:T(8,128)S(1)}, f32[4,40,128]{2,1,0:T(8,128)S(1)}, u32[]{:S(2)}, u32[]{:S(2)}) %collective-permute-start.13) | collective-permute-done | bytes 81952 | tf_op jit(solution)/shard_map/ppermute | solution.py:21
  77.0 2.6 %collective-permute-start.14 = (f32[8,72,128]{2,1,0:T(8,128)S(1)}, f32[8,72,128]{2,1,0:T(8,128)S(1)}, u32[]{:S(2)}, u32[]{:S(2)}) collective-permute-start(f32[8,72,128]{2,1,0:T(8,128)S(1)} %get-tuple-element.49), channel_id=1, source_target_pairs={{0,8},{4,12},{8,16},{12,20},{16,24},{20,28},{24,32},{28,36},{32,40... | collective-permute-start | bytes 884744 | tf_op jit(solution)/shard_map/ppermute | solution.py:16
  81.6 3.9 %collective-permute-start.16 = (f32[1,72,128]{2,1,0:T(8,128)S(1)}, f32[1,72,128]{2,1,0:T(8,128)S(1)}, u32[]{:S(2)}, u32[]{:S(2)}) collective-permute-start(f32[1,72,128]{2,1,0:T(8,128)S(1)} %get-tuple-element.90), channel_id=1, source_target_pairs={{0,1},{1,2},{2,3},{4,5},{5,6},{6,7},{8,9},{9,10},{10,11},{12,13},{... | collective-permute-start | bytes 110600 | tf_op jit(solution)/shard_map/ppermute | solution.py:27
  93.1 3.9 %collective-permute-start.19 = (f32[1,72,128]{2,1,0:T(8,128)S(1)}, f32[1,72,128]{2,1,0:T(8,128)S(1)}, u32[]{:S(2)}, u32[]{:S(2)}) collective-permute-start(f32[1,72,128]{2,1,0:T(8,128)S(1)} %get-tuple-element.88), channel_id=1, source_target_pairs={{0,1},{1,2},{2,3},{4,5},{5,6},{6,7},{8,9},{9,10},{10,11},{12,13},{... | collective-permute-start | bytes 110600 | tf_op jit(solution)/shard_map/ppermute | solution.py:27
  99.0 2.2 %collective-permute-done.17 = f32[8,72,128]{2,1,0:T(8,128)S(1)} collective-permute-done((f32[8,72,128]{2,1,0:T(8,128)S(1)}, f32[8,72,128]{2,1,0:T(8,128)S(1)}, u32[]{:S(2)}, u32[]{:S(2)}) %collective-permute-start.17) | collective-permute-done | bytes 294944 | tf_op jit(solution)/shard_map/ppermute | solution.py:16
  103.7 3.4 %collective-permute-start.20 = (f32[2,2,72,128]{3,2,1,0:T(8,128)S(1)}, f32[2,2,72,128]{3,2,1,0:T(8,128)S(1)}, u32[]{:S(2)}, u32[]{:S(2)}) collective-permute-start(f32[2,2,72,128]{3,2,1,0:T(8,128)S(1)} %get-tuple-element.45), channel_id=1, source_target_pairs={{0,1},{1,2},{2,3},{4,5},{5,6},{6,7},{8,9},{9,10},{10,11},{12,13},{... | collective-permute-start | bytes 442376 | tf_op jit(solution)/shard_map/ppermute | solution.py:27
  107.1 2.5 %collective-permute-start.21 = (f32[2,2,72,128]{3,2,1,0:T(8,128)S(1)}, f32[2,2,72,128]{3,2,1,0:T(8,128)S(1)}, u32[]{:S(2)}, u32[]{:S(2)}) collective-permute-start(f32[2,2,72,128]{3,2,1,0:T(8,128)S(1)} %get-tuple-element.46), channel_id=1, source_target_pairs={{1,0},{2,1},{3,2},{5,4},{6,5},{7,6},{9,8},{10,9},{11,10},{13,12},{... | collective-permute-start | bytes 442376 | tf_op jit(solution)/shard_map/ppermute | solution.py:28
  110.7 3.4 %collective-permute-done.21 = f32[2,2,72,128]{3,2,1,0:T(8,128)S(1)} collective-permute-done((f32[2,2,72,128]{3,2,1,0:T(8,128)S(1)}, f32[2,2,72,128]{3,2,1,0:T(8,128)S(1)}, u32[]{:S(2)}, u32[]{:S(2)}) %collective-permute-start.21) | collective-permute-done | bytes 147488 | tf_op jit(solution)/shard_map/ppermute | solution.py:28
  114.3 2.6 %collective-permute-done.22 = f32[2,8,72,128]{3,2,1,0:T(8,128)S(1)} collective-permute-done((f32[2,8,72,128]{3,2,1,0:T(8,128)S(1)}, f32[2,8,72,128]{3,2,1,0:T(8,128)S(1)}, u32[]{:S(2)}, u32[]{:S(2)}) %collective-permute-start.22) | collective-permute-done | bytes 589856 | tf_op jit(solution)/shard_map/ppermute | solution.py:16
  127.4 3.9 %collective-permute-start.24 = (f32[2,128,128]{2,1,0:T(8,128)S(1)}, f32[2,128,128]{2,1,0:T(8,128)S(1)}, u32[]{:S(2)}, u32[]{:S(2)}) collective-permute-start(f32[2,128,128]{2,1,0:T(8,128)S(1)} %pad_maximum_fusion.24), channel_id=1, source_target_pairs={{0,1},{1,2},{2,3},{4,5},{5,6},{6,7},{8,9},{9,10},{10,11},{12,13},{... | collective-permute-start | bytes 393224 | tf_op jit(solution)/shard_map/ppermute | solution.py:27
  134.7 2.5 %collective-permute-done.26 = f32[8,128,128]{2,1,0:T(8,128)S(1)} collective-permute-done((f32[8,128,128]{2,1,0:T(8,128)S(1)}, f32[8,128,128]{2,1,0:T(8,128)S(1)}, u32[]{:S(2)}, u32[]{:S(2)}) %collective-permute-start.26) | collective-permute-done | bytes 524320 | tf_op jit(solution)/shard_map/ppermute | solution.py:16
  (158 shorter events, 53.0 us)
Async XLA Ops:
  6.2 19.9 %collective-permute-start.1 = (f32[3,2,80,128]{3,2,1,0:T(8,128)S(1)}, f32[3,2,80,128]{3,2,1,0:T(8,128)S(1)}, u32[]{:S(2)}, u32[]{:S(2)}) collective-permute-start(f32[3,2,80,128]{3,2,1,0:T(8,128)S(1)} %get-tuple-element.30), channel_id=1, source_target_pairs={{0,1},{1,2},{2,3},{4,5},{5,6},{6,7},{8,9},{9,10},{10,11},{12,13},{... | collective-permute-start | bytes 737288 | tf_op jit(solution)/shard_map/ppermute | solution.py:27
  9.6 16.5 %collective-permute-start.2 = (f32[3,2,80,128]{3,2,1,0:T(8,128)S(1)}, f32[3,2,80,128]{3,2,1,0:T(8,128)S(1)}, u32[]{:S(2)}, u32[]{:S(2)}) collective-permute-start(f32[3,2,80,128]{3,2,1,0:T(8,128)S(1)} %get-tuple-element.31), channel_id=1, source_target_pairs={{1,0},{2,1},{3,2},{5,4},{6,5},{7,6},{9,8},{10,9},{11,10},{13,12},{... | collective-permute-start | bytes 737288 | tf_op jit(solution)/shard_map/ppermute | solution.py:28
  12.0 19.2 %collective-permute-start.3 = (f32[8,80,128]{2,1,0:T(8,128)S(1)}, f32[8,80,128]{2,1,0:T(8,128)S(1)}, u32[]{:S(2)}, u32[]{:S(2)}) collective-permute-start(f32[8,80,128]{2,1,0:T(8,128)S(1)} %get-tuple-element.33), channel_id=1, source_target_pairs={{0,8},{4,12},{8,16},{12,20},{16,24},{20,28},{24,32},{28,36},{32,40... | collective-permute-start | bytes 983048 | tf_op jit(solution)/shard_map/ppermute | solution.py:16
  16.3 14.9 %collective-permute-start.4 = (f32[1,80,128]{2,1,0:T(8,128)S(1)}, f32[1,80,128]{2,1,0:T(8,128)S(1)}, u32[]{:S(2)}, u32[]{:S(2)}) collective-permute-start(f32[1,80,128]{2,1,0:T(8,128)S(1)} %get-tuple-element.79), channel_id=1, source_target_pairs={{0,9},{1,10},{2,11},{4,13},{5,14},{6,15},{8,17},{9,18},{10,19},{12... | collective-permute-start | bytes 122888 | tf_op jit(solution)/shard_map/ppermute | solution.py:38
  21.5 11.5 %collective-permute-start.5 = (f32[1,80,128]{2,1,0:T(8,128)S(1)}, f32[1,80,128]{2,1,0:T(8,128)S(1)}, u32[]{:S(2)}, u32[]{:S(2)}) collective-permute-start(f32[1,80,128]{2,1,0:T(8,128)S(1)} %get-tuple-element.80), channel_id=1, source_target_pairs={{1,8},{2,9},{3,10},{5,12},{6,13},{7,14},{9,16},{10,17},{11,18},{13... | collective-permute-start | bytes 122888 | tf_op jit(solution)/shard_map/ppermute | solution.py:38
  35.5 12.1 %collective-permute-start.8 = (f32[15,40,128]{2,1,0:T(8,128)S(1)}, f32[15,40,128]{2,1,0:T(8,128)S(1)}, u32[]{:S(2)}, u32[]{:S(2)}) collective-permute-start(f32[15,40,128]{2,1,0:T(8,128)S(1)} %pad_maximum_fusion.12), channel_id=1, source_target_pairs={{1,0},{2,1},{3,2},{5,4},{6,5},{7,6},{9,8},{10,9},{11,10},{13,12},{... | collective-permute-start | bytes 921608 | tf_op jit(solution)/shard_map/ppermute | solution.py:28
  38.0 9.5 %collective-permute-start.7 = (f32[15,40,128]{2,1,0:T(8,128)S(1)}, f32[15,40,128]{2,1,0:T(8,128)S(1)}, u32[]{:S(2)}, u32[]{:S(2)}) collective-permute-start(f32[15,40,128]{2,1,0:T(8,128)S(1)} %pad_maximum_fusion.11), channel_id=1, source_target_pairs={{0,1},{1,2},{2,3},{4,5},{5,6},{6,7},{8,9},{9,10},{10,11},{12,13},{... | collective-permute-start | bytes 921608 | tf_op jit(solution)/shard_map/ppermute | solution.py:27
  41.5 35.1 %collective-permute-start.6 = (f32[2,8,72,128]{3,2,1,0:T(8,128)S(1)}, f32[2,8,72,128]{3,2,1,0:T(8,128)S(1)}, u32[]{:S(2)}, u32[]{:S(2)}) collective-permute-start(f32[2,8,72,128]{3,2,1,0:T(8,128)S(1)} %pad_maximum_fusion.5), channel_id=1, source_target_pairs={{0,8},{4,12},{8,16},{12,20},{16,24},{20,28},{24,32},{28,36},{32,40... | collective-permute-start | bytes 1769480 | tf_op jit(solution)/shard_map/ppermute | solution.py:16
  48.8 16.1 %collective-permute-start.9 = (f32[4,40,128]{2,1,0:T(8,128)S(1)}, f32[4,40,128]{2,1,0:T(8,128)S(1)}, u32[]{:S(2)}, u32[]{:S(2)}) collective-permute-start(f32[4,40,128]{2,1,0:T(8,128)S(1)} %get-tuple-element.107), channel_id=1, source_target_pairs={{0,16},{4,20},{8,24},{12,28},{16,32},{20,36},{24,40},{28,44},{32,4... | collective-permute-start | bytes 245768 | tf_op jit(solution)/shard_map/ppermute | solution.py:16
  50.7 14.5 %collective-permute-start.10 = (f32[4,40,128]{2,1,0:T(8,128)S(1)}, f32[4,40,128]{2,1,0:T(8,128)S(1)}, u32[]{:S(2)}, u32[]{:S(2)}) collective-permute-start(f32[4,40,128]{2,1,0:T(8,128)S(1)} %get-tuple-element.71), channel_id=1, source_target_pairs={{0,32},{4,36},{8,40},{12,44},{16,48},{20,52},{24,56},{28,60},{32,6... | collective-permute-start | bytes 245768 | tf_op jit(solution)/shard_map/ppermute | solution.py:16
  56.5 9.6 %collective-permute-start.11 = (f32[4,40,128]{2,1,0:T(8,128)S(1)}, f32[4,40,128]{2,1,0:T(8,128)S(1)}, u32[]{:S(2)}, u32[]{:S(2)}) collective-permute-start(f32[4,40,128]{2,1,0:T(8,128)S(1)} %get-tuple-element.72), channel_id=1, source_target_pairs={{0,48},{4,52},{8,56},{12,60},{16,64},{20,68},{24,72},{28,76},{32,8... | collective-permute-start | bytes 245768 | tf_op jit(solution)/shard_map/ppermute | solution.py:16
  62.2 7.5 %collective-permute-start.12 = (f32[4,40,128]{2,1,0:T(8,128)S(1)}, f32[4,40,128]{2,1,0:T(8,128)S(1)}, u32[]{:S(2)}, u32[]{:S(2)}) collective-permute-start(f32[4,40,128]{2,1,0:T(8,128)S(1)} %get-tuple-element.76), channel_id=1, source_target_pairs={{0,64},{4,68},{8,72},{12,76},{16,80},{20,84},{24,88},{28,92},{32,9... | collective-permute-start | bytes 245768 | tf_op jit(solution)/shard_map/ppermute | solution.py:16
  69.9 6.3 %collective-permute-start.13 = (f32[4,40,128]{2,1,0:T(8,128)S(1)}, f32[4,40,128]{2,1,0:T(8,128)S(1)}, u32[]{:S(2)}, u32[]{:S(2)}) collective-permute-start(f32[4,40,128]{2,1,0:T(8,128)S(1)} %fusion.249), channel_id=1, source_target_pairs={{0,8},{4,12},{8,0},{12,4},{16,24},{20,28},{24,16},{28,20},{32,40},... | collective-permute-start | bytes 245768 | tf_op jit(solution)/shard_map/ppermute | solution.py:21
  77.0 11.9 %collective-permute-start.14 = (f32[8,72,128]{2,1,0:T(8,128)S(1)}, f32[8,72,128]{2,1,0:T(8,128)S(1)}, u32[]{:S(2)}, u32[]{:S(2)}) collective-permute-start(f32[8,72,128]{2,1,0:T(8,128)S(1)} %get-tuple-element.49), channel_id=1, source_target_pairs={{0,8},{4,12},{8,16},{12,20},{16,24},{20,28},{24,32},{28,36},{32,40... | collective-permute-start | bytes 884744 | tf_op jit(solution)/shard_map/ppermute | solution.py:16
  79.7 5.9 %collective-permute-start.15 = (f32[1,72,128]{2,1,0:T(8,128)S(1)}, f32[1,72,128]{2,1,0:T(8,128)S(1)}, u32[]{:S(2)}, u32[]{:S(2)}) collective-permute-start(f32[1,72,128]{2,1,0:T(8,128)S(1)} %get-tuple-element.89), channel_id=1, source_target_pairs={{1,0},{2,1},{3,2},{5,4},{6,5},{7,6},{9,8},{10,9},{11,10},{13,12},{... | collective-permute-start | bytes 110600 | tf_op jit(solution)/shard_map/ppermute | solution.py:28
  81.6 5.9 %collective-permute-start.16 = (f32[1,72,128]{2,1,0:T(8,128)S(1)}, f32[1,72,128]{2,1,0:T(8,128)S(1)}, u32[]{:S(2)}, u32[]{:S(2)}) collective-permute-start(f32[1,72,128]{2,1,0:T(8,128)S(1)} %get-tuple-element.90), channel_id=1, source_target_pairs={{0,1},{1,2},{2,3},{4,5},{5,6},{6,7},{8,9},{9,10},{10,11},{12,13},{... | collective-permute-start | bytes 110600 | tf_op jit(solution)/shard_map/ppermute | solution.py:27
  89.3 11.9 %collective-permute-start.17 = (f32[8,72,128]{2,1,0:T(8,128)S(1)}, f32[8,72,128]{2,1,0:T(8,128)S(1)}, u32[]{:S(2)}, u32[]{:S(2)}) collective-permute-start(f32[8,72,128]{2,1,0:T(8,128)S(1)} %fusion.133), channel_id=1, source_target_pairs={{0,8},{4,12},{8,16},{12,20},{16,24},{20,28},{24,32},{28,36},{32,40... | collective-permute-start | bytes 884744 | tf_op jit(solution)/shard_map/ppermute | solution.py:16
  91.2 5.9 %collective-permute-start.18 = (f32[1,72,128]{2,1,0:T(8,128)S(1)}, f32[1,72,128]{2,1,0:T(8,128)S(1)}, u32[]{:S(2)}, u32[]{:S(2)}) collective-permute-start(f32[1,72,128]{2,1,0:T(8,128)S(1)} %get-tuple-element.87), channel_id=1, source_target_pairs={{1,0},{2,1},{3,2},{5,4},{6,5},{7,6},{9,8},{10,9},{11,10},{13,12},{... | collective-permute-start | bytes 110600 | tf_op jit(solution)/shard_map/ppermute | solution.py:28
  101.7 15.1 %collective-permute-start.22 = (f32[2,8,72,128]{3,2,1,0:T(8,128)S(1)}, f32[2,8,72,128]{3,2,1,0:T(8,128)S(1)}, u32[]{:S(2)}, u32[]{:S(2)}) collective-permute-start(f32[2,8,72,128]{3,2,1,0:T(8,128)S(1)} %pad_maximum_fusion.6), channel_id=1, source_target_pairs={{0,8},{4,12},{8,16},{12,20},{16,24},{20,28},{24,32},{28,36},{32,40... | collective-permute-start | bytes 1769480 | tf_op jit(solution)/shard_map/ppermute | solution.py:16
  103.7 7.0 %collective-permute-start.20 = (f32[2,2,72,128]{3,2,1,0:T(8,128)S(1)}, f32[2,2,72,128]{3,2,1,0:T(8,128)S(1)}, u32[]{:S(2)}, u32[]{:S(2)}) collective-permute-start(f32[2,2,72,128]{3,2,1,0:T(8,128)S(1)} %get-tuple-element.45), channel_id=1, source_target_pairs={{0,1},{1,2},{2,3},{4,5},{5,6},{6,7},{8,9},{9,10},{10,11},{12,13},{... | collective-permute-start | bytes 442376 | tf_op jit(solution)/shard_map/ppermute | solution.py:27
  107.1 7.0 %collective-permute-start.21 = (f32[2,2,72,128]{3,2,1,0:T(8,128)S(1)}, f32[2,2,72,128]{3,2,1,0:T(8,128)S(1)}, u32[]{:S(2)}, u32[]{:S(2)}) collective-permute-start(f32[2,2,72,128]{3,2,1,0:T(8,128)S(1)} %get-tuple-element.46), channel_id=1, source_target_pairs={{1,0},{2,1},{3,2},{5,4},{6,5},{7,6},{9,8},{10,9},{11,10},{13,12},{... | collective-permute-start | bytes 442376 | tf_op jit(solution)/shard_map/ppermute | solution.py:28
  123.4 13.8 %collective-permute-start.26 = (f32[8,128,128]{2,1,0:T(8,128)S(1)}, f32[8,128,128]{2,1,0:T(8,128)S(1)}, u32[]{:S(2)}, u32[]{:S(2)}) collective-permute-start(f32[8,128,128]{2,1,0:T(8,128)S(1)} %fusion.43), channel_id=1, source_target_pairs={{0,4},{4,8},{8,12},{12,16},{16,20},{20,24},{24,28},{28,32},{32,36}... | collective-permute-start | bytes 1572872 | tf_op jit(solution)/shard_map/ppermute | solution.py:16
  125.5 7.5 %collective-permute-start.25 = (f32[2,128,128]{2,1,0:T(8,128)S(1)}, f32[2,128,128]{2,1,0:T(8,128)S(1)}, u32[]{:S(2)}, u32[]{:S(2)}) collective-permute-start(f32[2,128,128]{2,1,0:T(8,128)S(1)} %pad_maximum_fusion.25), channel_id=1, source_target_pairs={{1,0},{2,1},{3,2},{5,4},{6,5},{7,6},{9,8},{10,9},{11,10},{13,12},{... | collective-permute-start | bytes 393224 | tf_op jit(solution)/shard_map/ppermute | solution.py:28
  127.4 7.3 %collective-permute-start.24 = (f32[2,128,128]{2,1,0:T(8,128)S(1)}, f32[2,128,128]{2,1,0:T(8,128)S(1)}, u32[]{:S(2)}, u32[]{:S(2)}) collective-permute-start(f32[2,128,128]{2,1,0:T(8,128)S(1)} %pad_maximum_fusion.24), channel_id=1, source_target_pairs={{0,1},{1,2},{2,3},{4,5},{5,6},{6,7},{8,9},{9,10},{10,11},{12,13},{... | collective-permute-start | bytes 393224 | tf_op jit(solution)/shard_map/ppermute | solution.py:27
  (10 other events, 102.0 us)

commit v6 on v5

--- a/solution.py
+++ b/solution.py
@@ -1,5 +1,6 @@
 import jax
 import jax.numpy as jnp
+import numpy as np
 from jax import lax
 from jax.sharding import PartitionSpec as P
 
@@ -70,9 +71,7 @@
 
 
 def pair_matrix(rows):
-    i = lax.broadcasted_iota(jnp.int32, (rows // 2, rows), 0)
-    j = lax.broadcasted_iota(jnp.int32, (rows // 2, rows), 1)
-    return (j // 2 == i).astype(jnp.float32)
+    return np.repeat(np.eye(rows // 2, dtype=np.float32), 2, axis=1)
 
 
 def coarsen(v):
@@ -106,10 +105,6 @@
     mine = window(source[0], low)
     got = flipped(window(source[0], ~low), 1)
     even, odd = jnp.where(low, mine, got), jnp.where(low, got, mine)
-    bundle = framed(jnp.stack([even, odd, window(conductivity, low)]), 2, 1)
-    g, cond = bundle[:2], bundle[2]
-    d0 = OMEGA / (1.0 + 6.0 * cond)
-    d1 = OMEGA / (1.0 + 12.0 * cond)
 
     def spill(v, n):
         return jnp.pad(v, ((n, n), (0, 0), (0, 0)))
@@ -120,7 +115,14 @@
     w = u1 + dw * (odd - applied(spill(u1, 1), cw)) + dw * (dw * even)
     w = w - cw * stencil(spill(dw * u1, 1))
     before_w = shifted(w, 2)
+    slab = jnp.stack([even, odd, cw]) + 0.0 * w
     lower, upper = slanted(odd[-1:], odd[:1])
+
+    bundle = framed(slab, 2, 1)
+    bundle = jnp.concatenate([bundle[:, :2] + 0.0 * before_w[:2], bundle[:, 2:]], axis=1)
+    g, cond = bundle[:2], bundle[2]
+    d0 = OMEGA / (1.0 + 6.0 * cond)
+    d1 = OMEGA / (1.0 + 12.0 * cond)
 
     c10, c8 = inner(cond, 1), inner(cond, 2)
     u1 = d0 * g
@@ -230,13 +232,14 @@
     outside = db * beyond * (de + db) * lead
     outside = jnp.where(low, outside, 0.0)
 
-    def mended(v, keep):
-        fix = jnp.where(keep, inside, 0.0)
-        return jnp.concatenate([v[:1] + fix[:1], v[1:-1], v[-1:] + fix[1:]])
-
-    state, earlier = mended(state, low), mended(earlier, ~low)
+    def spread(v):
+        gap = jnp.pad(v[:1], ((0, planes - 1), (0, 0), (0, 0)))
+        return gap + jnp.pad(v[1:], ((planes - 1, 0), (0, 0), (0, 0)))
+
+    fix = spread(inside)
+    state = state + jnp.where(low, fix, 0.0)
     wide = jnp.concatenate([below[:1] + outside[:1], state, above[:1] + outside[1:]])
-    last = source[0] + earlier - applied(wide, conductivity)
+    last = source[0] + (earlier + jnp.where(low, 0.0, fix)) - applied(wide, conductivity)
     return state[None], last[None]
 
 

time: 141 us -> 141 us (level)
  the two profiles are of different devices: /device:TPU:34 before, /device:TPU:38 now
where the time goes in v6:
time: 141 us; the launch traced here: 140 us
  starting transfers between devices  77.7 us (55%)
  waiting for transfers between devices  45.4 us (32%)
  other arithmetic  12.1 us (9%)
  local copies, waits for them, and re-layouts  2.4 us (2%)
  between operations  1.71 us (1%)
    ppermute x10, starting transfers between devices, shifted(): lax.ppermute(value, 'tm', [(i, i + by) for i in range(peers) if 0 <= i +...  32.6 us
    ppermute x6, starting transfers between devices, exchanged(): above = lax.ppermute(downward, 'space', [(j, i) for i, j in up])  21.9 us
    ppermute x6, waiting for transfers between devices, exchanged(): below = lax.ppermute(upward, 'space', up)  19.4 us
    ppermute x10, waiting for transfers between devices, shifted(): lax.ppermute(value, 'tm', [(i, i + by) for i in range(peers) if 0 <= i +...  13.6 us
    ppermute x2, starting transfers between devices, slanted(): return (lax.ppermute(upward, axes, up), lax.ppermute(downward, axes, down))  9.46 us
    ppermute x6, starting transfers between devices, exchanged(): below = lax.ppermute(upward, 'space', up)  7.75 us
    ppermute x3, waiting for transfers between devices, flipped(): return lax.ppermute(value, 'tm', [(i, i ^ mask) for i in range(peers)])  7.32 us
    ppermute x3, starting transfers between devices, flipped(): return lax.ppermute(value, 'tm', [(i, i ^ mask) for i in range(peers)])  6.01 us
  transfers between devices with their start and end apart: 27, of which 20 were waited for; matrix products, arithmetic and copies ran while one was open for 3% of the time, Pallas kernels for 0%

profile of v6, /device:TPU:38, one launch (start us, length us, event | category | flops | bytes accessed | tf_op | source)
XLA Modules:
  0.0 140.3 jit_solution(13111114570473947521)
XLA Ops:
  7.7 4.3 %collective-permute-start.2 = (f32[8,80,128]{2,1,0:T(8,128)S(1)}, f32[8,80,128]{2,1,0:T(8,128)S(1)}, u32[]{:S(2)}, u32[]{:S(2)}) collective-permute-start(f32[8,80,128]{2,1,0:T(8,128)S(1)} %get-tuple-element.18), channel_id=1, source_target_pairs={{0,8},{4,12},{8,16},{12,20},{16,24},{20,28},{24,32},{28,36},{32,40... | collective-permute-start | bytes 983048 | tf_op jit(solution)/shard_map/ppermute | solution.py:17
  12.0 4.6 %collective-permute-start.3 = (f32[3,2,80,128]{3,2,1,0:T(8,128)S(1)}, f32[3,2,80,128]{3,2,1,0:T(8,128)S(1)}, u32[]{:S(2)}, u32[]{:S(2)}) collective-permute-start(f32[3,2,80,128]{3,2,1,0:T(8,128)S(1)} %get-tuple-element.31), channel_id=1, source_target_pairs={{1,0},{2,1},{3,2},{5,4},{6,5},{7,6},{9,8},{10,9},{11,10},{13,12},{... | collective-permute-start | bytes 737288 | tf_op jit(solution)/shard_map/ppermute | solution.py:29
  17.8 8.2 %collective-permute-start.5 = (f32[1,80,128]{2,1,0:T(8,128)S(1)}, f32[1,80,128]{2,1,0:T(8,128)S(1)}, u32[]{:S(2)}, u32[]{:S(2)}) collective-permute-start(f32[1,80,128]{2,1,0:T(8,128)S(1)} %get-tuple-element.76), channel_id=1, source_target_pairs={{1,8},{2,9},{3,10},{5,12},{6,13},{7,14},{9,16},{10,17},{11,18},{13... | collective-permute-start | bytes 122888 | tf_op jit(solution)/shard_map/ppermute | solution.py:39
  32.8 4.8 %collective-permute-start.8 = (f32[15,40,128]{2,1,0:T(8,128)S(1)}, f32[15,40,128]{2,1,0:T(8,128)S(1)}, u32[]{:S(2)}, u32[]{:S(2)}) collective-permute-start(f32[15,40,128]{2,1,0:T(8,128)S(1)} %pad_maximum_fusion.13), channel_id=1, source_target_pairs={{1,0},{2,1},{3,2},{5,4},{6,5},{7,6},{9,8},{10,9},{11,10},{13,12},{... | collective-permute-start | bytes 921608 | tf_op jit(solution)/shard_map/ppermute | solution.py:29
  41.0 5.6 %collective-permute-done.7 = f32[15,40,128]{2,1,0:T(8,128)S(1)} collective-permute-done((f32[15,40,128]{2,1,0:T(8,128)S(1)}, f32[15,40,128]{2,1,0:T(8,128)S(1)}, u32[]{:S(2)}, u32[]{:S(2)}) %collective-permute-start.7) | collective-permute-done | bytes 307232 | tf_op jit(solution)/shard_map/ppermute | solution.py:28
  47.9 3.8 %collective-permute-start.9 = (f32[4,40,128]{2,1,0:T(8,128)S(1)}, f32[4,40,128]{2,1,0:T(8,128)S(1)}, u32[]{:S(2)}, u32[]{:S(2)}) collective-permute-start(f32[4,40,128]{2,1,0:T(8,128)S(1)} %get-tuple-element.103), channel_id=1, source_target_pairs={{0,16},{4,20},{8,24},{12,28},{16,32},{20,36},{24,40},{28,44},{32,4... | collective-permute-start | bytes 245768 | tf_op jit(solution)/shard_map/ppermute | solution.py:17
  51.7 5.0 %collective-permute-start.10 = (f32[4,40,128]{2,1,0:T(8,128)S(1)}, f32[4,40,128]{2,1,0:T(8,128)S(1)}, u32[]{:S(2)}, u32[]{:S(2)}) collective-permute-start(f32[4,40,128]{2,1,0:T(8,128)S(1)} %get-tuple-element.67), channel_id=1, source_target_pairs={{0,32},{4,36},{8,40},{12,44},{16,48},{20,52},{24,56},{28,60},{32,6... | collective-permute-start | bytes 245768 | tf_op jit(solution)/shard_map/ppermute | solution.py:17
  56.6 6.1 %collective-permute-start.11 = (f32[4,40,128]{2,1,0:T(8,128)S(1)}, f32[4,40,128]{2,1,0:T(8,128)S(1)}, u32[]{:S(2)}, u32[]{:S(2)}) collective-permute-start(f32[4,40,128]{2,1,0:T(8,128)S(1)} %get-tuple-element.68), channel_id=1, source_target_pairs={{0,48},{4,52},{8,56},{12,60},{16,64},{20,68},{24,72},{28,76},{32,8... | collective-permute-start | bytes 245768 | tf_op jit(solution)/shard_map/ppermute | solution.py:17
  62.8 2.6 %collective-permute-start.12 = (f32[4,40,128]{2,1,0:T(8,128)S(1)}, f32[4,40,128]{2,1,0:T(8,128)S(1)}, u32[]{:S(2)}, u32[]{:S(2)}) collective-permute-start(f32[4,40,128]{2,1,0:T(8,128)S(1)} %get-tuple-element.72), channel_id=1, source_target_pairs={{0,64},{4,68},{8,72},{12,76},{16,80},{20,84},{24,88},{28,92},{32,9... | collective-permute-start | bytes 245768 | tf_op jit(solution)/shard_map/ppermute | solution.py:17
  67.2 3.1 %collective-permute-done.12 = f32[4,40,128]{2,1,0:T(8,128)S(1)} collective-permute-done((f32[4,40,128]{2,1,0:T(8,128)S(1)}, f32[4,40,128]{2,1,0:T(8,128)S(1)}, u32[]{:S(2)}, u32[]{:S(2)}) %collective-permute-start.12) | collective-permute-done | bytes 81952 | tf_op jit(solution)/shard_map/ppermute | solution.py:17
  70.5 2.2 %collective-permute-start.13 = (f32[4,40,128]{2,1,0:T(8,128)S(1)}, f32[4,40,128]{2,1,0:T(8,128)S(1)}, u32[]{:S(2)}, u32[]{:S(2)}) collective-permute-start(f32[4,40,128]{2,1,0:T(8,128)S(1)} %fusion.249), channel_id=1, source_target_pairs={{0,8},{4,12},{8,0},{12,4},{16,24},{20,28},{24,16},{28,20},{32,40},... | collective-permute-start | bytes 245768 | tf_op jit(solution)/shard_map/ppermute | solution.py:22
  72.7 4.1 %collective-permute-done.13 = f32[4,40,128]{2,1,0:T(8,128)S(1)} collective-permute-done((f32[4,40,128]{2,1,0:T(8,128)S(1)}, f32[4,40,128]{2,1,0:T(8,128)S(1)}, u32[]{:S(2)}, u32[]{:S(2)}) %collective-permute-start.13) | collective-permute-done | bytes 81952 | tf_op jit(solution)/shard_map/ppermute | solution.py:22
  77.6 3.0 %collective-permute-start.14 = (f32[8,72,128]{2,1,0:T(8,128)S(1)}, f32[8,72,128]{2,1,0:T(8,128)S(1)}, u32[]{:S(2)}, u32[]{:S(2)}) collective-permute-start(f32[8,72,128]{2,1,0:T(8,128)S(1)} %get-tuple-element.47), channel_id=1, source_target_pairs={{0,8},{4,12},{8,16},{12,20},{16,24},{20,28},{24,32},{28,36},{32,40... | collective-permute-start | bytes 884744 | tf_op jit(solution)/shard_map/ppermute | solution.py:17
  80.7 2.6 %collective-permute-start.15 = (f32[1,72,128]{2,1,0:T(8,128)S(1)}, f32[1,72,128]{2,1,0:T(8,128)S(1)}, u32[]{:S(2)}, u32[]{:S(2)}) collective-permute-start(f32[1,72,128]{2,1,0:T(8,128)S(1)} %get-tuple-element.85), channel_id=1, source_target_pairs={{1,0},{2,1},{3,2},{5,4},{6,5},{7,6},{9,8},{10,9},{11,10},{13,12},{... | collective-permute-start | bytes 110600 | tf_op jit(solution)/shard_map/ppermute | solution.py:29
  84.9 4.2 %collective-permute-done.16 = f32[1,72,128]{2,1,0:T(8,128)S(1)} collective-permute-done((f32[1,72,128]{2,1,0:T(8,128)S(1)}, f32[1,72,128]{2,1,0:T(8,128)S(1)}, u32[]{:S(2)}, u32[]{:S(2)}) %collective-permute-start.16) | collective-permute-done | bytes 36896 | tf_op jit(solution)/shard_map/ppermute | solution.py:28
  91.8 2.7 %collective-permute-start.18 = (f32[1,72,128]{2,1,0:T(8,128)S(1)}, f32[1,72,128]{2,1,0:T(8,128)S(1)}, u32[]{:S(2)}, u32[]{:S(2)}) collective-permute-start(f32[1,72,128]{2,1,0:T(8,128)S(1)} %get-tuple-element.83), channel_id=1, source_target_pairs={{1,0},{2,1},{3,2},{5,4},{6,5},{7,6},{9,8},{10,9},{11,10},{13,12},{... | collective-permute-start | bytes 110600 | tf_op jit(solution)/shard_map/ppermute | solution.py:29
  96.2 4.5 %collective-permute-done.19 = f32[1,72,128]{2,1,0:T(8,128)S(1)} collective-permute-done((f32[1,72,128]{2,1,0:T(8,128)S(1)}, f32[1,72,128]{2,1,0:T(8,128)S(1)}, u32[]{:S(2)}, u32[]{:S(2)}) %collective-permute-start.19) | collective-permute-done | bytes 36896 | tf_op jit(solution)/shard_map/ppermute | solution.py:28
  105.9 4.7 %collective-permute-start.21 = (f32[2,2,72,128]{3,2,1,0:T(8,128)S(1)}, f32[2,2,72,128]{3,2,1,0:T(8,128)S(1)}, u32[]{:S(2)}, u32[]{:S(2)}) collective-permute-start(f32[2,2,72,128]{3,2,1,0:T(8,128)S(1)} %get-tuple-element.44), channel_id=1, source_target_pairs={{1,0},{2,1},{3,2},{5,4},{6,5},{7,6},{9,8},{10,9},{11,10},{13,12},{... | collective-permute-start | bytes 442376 | tf_op jit(solution)/shard_map/ppermute | solution.py:29
  113.2 4.5 %collective-permute-done.22 = f32[2,8,72,128]{3,2,1,0:T(8,128)S(1)} collective-permute-done((f32[2,8,72,128]{3,2,1,0:T(8,128)S(1)}, f32[2,8,72,128]{3,2,1,0:T(8,128)S(1)}, u32[]{:S(2)}, u32[]{:S(2)}) %collective-permute-start.22) | collective-permute-done | bytes 589856 | tf_op jit(solution)/shard_map/ppermute | solution.py:17
  120.5 1.9 %collective-permute-start.23 = (f32[12,64,128]{2,1,0:T(8,128)S(1)}, f32[12,64,128]{2,1,0:T(8,128)S(1)}, u32[]{:S(2)}, u32[]{:S(2)}) collective-permute-start(f32[12,64,128]{2,1,0:T(8,128)S(1)} %pad_maximum_fusion.9), channel_id=1, source_target_pairs={{0,4},{4,0},{8,12},{12,8},{16,20},{20,16},{24,28},{28,24},{32,36},... | collective-permute-start | bytes 1179656 | tf_op jit(solution)/shard_map/ppermute | solution.py:22
  124.2 2.0 %collective-permute-start.26 = (f32[8,128,128]{2,1,0:T(8,128)S(1)}, f32[8,128,128]{2,1,0:T(8,128)S(1)}, u32[]{:S(2)}, u32[]{:S(2)}) collective-permute-start(f32[8,128,128]{2,1,0:T(8,128)S(1)} %fusion.43), channel_id=1, source_target_pairs={{0,4},{4,8},{8,12},{12,16},{16,20},{20,24},{24,28},{28,32},{32,36}... | collective-permute-start | bytes 1572872 | tf_op jit(solution)/shard_map/ppermute | solution.py:17
  126.3 2.5 %collective-permute-start.25 = (f32[2,128,128]{2,1,0:T(8,128)S(1)}, f32[2,128,128]{2,1,0:T(8,128)S(1)}, u32[]{:S(2)}, u32[]{:S(2)}) collective-permute-start(f32[2,128,128]{2,1,0:T(8,128)S(1)} %pad_maximum_fusion.23), channel_id=1, source_target_pairs={{1,0},{2,1},{3,2},{5,4},{6,5},{7,6},{9,8},{10,9},{11,10},{13,12},{... | collective-permute-start | bytes 393224 | tf_op jit(solution)/shard_map/ppermute | solution.py:29
  131.8 4.1 %collective-permute-done.24 = f32[2,128,128]{2,1,0:T(8,128)S(1)} collective-permute-done((f32[2,128,128]{2,1,0:T(8,128)S(1)}, f32[2,128,128]{2,1,0:T(8,128)S(1)}, u32[]{:S(2)}, u32[]{:S(2)}) %collective-permute-start.24) | collective-permute-done | bytes 131104 | tf_op jit(solution)/shard_map/ppermute | solution.py:28
  135.9 2.2 %collective-permute-done.26 = f32[8,128,128]{2,1,0:T(8,128)S(1)} collective-permute-done((f32[8,128,128]{2,1,0:T(8,128)S(1)}, f32[8,128,128]{2,1,0:T(8,128)S(1)}, u32[]{:S(2)}, u32[]{:S(2)}) %collective-permute-start.26) | collective-permute-done | bytes 524320 | tf_op jit(solution)/shard_map/ppermute | solution.py:17
  (157 shorter events, 45.3 us)
Async XLA Ops:
  6.4 20.2 %collective-permute-start.1 = (f32[3,2,80,128]{3,2,1,0:T(8,128)S(1)}, f32[3,2,80,128]{3,2,1,0:T(8,128)S(1)}, u32[]{:S(2)}, u32[]{:S(2)}) collective-permute-start(f32[3,2,80,128]{3,2,1,0:T(8,128)S(1)} %get-tuple-element.30), channel_id=1, source_target_pairs={{0,1},{1,2},{2,3},{4,5},{5,6},{6,7},{8,9},{9,10},{10,11},{12,13},{... | collective-permute-start | bytes 737288 | tf_op jit(solution)/shard_map/ppermute | solution.py:28
  7.7 18.8 %collective-permute-start.2 = (f32[8,80,128]{2,1,0:T(8,128)S(1)}, f32[8,80,128]{2,1,0:T(8,128)S(1)}, u32[]{:S(2)}, u32[]{:S(2)}) collective-permute-start(f32[8,80,128]{2,1,0:T(8,128)S(1)} %get-tuple-element.18), channel_id=1, source_target_pairs={{0,8},{4,12},{8,16},{12,20},{16,24},{20,28},{24,32},{28,36},{32,40... | collective-permute-start | bytes 983048 | tf_op jit(solution)/shard_map/ppermute | solution.py:17
  12.0 14.6 %collective-permute-start.3 = (f32[3,2,80,128]{3,2,1,0:T(8,128)S(1)}, f32[3,2,80,128]{3,2,1,0:T(8,128)S(1)}, u32[]{:S(2)}, u32[]{:S(2)}) collective-permute-start(f32[3,2,80,128]{3,2,1,0:T(8,128)S(1)} %get-tuple-element.31), channel_id=1, source_target_pairs={{1,0},{2,1},{3,2},{5,4},{6,5},{7,6},{9,8},{10,9},{11,10},{13,12},{... | collective-permute-start | bytes 737288 | tf_op jit(solution)/shard_map/ppermute | solution.py:29
  16.5 13.0 %collective-permute-start.4 = (f32[1,80,128]{2,1,0:T(8,128)S(1)}, f32[1,80,128]{2,1,0:T(8,128)S(1)}, u32[]{:S(2)}, u32[]{:S(2)}) collective-permute-start(f32[1,80,128]{2,1,0:T(8,128)S(1)} %get-tuple-element.75), channel_id=1, source_target_pairs={{0,9},{1,10},{2,11},{4,13},{5,14},{6,15},{8,17},{9,18},{10,19},{12... | collective-permute-start | bytes 122888 | tf_op jit(solution)/shard_map/ppermute | solution.py:39
  17.8 11.7 %collective-permute-start.5 = (f32[1,80,128]{2,1,0:T(8,128)S(1)}, f32[1,80,128]{2,1,0:T(8,128)S(1)}, u32[]{:S(2)}, u32[]{:S(2)}) collective-permute-start(f32[1,80,128]{2,1,0:T(8,128)S(1)} %get-tuple-element.76), channel_id=1, source_target_pairs={{1,8},{2,9},{3,10},{5,12},{6,13},{7,14},{9,16},{10,17},{11,18},{13... | collective-permute-start | bytes 122888 | tf_op jit(solution)/shard_map/ppermute | solution.py:39
  32.8 13.9 %collective-permute-start.8 = (f32[15,40,128]{2,1,0:T(8,128)S(1)}, f32[15,40,128]{2,1,0:T(8,128)S(1)}, u32[]{:S(2)}, u32[]{:S(2)}) collective-permute-start(f32[15,40,128]{2,1,0:T(8,128)S(1)} %pad_maximum_fusion.13), channel_id=1, source_target_pairs={{1,0},{2,1},{3,2},{5,4},{6,5},{7,6},{9,8},{10,9},{11,10},{13,12},{... | collective-permute-start | bytes 921608 | tf_op jit(solution)/shard_map/ppermute | solution.py:29
  37.6 9.0 %collective-permute-start.7 = (f32[15,40,128]{2,1,0:T(8,128)S(1)}, f32[15,40,128]{2,1,0:T(8,128)S(1)}, u32[]{:S(2)}, u32[]{:S(2)}) collective-permute-start(f32[15,40,128]{2,1,0:T(8,128)S(1)} %pad_maximum_fusion.12), channel_id=1, source_target_pairs={{0,1},{1,2},{2,3},{4,5},{5,6},{6,7},{8,9},{9,10},{10,11},{12,13},{... | collective-permute-start | bytes 921608 | tf_op jit(solution)/shard_map/ppermute | solution.py:28
  39.0 38.1 %collective-permute-start.6 = (f32[2,8,72,128]{3,2,1,0:T(8,128)S(1)}, f32[2,8,72,128]{3,2,1,0:T(8,128)S(1)}, u32[]{:S(2)}, u32[]{:S(2)}) collective-permute-start(f32[2,8,72,128]{3,2,1,0:T(8,128)S(1)} %pad_maximum_fusion.5), channel_id=1, source_target_pairs={{0,8},{4,12},{8,16},{12,20},{16,24},{20,28},{24,32},{28,36},{32,40... | collective-permute-start | bytes 1769480 | tf_op jit(solution)/shard_map/ppermute | solution.py:17
  47.9 17.5 %collective-permute-start.9 = (f32[4,40,128]{2,1,0:T(8,128)S(1)}, f32[4,40,128]{2,1,0:T(8,128)S(1)}, u32[]{:S(2)}, u32[]{:S(2)}) collective-permute-start(f32[4,40,128]{2,1,0:T(8,128)S(1)} %get-tuple-element.103), channel_id=1, source_target_pairs={{0,16},{4,20},{8,24},{12,28},{16,32},{20,36},{24,40},{28,44},{32,4... | collective-permute-start | bytes 245768 | tf_op jit(solution)/shard_map/ppermute | solution.py:17
  51.7 13.8 %collective-permute-start.10 = (f32[4,40,128]{2,1,0:T(8,128)S(1)}, f32[4,40,128]{2,1,0:T(8,128)S(1)}, u32[]{:S(2)}, u32[]{:S(2)}) collective-permute-start(f32[4,40,128]{2,1,0:T(8,128)S(1)} %get-tuple-element.67), channel_id=1, source_target_pairs={{0,32},{4,36},{8,40},{12,44},{16,48},{20,52},{24,56},{28,60},{32,6... | collective-permute-start | bytes 245768 | tf_op jit(solution)/shard_map/ppermute | solution.py:17
  56.6 10.6 %collective-permute-start.11 = (f32[4,40,128]{2,1,0:T(8,128)S(1)}, f32[4,40,128]{2,1,0:T(8,128)S(1)}, u32[]{:S(2)}, u32[]{:S(2)}) collective-permute-start(f32[4,40,128]{2,1,0:T(8,128)S(1)} %get-tuple-element.68), channel_id=1, source_target_pairs={{0,48},{4,52},{8,56},{12,60},{16,64},{20,68},{24,72},{28,76},{32,8... | collective-permute-start | bytes 245768 | tf_op jit(solution)/shard_map/ppermute | solution.py:17
  62.8 7.5 %collective-permute-start.12 = (f32[4,40,128]{2,1,0:T(8,128)S(1)}, f32[4,40,128]{2,1,0:T(8,128)S(1)}, u32[]{:S(2)}, u32[]{:S(2)}) collective-permute-start(f32[4,40,128]{2,1,0:T(8,128)S(1)} %get-tuple-element.72), channel_id=1, source_target_pairs={{0,64},{4,68},{8,72},{12,76},{16,80},{20,84},{24,88},{28,92},{32,9... | collective-permute-start | bytes 245768 | tf_op jit(solution)/shard_map/ppermute | solution.py:17
  70.5 6.3 %collective-permute-start.13 = (f32[4,40,128]{2,1,0:T(8,128)S(1)}, f32[4,40,128]{2,1,0:T(8,128)S(1)}, u32[]{:S(2)}, u32[]{:S(2)}) collective-permute-start(f32[4,40,128]{2,1,0:T(8,128)S(1)} %fusion.249), channel_id=1, source_target_pairs={{0,8},{4,12},{8,0},{12,4},{16,24},{20,28},{24,16},{28,20},{32,40},... | collective-permute-start | bytes 245768 | tf_op jit(solution)/shard_map/ppermute | solution.py:22
  77.6 11.9 %collective-permute-start.14 = (f32[8,72,128]{2,1,0:T(8,128)S(1)}, f32[8,72,128]{2,1,0:T(8,128)S(1)}, u32[]{:S(2)}, u32[]{:S(2)}) collective-permute-start(f32[8,72,128]{2,1,0:T(8,128)S(1)} %get-tuple-element.47), channel_id=1, source_target_pairs={{0,8},{4,12},{8,16},{12,20},{16,24},{20,28},{24,32},{28,36},{32,40... | collective-permute-start | bytes 884744 | tf_op jit(solution)/shard_map/ppermute | solution.py:17
  83.3 5.9 %collective-permute-start.16 = (f32[1,72,128]{2,1,0:T(8,128)S(1)}, f32[1,72,128]{2,1,0:T(8,128)S(1)}, u32[]{:S(2)}, u32[]{:S(2)}) collective-permute-start(f32[1,72,128]{2,1,0:T(8,128)S(1)} %get-tuple-element.86), channel_id=1, source_target_pairs={{0,1},{1,2},{2,3},{4,5},{5,6},{6,7},{8,9},{9,10},{10,11},{12,13},{... | collective-permute-start | bytes 110600 | tf_op jit(solution)/shard_map/ppermute | solution.py:28
  89.9 12.2 %collective-permute-start.17 = (f32[8,72,128]{2,1,0:T(8,128)S(1)}, f32[8,72,128]{2,1,0:T(8,128)S(1)}, u32[]{:S(2)}, u32[]{:S(2)}) collective-permute-start(f32[8,72,128]{2,1,0:T(8,128)S(1)} %fusion.133), channel_id=1, source_target_pairs={{0,8},{4,12},{8,16},{12,20},{16,24},{20,28},{24,32},{28,36},{32,40... | collective-permute-start | bytes 884744 | tf_op jit(solution)/shard_map/ppermute | solution.py:17
  91.8 4.3 %collective-permute-start.18 = (f32[1,72,128]{2,1,0:T(8,128)S(1)}, f32[1,72,128]{2,1,0:T(8,128)S(1)}, u32[]{:S(2)}, u32[]{:S(2)}) collective-permute-start(f32[1,72,128]{2,1,0:T(8,128)S(1)} %get-tuple-element.83), channel_id=1, source_target_pairs={{1,0},{2,1},{3,2},{5,4},{6,5},{7,6},{9,8},{10,9},{11,10},{13,12},{... | collective-permute-start | bytes 110600 | tf_op jit(solution)/shard_map/ppermute | solution.py:29
  94.6 6.1 %collective-permute-start.19 = (f32[1,72,128]{2,1,0:T(8,128)S(1)}, f32[1,72,128]{2,1,0:T(8,128)S(1)}, u32[]{:S(2)}, u32[]{:S(2)}) collective-permute-start(f32[1,72,128]{2,1,0:T(8,128)S(1)} %get-tuple-element.84), channel_id=1, source_target_pairs={{0,1},{1,2},{2,3},{4,5},{5,6},{6,7},{8,9},{9,10},{10,11},{12,13},{... | collective-permute-start | bytes 110600 | tf_op jit(solution)/shard_map/ppermute | solution.py:28
  102.6 15.1 %collective-permute-start.22 = (f32[2,8,72,128]{3,2,1,0:T(8,128)S(1)}, f32[2,8,72,128]{3,2,1,0:T(8,128)S(1)}, u32[]{:S(2)}, u32[]{:S(2)}) collective-permute-start(f32[2,8,72,128]{3,2,1,0:T(8,128)S(1)} %pad_maximum_fusion.6), channel_id=1, source_target_pairs={{0,8},{4,12},{8,16},{12,20},{16,24},{20,28},{24,32},{28,36},{32,40... | collective-permute-start | bytes 1769480 | tf_op jit(solution)/shard_map/ppermute | solution.py:17
  104.6 7.0 %collective-permute-start.20 = (f32[2,2,72,128]{3,2,1,0:T(8,128)S(1)}, f32[2,2,72,128]{3,2,1,0:T(8,128)S(1)}, u32[]{:S(2)}, u32[]{:S(2)}) collective-permute-start(f32[2,2,72,128]{3,2,1,0:T(8,128)S(1)} %get-tuple-element.43), channel_id=1, source_target_pairs={{0,1},{1,2},{2,3},{4,5},{5,6},{6,7},{8,9},{9,10},{10,11},{12,13},{... | collective-permute-start | bytes 442376 | tf_op jit(solution)/shard_map/ppermute | solution.py:28
  105.9 7.2 %collective-permute-start.21 = (f32[2,2,72,128]{3,2,1,0:T(8,128)S(1)}, f32[2,2,72,128]{3,2,1,0:T(8,128)S(1)}, u32[]{:S(2)}, u32[]{:S(2)}) collective-permute-start(f32[2,2,72,128]{3,2,1,0:T(8,128)S(1)} %get-tuple-element.44), channel_id=1, source_target_pairs={{1,0},{2,1},{3,2},{5,4},{6,5},{7,6},{9,8},{10,9},{11,10},{13,12},{... | collective-permute-start | bytes 442376 | tf_op jit(solution)/shard_map/ppermute | solution.py:29
  124.2 13.8 %collective-permute-start.26 = (f32[8,128,128]{2,1,0:T(8,128)S(1)}, f32[8,128,128]{2,1,0:T(8,128)S(1)}, u32[]{:S(2)}, u32[]{:S(2)}) collective-permute-start(f32[8,128,128]{2,1,0:T(8,128)S(1)} %fusion.43), channel_id=1, source_target_pairs={{0,4},{4,8},{8,12},{12,16},{16,20},{20,24},{24,28},{28,32},{32,36}... | collective-permute-start | bytes 1572872 | tf_op jit(solution)/shard_map/ppermute | solution.py:17
  126.3 5.4 %collective-permute-start.25 = (f32[2,128,128]{2,1,0:T(8,128)S(1)}, f32[2,128,128]{2,1,0:T(8,128)S(1)}, u32[]{:S(2)}, u32[]{:S(2)}) collective-permute-start(f32[2,128,128]{2,1,0:T(8,128)S(1)} %pad_maximum_fusion.23), channel_id=1, source_target_pairs={{1,0},{2,1},{3,2},{5,4},{6,5},{7,6},{9,8},{10,9},{11,10},{13,12},{... | collective-permute-start | bytes 393224 | tf_op jit(solution)/shard_map/ppermute | solution.py:29
  128.9 7.0 %collective-permute-start.24 = (f32[2,128,128]{2,1,0:T(8,128)S(1)}, f32[2,128,128]{2,1,0:T(8,128)S(1)}, u32[]{:S(2)}, u32[]{:S(2)}) collective-permute-start(f32[2,128,128]{2,1,0:T(8,128)S(1)} %pad_maximum_fusion.22), channel_id=1, source_target_pairs={{0,1},{1,2},{2,3},{4,5},{5,6},{6,7},{8,9},{9,10},{10,11},{12,13},{... | collective-permute-start | bytes 393224 | tf_op jit(solution)/shard_map/ppermute | solution.py:28
  (10 other events, 119.4 us)
